TPU v7x, 256 devices: a whole 4x4x8 slice. The times are simulated.
256 devices in a mesh: ctx: 16 (over x, y), exp: 16 (over z, core).
Axes of the slice: x: 4, y: 4, z: 8, core: 2. Of those that a mesh axis runs over, the one named last changes fastest.
Arguments:
- queries: bfloat16 [16, 2048, 16, 128], P('exp', 'ctx'), may hold values from -10.5 to 10.5
- keys: bfloat16 [16, 2048, 16, 128], P('exp', 'ctx'), may hold values from -10.5 to 10.5
- values: bfloat16 [16, 2048, 16, 128], P('exp', 'ctx'), may hold values from -6 to 6
- cotangent: bfloat16 [16, 2048, 16, 128], P('exp', 'ctx'), may hold values from -6 to 6
- history: int32 [16, 2048], P('exp', 'ctx'), may hold values from 0 to 1, never falling along the last dimension, each value on 1 to 1536 neighbouring positions
- temper: float32 [16], replicated, may hold values from 0.4 to 1.6
Outputs:
- attn_out: bfloat16 [16, 2048, 16, 128], P('exp', 'ctx')
- grad_queries: bfloat16 [16, 2048, 16, 128], P('exp', 'ctx')
- grad_keys: bfloat16 [16, 2048, 16, 128], P('exp', 'ctx')
- grad_values: bfloat16 [16, 2048, 16, 128], P('exp', 'ctx')
- grad_temper: float32 [16], P('ctx')
Inputs may be any that keep to these rules, and one draw needn't show every extreme that they name: Along each batch the history ids never fall; each of the 2 histories holds 1 to 1536 positions.
All inputs are finite; a program needn't handle non-finite values.
Results may differ from a plain program's by a relative error of at most 0.0069.
Values may be sent and summed in bfloat16 or wider, within the bound.
No kernel may reach another device: no remote copies, remote signals or barrier semaphores. Data moves between devices by JAX's collectives and lax.ppermute only.
A program may use at most 64 MiB of HBM per device.

v0:
```python
import functools

import jax
import jax.numpy as jnp
from jax import lax
from jax.experimental import pallas as pl
from jax.experimental.pallas import tpu as pltpu
from jax.sharding import PartitionSpec as P

NT = (((1,), (1,)), ((), ()))
NN = (((1,), (0,)), ((), ()))
LOG2E = 1.4426950408889634
HIDE = -1e30
BLK = 256
PAD = 16
VMEM_LIMIT = 56 * 1024 * 1024


def dot(a, b, dims):
    return lax.dot_general(a, b, dims, preferred_element_type=jnp.float32)


def pack_body(q_ref, k_ref, v_ref, c_ref, hist_ref, out_ref, wide):
    rows, heads, hd = q_ref.shape
    for place, ref in enumerate((q_ref, k_ref, v_ref, c_ref)):
        wide[place] = ref[...].astype(jnp.float32).reshape(rows * heads, hd)
        for head in range(heads):
            part = wide[place, pl.ds(head, rows, stride=heads), :]
            out_ref[head, place * rows : (place + 1) * rows, :] = part.astype(jnp.bfloat16)
    ids = jnp.broadcast_to(hist_ref[...].astype(jnp.float32), (PAD, rows)).astype(jnp.bfloat16)
    for head in range(heads):
        out_ref[head, 4 * rows :, :] = ids


def unpack_body(in_ref, a_ref, b_ref, c_ref, d_ref, wide):
    rows, heads, hd = a_ref.shape
    for place, ref in enumerate((a_ref, b_ref, c_ref, d_ref)):
        for head in range(heads):
            part = in_ref[head, place * rows : (place + 1) * rows, :]
            wide[place, pl.ds(head, rows, stride=heads), :] = part.astype(jnp.float32)
        ref[...] = wide[place].reshape(rows, heads, hd).astype(jnp.bfloat16)


def attend_body(
    temper_ref, in_ref, out_ref, gt_ref, logit, pgrad, k_t, v_t, dk_acc, dv_acc, o_acc, dq_acc
):
    shards, _, hd = in_ref.shape
    rows = 128
    per = BLK // rows
    blocks = shards // per
    seq = shards * rows
    temper = temper_ref[lax.axis_index("ctx")]
    inv_root = hd ** (-0.5)
    logit_scale = temper * (inv_root * LOG2E)

    ids = in_ref[:, 4 * rows :, :].astype(jnp.float32)
    later = jnp.sum(ids) * (1.0 / PAD)
    bound = seq - later.astype(jnp.int32)

    def rows_of(place, block):
        part = in_ref[pl.ds(block * per, per), place * rows : (place + 1) * rows, :]
        return part.reshape(BLK, hd)

    def identity(size):
        return (
            lax.broadcasted_iota(jnp.int32, (size, size), 0)
            == lax.broadcasted_iota(jnp.int32, (size, size), 1)
        ).astype(jnp.bfloat16)

    eye_hd = identity(hd)
    eye_blk = identity(BLK)

    def prepare(block, carry):
        k_t[block] = dot(eye_hd, rows_of(1, block), NT).astype(jnp.bfloat16)
        v_t[block] = dot(eye_hd, rows_of(2, block), NT).astype(jnp.bfloat16)
        dk_acc[block] = jnp.zeros((BLK, hd), jnp.float32)
        dv_acc[block] = jnp.zeros((BLK, hd), jnp.float32)
        return carry

    lax.fori_loop(0, blocks, prepare, 0)

    def query_block(i, gt):
        q_i = rows_of(0, i)
        c_i = rows_of(3, i)
        first_i = i * BLK
        start = jnp.where(first_i >= bound, bound // BLK, 0)
        i_splits = (first_i < bound) & (bound < first_i + BLK)

        def scan_keys(j, carry):
            top, total, delta = carry
            first_j = j * BLK
            s = dot(rows_of(1, j), q_i, NT) * logit_scale
            hides = (j == i) | i_splits | ((first_j < bound) & (bound < first_j + BLK))

            def hide(s):
                row = first_j + lax.broadcasted_iota(jnp.int32, (BLK, BLK), 0)
                col = first_i + lax.broadcasted_iota(jnp.int32, (BLK, BLK), 1)
                low = jnp.where(col >= bound, bound, 0)
                return jnp.where((row <= col) & (row >= low), s, HIDE)

            logit[j] = s

            @pl.when(hides)
            def _():
                logit[j] = hide(s)

            s = logit[j].reshape(BLK // 8, 8, BLK)
            g = dot(rows_of(2, j), c_i, NT)
            pgrad[j] = g
            new_top = jnp.maximum(top, jnp.max(s, axis=0))
            keep = jnp.exp2(top - new_top)
            e = jnp.exp2(s - new_top[None])
            total = total * keep + jnp.sum(e, axis=0)
            delta = delta * keep + jnp.sum(e * g.reshape(BLK // 8, 8, BLK), axis=0)
            return new_top, total, delta

        zero = jnp.zeros((8, BLK), jnp.float32)
        top, total, delta = lax.fori_loop(
            start, i + 1, scan_keys, (jnp.full((8, BLK), HIDE, jnp.float32), zero, zero)
        )
        top_all = jnp.max(top, axis=0, keepdims=True)
        part = jnp.exp2(top - top_all)
        total = jnp.sum(total * part, axis=0, keepdims=True)
        delta = jnp.sum(delta * part, axis=0, keepdims=True) / total
        norm = top_all + jnp.log2(total)
        o_acc[...] = jnp.zeros((hd, BLK), jnp.float32)
        dq_acc[...] = jnp.zeros((hd, BLK), jnp.float32)

        def gradients(j, gt):
            s = logit[j]
            p = jnp.exp2(s - norm)
            ds = p * (pgrad[j] - delta)
            gt = gt + jnp.sum((ds * s).reshape(BLK // 8, 8, BLK), axis=0)
            p_low = p.astype(jnp.bfloat16)
            ds_low = ds.astype(jnp.bfloat16)
            dv_acc[j] += dot(p_low, c_i, NN)
            dk_acc[j] += dot(ds_low, q_i, NN)
            o_acc[...] += dot(v_t[j], p_low, NN)
            dq_acc[...] += dot(k_t[j], ds_low, NN)
            return gt

        gt = lax.fori_loop(start, i + 1, gradients, gt)
        o = dot(eye_blk, o_acc[...].astype(jnp.bfloat16), NT).astype(jnp.bfloat16)
        dq = (dq_acc[...] * (temper * inv_root)).astype(jnp.bfloat16)
        dq = dot(eye_blk, dq, NT).astype(jnp.bfloat16)
        out_ref[pl.ds(i * per, per), 0:rows, :] = o.reshape(per, rows, hd)
        out_ref[pl.ds(i * per, per), rows : 2 * rows, :] = dq.reshape(per, rows, hd)
        return gt

    gt = lax.fori_loop(0, blocks, query_block, jnp.zeros((8, BLK), jnp.float32))

    def finish(block, carry):
        dk = (dk_acc[block] * (temper * inv_root)).astype(jnp.bfloat16)
        dv = dv_acc[block].astype(jnp.bfloat16)
        out_ref[pl.ds(block * per, per), 2 * rows : 3 * rows, :] = dk.reshape(per, rows, hd)
        out_ref[pl.ds(block * per, per), 3 * rows : 4 * rows, :] = dv.reshape(per, rows, hd)
        return carry

    lax.fori_loop(0, blocks, finish, 0)
    gt_ref[0] = jnp.sum(gt) / (temper * LOG2E)


def vmem_spec():
    return pl.BlockSpec(memory_space=pltpu.VMEM)


def body(queries, keys, values, cotangent, history, temper):
    _, rows, heads, hd = queries.shape
    shards = lax.axis_size("ctx")
    blocks = shards * rows // BLK
    params = pltpu.CompilerParams(vmem_limit_bytes=VMEM_LIMIT)
    low, f32 = jnp.bfloat16, jnp.float32

    send = pl.pallas_call(
        pack_body,
        out_shape=jax.ShapeDtypeStruct((heads, 4 * rows + PAD, hd), low),
        in_specs=[vmem_spec()] * 5,
        out_specs=vmem_spec(),
        scratch_shapes=[pltpu.VMEM((4, rows * heads, hd), f32)],
        compiler_params=params,
    )(queries[0], keys[0], values[0], cotangent[0], history)
    recv = lax.all_to_all(send, "ctx", split_axis=0, concat_axis=0, tiled=True)
    results, gt = pl.pallas_call(
        attend_body,
        out_shape=(
            jax.ShapeDtypeStruct((shards, 4 * rows, hd), low),
            jax.ShapeDtypeStruct((1,), f32),
        ),
        in_specs=[pl.BlockSpec(memory_space=pltpu.SMEM), vmem_spec()],
        out_specs=(vmem_spec(), pl.BlockSpec(memory_space=pltpu.SMEM)),
        scratch_shapes=[
            pltpu.VMEM((blocks, BLK, BLK), f32),
            pltpu.VMEM((blocks, BLK, BLK), f32),
            pltpu.VMEM((blocks, hd, BLK), low),
            pltpu.VMEM((blocks, hd, BLK), low),
            pltpu.VMEM((blocks, BLK, hd), f32),
            pltpu.VMEM((blocks, BLK, hd), f32),
            pltpu.VMEM((hd, BLK), f32),
            pltpu.VMEM((hd, BLK), f32),
        ],
        compiler_params=params,
    )(temper, recv)
    back = lax.all_to_all(results, "ctx", split_axis=0, concat_axis=0, tiled=True)
    exp_size = lax.axis_size("exp")
    step = 1
    while step < exp_size:
        gt = gt + lax.ppermute(gt, "exp", [(n, (n + step) % exp_size) for n in range(exp_size)])
        step *= 2
    outs = pl.pallas_call(
        unpack_body,
        out_shape=[jax.ShapeDtypeStruct((rows, heads, hd), low)] * 4,
        in_specs=[vmem_spec()],
        out_specs=[vmem_spec()] * 4,
        scratch_shapes=[pltpu.VMEM((4, rows * heads, hd), f32)],
        compiler_params=params,
    )(back)
    attn_out, grad_q, grad_k, grad_v = [part[None] for part in outs]
    return attn_out, grad_q, grad_k, grad_v, gt


def solution(mesh):
    placed = P("exp", "ctx", None, None)
    return jax.shard_map(
        body,
        mesh=mesh,
        in_specs=(placed, placed, placed, placed, P("exp", "ctx"), P()),
        out_specs=(placed, placed, placed, placed, P("ctx")),
        check_vma=False,
    )
```

profile of v0, /device:TPU:192, one launch (start us, length us, event | category | flops | bytes accessed | tf_op | source)
XLA Modules:
  0.0 107.0 jit_solution(4122014334356506601)
XLA Ops:
  0.6 4.4 %shard_map.101 = bf16[16,528,128]{2,1,0:T(8,128)(2,1)} custom-call(bf16[128,16,128]{2,1,0:T(8,128)(2,1)} %bitcast.8, bf16[128,16,128]{2,1,0:T(8,128)(2,1)} %bitcast.9, bf16[128,16,128]{2,1,0:T(8,128)(2,1)} %bitcast.10, bf16[128,16,128]{2,1,0:T(8,128)(2,1)} %bitcast.11, s32[1,128]{1,0:T(1,128)} %hist_ref.1), custom_call_target="tpu_custom_call" | custom-call | tf_op jit(solution)/shard_map/pallas_call | solution.py:174
  5.0 36.5 %all_to_all.10.in_ref = bf16[16,528,128]{2,1,0:T(8,128)(2,1)} all-to-all(bf16[16,528,128]{2,1,0:T(8,128)(2,1)} %shard_map.101), channel_id=1, replica_groups=mesh['ctx'=16,'exp'=16] {'ctx'}, dimensions={0} | all-to-all | bytes 4325376 | tf_op jit(solution)/shard_map/all_to_all | solution.py:182
  41.5 26.0 %shard_map.102 = (bf16[16,512,128]{2,1,0:T(8,128)(2,1)}, f32[1]{0:T(128)}) custom-call(f32[16]{0:T(128)} %temper_ref.1, bf16[16,528,128]{2,1,0:T(8,128)(2,1)} %all_to_all.10.in_ref), custom_call_target="tpu_custom_call" | custom-call | tf_op jit(solution)/shard_map/pallas_call | solution.py:183
  67.5 3.7 %all-to-all-start.1 = ((bf16[16,512,128]{2,1,0:T(8,128)(2,1)}), bf16[16,512,128]{2,1,0:T(8,128)(2,1)S(1)}, u32[]{:S(2)}, u32[]{:S(2)}) async-start(bf16[16,512,128]{2,1,0:T(8,128)(2,1)} %get-tuple-element.11), calls=%async_computation.1 | async-start | bytes 4194304 | tf_op jit(solution)/shard_map/all_to_all | solution.py:203
  71.3 0.0 collective-permute-start
  71.3 3.0 %collective-permute-done = f32[1]{0:T(128)} collective-permute-done((f32[1]{0:T(128)}, f32[1]{0:T(128)}, u32[]{:S(2)}, u32[]{:S(2)}) %collective-permute-start) | collective-permute-done | bytes 36 | tf_op jit(solution)/shard_map/ppermute | solution.py:207
  75.7 2.4 %collective-permute-start.1 = (f32[1]{0:T(128)}, f32[1]{0:T(128)}, u32[]{:S(2)}, u32[]{:S(2)}) collective-permute-start(f32[1]{0:T(128)} %add.12), channel_id=1, source_target_pairs={{0,2},{1,3},{2,4},{3,5},{4,6},{5,7},{6,8},{7,9},{8,10},{9,11},{10,... | collective-permute-start | bytes 20 | tf_op jit(solution)/shard_map/ppermute | solution.py:207
  78.0 1.2 %collective-permute-done.1 = f32[1]{0:T(128)} collective-permute-done((f32[1]{0:T(128)}, f32[1]{0:T(128)}, u32[]{:S(2)}, u32[]{:S(2)}) %collective-permute-start.1) | collective-permute-done | bytes 36 | tf_op jit(solution)/shard_map/ppermute | solution.py:207
  79.9 3.0 %collective-permute-start.2 = (f32[1]{0:T(128)}, f32[1]{0:T(128)}, u32[]{:S(2)}, u32[]{:S(2)}) collective-permute-start(f32[1]{0:T(128)} %add.13), channel_id=1, source_target_pairs={{0,4},{1,5},{2,6},{3,7},{4,8},{5,9},{6,10},{7,11},{8,12},{9,13},{1... | collective-permute-start | bytes 20 | tf_op jit(solution)/shard_map/ppermute | solution.py:207
  83.0 1.4 %collective-permute-done.2 = f32[1]{0:T(128)} collective-permute-done((f32[1]{0:T(128)}, f32[1]{0:T(128)}, u32[]{:S(2)}, u32[]{:S(2)}) %collective-permute-start.2) | collective-permute-done | bytes 36 | tf_op jit(solution)/shard_map/ppermute | solution.py:207
  85.1 4.3 %collective-permute-start.3 = (f32[1]{0:T(128)}, f32[1]{0:T(128)}, u32[]{:S(2)}, u32[]{:S(2)}) collective-permute-start(f32[1]{0:T(128)} %add.14), channel_id=1, source_target_pairs={{0,8},{1,9},{2,10},{3,11},{4,12},{5,13},{6,14},{7,15},{8,0},{9,1},... | collective-permute-start | bytes 20 | tf_op jit(solution)/shard_map/ppermute | solution.py:207
  89.4 3.2 %collective-permute-done.3 = f32[1]{0:T(128)} collective-permute-done((f32[1]{0:T(128)}, f32[1]{0:T(128)}, u32[]{:S(2)}, u32[]{:S(2)}) %collective-permute-start.3) | collective-permute-done | bytes 36 | tf_op jit(solution)/shard_map/ppermute | solution.py:207
  93.2 6.6 %all-to-all-done.1.in_ref = bf16[16,512,128]{2,1,0:T(8,128)(2,1)S(1)} async-done(((bf16[16,512,128]{2,1,0:T(8,128)(2,1)}), bf16[16,512,128]{2,1,0:T(8,128)(2,1)S(1)}, u32[]{:S(2)}, u32[]{:S(2)}) %all-to-all-start.1) | async-done | bytes 2097184 | tf_op jit(solution)/shard_map/all_to_all | solution.py:203
  99.8 0.0 copy-start
  99.8 1.3 %copy-done = bf16[16,512,128]{2,1,0:T(8,128)(2,1)} copy-done((bf16[16,512,128]{2,1,0:T(8,128)(2,1)}, bf16[16,512,128]{2,1,0:T(8,128)(2,1)S(1)}, u32[]{:S(2)}) %copy-start) | copy-done | bytes 2097176
  101.2 4.7 %shard_map.103 = (bf16[128,16,128]{2,1,0:T(8,128)(2,1)}, bf16[128,16,128]{2,1,0:T(8,128)(2,1)}, bf16[128,16,128]{2,1,0:T(8,128)(2,1)}, bf16[128,16,128]{2,1,0:T(8,128)(2,1)}) custom-call(bf16[16,512,128]{2,1,0:T(8,128)(2,1)} %copy-done), custom_call_target="tpu_custom_call" | custom-call | tf_op jit(solution)/shard_map/pallas_call | solution.py:209
Async XLA Ops:
  67.5 32.3 %all-to-all-start.1 = ((bf16[16,512,128]{2,1,0:T(8,128)(2,1)}), bf16[16,512,128]{2,1,0:T(8,128)(2,1)S(1)}, u32[]{:S(2)}, u32[]{:S(2)}) async-start(bf16[16,512,128]{2,1,0:T(8,128)(2,1)} %get-tuple-element.11), calls=%async_computation.1 | async-start | bytes 4194304 | tf_op jit(solution)/shard_map/all_to_all | solution.py:203
  71.3 3.1 %collective-permute-start = (f32[1]{0:T(128)}, f32[1]{0:T(128)}, u32[]{:S(2)}, u32[]{:S(2)}) collective-permute-start(f32[1]{0:T(128)} %get-tuple-element.16), channel_id=1, source_target_pairs={{0,1},{1,2},{2,3},{3,4},{4,5},{5,6},{6,7},{7,8},{8,9},{9,10},{10,1... | collective-permute-start | bytes 20 | tf_op jit(solution)/shard_map/ppermute | solution.py:207
  75.7 3.6 %collective-permute-start.1 = (f32[1]{0:T(128)}, f32[1]{0:T(128)}, u32[]{:S(2)}, u32[]{:S(2)}) collective-permute-start(f32[1]{0:T(128)} %add.12), channel_id=1, source_target_pairs={{0,2},{1,3},{2,4},{3,5},{4,6},{5,7},{6,8},{7,9},{8,10},{9,11},{10,... | collective-permute-start | bytes 20 | tf_op jit(solution)/shard_map/ppermute | solution.py:207
  79.9 4.5 %collective-permute-start.2 = (f32[1]{0:T(128)}, f32[1]{0:T(128)}, u32[]{:S(2)}, u32[]{:S(2)}) collective-permute-start(f32[1]{0:T(128)} %add.13), channel_id=1, source_target_pairs={{0,4},{1,5},{2,6},{3,7},{4,8},{5,9},{6,10},{7,11},{8,12},{9,13},{1... | collective-permute-start | bytes 20 | tf_op jit(solution)/shard_map/ppermute | solution.py:207
  85.1 7.5 %collective-permute-start.3 = (f32[1]{0:T(128)}, f32[1]{0:T(128)}, u32[]{:S(2)}, u32[]{:S(2)}) collective-permute-start(f32[1]{0:T(128)} %add.14), channel_id=1, source_target_pairs={{0,8},{1,9},{2,10},{3,11},{4,12},{5,13},{6,14},{7,15},{8,0},{9,1},... | collective-permute-start | bytes 20 | tf_op jit(solution)/shard_map/ppermute | solution.py:207
  99.8 1.3 %copy-start = (bf16[16,512,128]{2,1,0:T(8,128)(2,1)}, bf16[16,512,128]{2,1,0:T(8,128)(2,1)S(1)}, u32[]{:S(2)}) copy-start(bf16[16,512,128]{2,1,0:T(8,128)(2,1)S(1)} %all-to-all-done.1.in_ref) | copy-start | bytes 6291460
where the time goes:
time: 108 us; the launch traced here: 107 us
  blocking collectives  36.5 us (34%)
  Pallas kernels  35.1 us (32%)
  waiting for transfers between devices  15.4 us (14%)
  starting transfers between devices  13.5 us (12%)
  between operations  5.19 us (5%)
  local copies, waits for them, and re-layouts  1.34 us (1%)
    all_to_all x1, blocking collectives, body(): recv = lax.all_to_all(send, 'ctx', split_axis=0, concat_axis=0, tiled=True)  36.5 us
    pallas_call x1, Pallas kernels, body(): pl.pallas_call(attend_body, out_shape=(jax.ShapeDtypeStruct((shards, 4 *...  26 us
    ppermute x4, starting transfers between devices, body(): lax.ppermute(gt, 'exp', [(n, (n + step) % exp_size) for n in range(exp_si...  9.8 us
    ppermute x4, waiting for transfers between devices, body(): lax.ppermute(gt, 'exp', [(n, (n + step) % exp_size) for n in range(exp_si...  8.78 us
    all_to_all x1, waiting for transfers between devices, body(): lax.all_to_all(results, 'ctx', split_axis=0, concat_axis=0, tiled=True)  6.6 us
    pallas_call x1, Pallas kernels, body(): pl.pallas_call(unpack_body, out_shape=[jax.ShapeDtypeStruct((rows, heads,...  4.71 us
    pallas_call x1, Pallas kernels, body(): pl.pallas_call(pack_body, out_shape=jax.ShapeDtypeStruct((heads, 4 * rows...  4.38 us
    all_to_all x1, starting transfers between devices, body(): lax.all_to_all(results, 'ctx', split_axis=0, concat_axis=0, tiled=True)  3.73 us
  transfers between devices with their start and end apart: 5, of which 5 were waited for; matrix products, arithmetic and copies ran while one was open for 0% of the time, Pallas kernels for 0%

commit v1 on v0

--- a/solution.py
+++ b/solution.py
@@ -1,4 +1,4 @@
-import functools
+import math
 
 import jax
 import jax.numpy as jnp
@@ -11,45 +11,123 @@
 NN = (((1,), (0,)), ((), ()))
 LOG2E = 1.4426950408889634
 HIDE = -1e30
-BLK = 256
+BLK = 512
 PAD = 16
-VMEM_LIMIT = 56 * 1024 * 1024
+MIB = 1024 * 1024
+
+
+def offsets(size):
+    side = math.isqrt(size)
+    steps = [(dx, dy) for dx in range(side) for dy in range(side) if (dx, dy) != (0, 0)]
+    return side, sorted(steps, key=lambda s: -sum(min(d, side - d) for d in s))
+
+
+def moved(index, step, side):
+    return (index // side + step[0]) % side * side + (index % side + step[1]) % side
+
+
+def exchange(parts, axis):
+    size = len(parts)
+    side, steps = offsets(size)
+    got = [parts[0]]
+    for part, step in zip(parts[1:], steps):
+        got.append(lax.ppermute(part, axis, [(n, moved(n, step, side)) for n in range(size)]))
+    return got
+
+
+def targets(me, size, sign):
+    side, steps = offsets(size)
+    ends = [me]
+    for dx, dy in steps:
+        x = lax.rem(lax.div(me, side) + side + sign * dx, side)
+        y = lax.rem(lax.rem(me, side) + side + sign * dy, side)
+        ends.append(x * side + y)
+    return ends
 
 
 def dot(a, b, dims):
     return lax.dot_general(a, b, dims, preferred_element_type=jnp.float32)
 
 
-def pack_body(q_ref, k_ref, v_ref, c_ref, hist_ref, out_ref, wide):
-    rows, heads, hd = q_ref.shape
-    for place, ref in enumerate((q_ref, k_ref, v_ref, c_ref)):
-        wide[place] = ref[...].astype(jnp.float32).reshape(rows * heads, hd)
-        for head in range(heads):
-            part = wide[place, pl.ds(head, rows, stride=heads), :]
-            out_ref[head, place * rows : (place + 1) * rows, :] = part.astype(jnp.bfloat16)
+def pack_body(q_hbm, k_hbm, v_hbm, c_hbm, hist_ref, *refs):
+    *outs, held, wide, packed, in_sem, out_sem = refs
+    _, rows, heads, hd = held.shape
+    ends = targets(lax.axis_index("ctx"), heads, 1)
+    loads = [
+        pltpu.make_async_copy(ref, held.at[place], in_sem.at[place])
+        for place, ref in enumerate((q_hbm, k_hbm, v_hbm, c_hbm))
+    ]
+    for load in loads:
+        load.start()
     ids = jnp.broadcast_to(hist_ref[...].astype(jnp.float32), (PAD, rows)).astype(jnp.bfloat16)
     for head in range(heads):
-        out_ref[head, 4 * rows :, :] = ids
-
-
-def unpack_body(in_ref, a_ref, b_ref, c_ref, d_ref, wide):
-    rows, heads, hd = a_ref.shape
-    for place, ref in enumerate((a_ref, b_ref, c_ref, d_ref)):
+        packed[head, 4 * rows :, :] = ids
+    stores = []
+    for place, load in enumerate(loads):
+        load.wait()
+        wide[place % 2] = held[place].astype(jnp.float32).reshape(rows * heads, hd)
         for head in range(heads):
-            part = in_ref[head, place * rows : (place + 1) * rows, :]
-            wide[place, pl.ds(head, rows, stride=heads), :] = part.astype(jnp.float32)
-        ref[...] = wide[place].reshape(rows, heads, hd).astype(jnp.bfloat16)
-
-
-def attend_body(
-    temper_ref, in_ref, out_ref, gt_ref, logit, pgrad, k_t, v_t, dk_acc, dv_acc, o_acc, dq_acc
-):
+            part = wide[place % 2, pl.ds(head, rows, stride=heads), :]
+            packed[head, place * rows : (place + 1) * rows, :] = part.astype(jnp.bfloat16)
+        if place % 2 == 0:
+            continue
+        span = pl.ds((place - 1) * rows, 2 * rows if place < 3 else 2 * rows + PAD)
+        for n, (out, end) in enumerate(zip(outs, ends)):
+            store = pltpu.make_async_copy(
+                packed.at[end, span, :], out.at[span, :], out_sem.at[place // 2, n]
+            )
+            store.start()
+            stores.append(store)
+    for store in stores:
+        store.wait()
+
+
+def unpack_body(*refs):
+    held, wide, packed, in_sem, out_sem = refs[-5:]
+    _, rows, heads, hd = packed.shape
+    ins, outs = refs[:heads], refs[heads:-5]
+    ends = targets(lax.axis_index("ctx"), heads, -1)
+    loads = [[] for _ in range(4)]
+    for place in range(4):
+        span = pl.ds(place * rows, rows)
+        for n, (ref, end) in enumerate(zip(ins, ends)):
+            load = pltpu.make_async_copy(
+                ref.at[span, :], held.at[end, span, :], in_sem.at[place, n]
+            )
+            load.start()
+            loads[place].append(load)
+    stores = []
+    for place, ref in enumerate(outs):
+        for load in loads[place]:
+            load.wait()
+        for head in range(heads):
+            part = held[head, place * rows : (place + 1) * rows, :]
+            wide[place % 2, pl.ds(head, rows, stride=heads), :] = part.astype(jnp.float32)
+        packed[place] = wide[place % 2].reshape(rows, heads, hd).astype(jnp.bfloat16)
+        store = pltpu.make_async_copy(packed.at[place], ref, out_sem.at[place])
+        store.start()
+        stores.append(store)
+    for store in stores:
+        store.wait()
+
+
+def attend_body(temper_ref, *refs):
+    in_ref, out_ref, logit, pgrad, k_t, v_t, dk_acc, dv_acc, o_acc, dq_acc, sem = refs[-11:]
     shards, _, hd = in_ref.shape
+    ins, outs, gt_ref = refs[:shards], refs[shards : 2 * shards], refs[2 * shards]
+    me = lax.axis_index("ctx")
+    loads = []
+    for n, (ref, end) in enumerate(zip(ins, targets(me, shards, -1))):
+        load = pltpu.make_async_copy(ref, in_ref.at[end], sem.at[n])
+        load.start()
+        loads.append(load)
+    for load in loads:
+        load.wait()
     rows = 128
     per = BLK // rows
     blocks = shards // per
     seq = shards * rows
-    temper = temper_ref[lax.axis_index("ctx")]
+    temper = temper_ref[me]
     inv_root = hd ** (-0.5)
     logit_scale = temper * (inv_root * LOG2E)
 
@@ -77,34 +155,25 @@
         dv_acc[block] = jnp.zeros((BLK, hd), jnp.float32)
         return carry
 
-    lax.fori_loop(0, blocks, prepare, 0)
+    lax.fori_loop(0, blocks, prepare, 0, unroll=True)
 
     def query_block(i, gt):
         q_i = rows_of(0, i)
         c_i = rows_of(3, i)
         first_i = i * BLK
         start = jnp.where(first_i >= bound, bound // BLK, 0)
-        i_splits = (first_i < bound) & (bound < first_i + BLK)
+        cols = first_i + lax.broadcasted_iota(jnp.int32, (1, BLK), 1)
+        low = jnp.where(cols >= bound, bound, 0)
 
         def scan_keys(j, carry):
             top, total, delta = carry
             first_j = j * BLK
             s = dot(rows_of(1, j), q_i, NT) * logit_scale
-            hides = (j == i) | i_splits | ((first_j < bound) & (bound < first_j + BLK))
-
-            def hide(s):
-                row = first_j + lax.broadcasted_iota(jnp.int32, (BLK, BLK), 0)
-                col = first_i + lax.broadcasted_iota(jnp.int32, (BLK, BLK), 1)
-                low = jnp.where(col >= bound, bound, 0)
-                return jnp.where((row <= col) & (row >= low), s, HIDE)
-
+            row = first_j + lax.broadcasted_iota(jnp.int32, (BLK, BLK), 0)
+            col = first_i + lax.broadcasted_iota(jnp.int32, (BLK, BLK), 1)
+            s = jnp.where((row <= col) & (row >= low), s, HIDE)
             logit[j] = s
-
-            @pl.when(hides)
-            def _():
-                logit[j] = hide(s)
-
-            s = logit[j].reshape(BLK // 8, 8, BLK)
+            s = s.reshape(BLK // 8, 8, BLK)
             g = dot(rows_of(2, j), c_i, NT)
             pgrad[j] = g
             new_top = jnp.maximum(top, jnp.max(s, axis=0))
@@ -156,39 +225,60 @@
         out_ref[pl.ds(block * per, per), 3 * rows : 4 * rows, :] = dv.reshape(per, rows, hd)
         return carry
 
-    lax.fori_loop(0, blocks, finish, 0)
+    lax.fori_loop(0, blocks, finish, 0, unroll=True)
     gt_ref[0] = jnp.sum(gt) / (temper * LOG2E)
+    stores = []
+    for n, (ref, end) in enumerate(zip(outs, targets(me, shards, 1))):
+        store = pltpu.make_async_copy(out_ref.at[end], ref, sem.at[n])
+        store.start()
+        stores.append(store)
+    for store in stores:
+        store.wait()
 
 
 def vmem_spec():
     return pl.BlockSpec(memory_space=pltpu.VMEM)
+
+
+def any_spec():
+    return pl.BlockSpec(memory_space=pl.ANY)
+
+
+def grant(mib):
+    return pltpu.CompilerParams(vmem_limit_bytes=mib * MIB)
 
 
 def body(queries, keys, values, cotangent, history, temper):
     _, rows, heads, hd = queries.shape
     shards = lax.axis_size("ctx")
     blocks = shards * rows // BLK
-    params = pltpu.CompilerParams(vmem_limit_bytes=VMEM_LIMIT)
     low, f32 = jnp.bfloat16, jnp.float32
 
-    send = pl.pallas_call(
+    sends = pl.pallas_call(
         pack_body,
-        out_shape=jax.ShapeDtypeStruct((heads, 4 * rows + PAD, hd), low),
-        in_specs=[vmem_spec()] * 5,
-        out_specs=vmem_spec(),
-        scratch_shapes=[pltpu.VMEM((4, rows * heads, hd), f32)],
-        compiler_params=params,
+        out_shape=[jax.ShapeDtypeStruct((4 * rows + PAD, hd), low)] * heads,
+        in_specs=[any_spec()] * 4 + [vmem_spec()],
+        out_specs=[any_spec()] * heads,
+        scratch_shapes=[
+            pltpu.VMEM((4, rows, heads, hd), low),
+            pltpu.VMEM((2, rows * heads, hd), f32),
+            pltpu.VMEM((heads, 4 * rows + PAD, hd), low),
+            pltpu.SemaphoreType.DMA((4,)),
+            pltpu.SemaphoreType.DMA((2, heads)),
+        ],
+        compiler_params=grant(56),
     )(queries[0], keys[0], values[0], cotangent[0], history)
-    recv = lax.all_to_all(send, "ctx", split_axis=0, concat_axis=0, tiled=True)
-    results, gt = pl.pallas_call(
+    received = exchange(sends, "ctx")
+    smem_spec = pl.BlockSpec(memory_space=pltpu.SMEM)
+    *results, gt = pl.pallas_call(
         attend_body,
-        out_shape=(
-            jax.ShapeDtypeStruct((shards, 4 * rows, hd), low),
-            jax.ShapeDtypeStruct((1,), f32),
-        ),
-        in_specs=[pl.BlockSpec(memory_space=pltpu.SMEM), vmem_spec()],
-        out_specs=(vmem_spec(), pl.BlockSpec(memory_space=pltpu.SMEM)),
+        out_shape=[jax.ShapeDtypeStruct((4 * rows, hd), low)] * shards
+        + [jax.ShapeDtypeStruct((1,), f32)],
+        in_specs=[smem_spec] + [any_spec()] * shards,
+        out_specs=[any_spec()] * shards + [smem_spec],
         scratch_shapes=[
+            pltpu.VMEM((shards, 4 * rows + PAD, hd), low),
+            pltpu.VMEM((shards, 4 * rows, hd), low),
             pltpu.VMEM((blocks, BLK, BLK), f32),
             pltpu.VMEM((blocks, BLK, BLK), f32),
             pltpu.VMEM((blocks, hd, BLK), low),
@@ -197,10 +287,11 @@
             pltpu.VMEM((blocks, BLK, hd), f32),
             pltpu.VMEM((hd, BLK), f32),
             pltpu.VMEM((hd, BLK), f32),
+            pltpu.SemaphoreType.DMA((shards,)),
         ],
-        compiler_params=params,
-    )(temper, recv)
-    back = lax.all_to_all(results, "ctx", split_axis=0, concat_axis=0, tiled=True)
+        compiler_params=grant(56),
+    )(temper, *received)
+    back = exchange(results, "ctx")
     exp_size = lax.axis_size("exp")
     step = 1
     while step < exp_size:
@@ -209,11 +300,17 @@
     outs = pl.pallas_call(
         unpack_body,
         out_shape=[jax.ShapeDtypeStruct((rows, heads, hd), low)] * 4,
-        in_specs=[vmem_spec()],
-        out_specs=[vmem_spec()] * 4,
-        scratch_shapes=[pltpu.VMEM((4, rows * heads, hd), f32)],
-        compiler_params=params,
-    )(back)
+        in_specs=[any_spec()] * shards,
+        out_specs=[any_spec()] * 4,
+        scratch_shapes=[
+            pltpu.VMEM((heads, 4 * rows, hd), low),
+            pltpu.VMEM((2, rows * heads, hd), f32),
+            pltpu.VMEM((4, rows, heads, hd), low),
+            pltpu.SemaphoreType.DMA((4, shards)),
+            pltpu.SemaphoreType.DMA((4,)),
+        ],
+        compiler_params=grant(24),
+    )(*back)
     attn_out, grad_q, grad_k, grad_v = [part[None] for part in outs]
     return attn_out, grad_q, grad_k, grad_v, gt
 

time: 108 us -> 131 us (1.21)
  the two profiles are of different devices: /device:TPU:192 before, /device:TPU:6 now
where the time goes in v1:
time: 131 us
  starting transfers between devices  67.6 us (52%)
  waiting for transfers between devices  28.3 us (22%)
  Pallas kernels  28.1 us (21%)
  between operations  5.17 us (4%)
  local copies, waits for them, and re-layouts  1.49 us (1%)
    ppermute x30, starting transfers between devices, exchange(): lax.ppermute(part, axis, [(n, moved(n, step, side)) for n in range(size)])  56.6 us
    ppermute x30, waiting for transfers between devices, exchange(): lax.ppermute(part, axis, [(n, moved(n, step, side)) for n in range(size)])  18.3 us
    pallas_call x1, Pallas kernels, body(): pl.pallas_call(attend_body, out_shape=[jax.ShapeDtypeStruct((4 * rows, hd...  16.5 us
    ppermute x4, starting transfers between devices, body(): lax.ppermute(gt, 'exp', [(n, (n + step) % exp_size) for n in range(exp_si...  11 us
    ppermute x4, waiting for transfers between devices, body(): lax.ppermute(gt, 'exp', [(n, (n + step) % exp_size) for n in range(exp_si...  9.97 us
    pallas_call x1, Pallas kernels, body(): pl.pallas_call(unpack_body, out_shape=[jax.ShapeDtypeStruct((rows, heads,...  7.09 us
    pallas_call x1, Pallas kernels, body(): pl.pallas_call(pack_body, out_shape=[jax.ShapeDtypeStruct((4 * rows + PAD...  4.55 us
  transfers between devices with their start and end apart: 34, of which 14 were waited for; matrix products, arithmetic and copies ran while one was open for 0% of the time, Pallas kernels for 0%

profile of v1, /device:TPU:6, one launch (start us, length us, event | category | flops | bytes accessed | tf_op | source)
XLA Modules:
  0.0 130.7 jit_solution(11658697692389382493)
XLA Ops:
  0.6 4.6 %shard_map.101 = (bf16[528,128]{1,0:T(8,128)(2,1)}, bf16[528,128]{1,0:T(8,128)(2,1)}, bf16[528,128]{1,0:T(8,128)(2,1)}, bf16[528,128]{1,0:T(8,128)(2,1)}, bf16[5...) custom-call(bf16[128,16,128]{2,1,0:T(8,128)(2,1)} %bitcast.8, ...), custom_call_target="tpu_custom_call" | custom-call | tf_op jit(solution)/shard_map/pallas_call | solution.py:257
  5.2 4.1 %collective-permute-start = (bf16[528,128]{1,0:T(8,128)(2,1)}, bf16[528,128]{1,0:T(8,128)(2,1)S(1)}, u32[]{:S(2)}, u32[]{:S(2)}) collective-permute-start(bf16[528,128]{1,0:T(8,128)(2,1)} %get-tuple-element.43), channel_id=1, source_target_pairs={{0,160},{16,176},{32,128},{48,144},{64,224},{80,240},{96,192},{112... | collective-permute-start | bytes 405512 | tf_op jit(solution)/shard_map/ppermute | solution.py:34
  9.3 1.9 %collective-permute-start.1 = (bf16[528,128]{1,0:T(8,128)(2,1)}, bf16[528,128]{1,0:T(8,128)(2,1)S(1)}, u32[]{:S(2)}, u32[]{:S(2)}) collective-permute-start(bf16[528,128]{1,0:T(8,128)(2,1)} %get-tuple-element.44), channel_id=1, source_target_pairs={{0,96},{16,112},{32,64},{48,80},{64,160},{80,176},{96,128},{112,14... | collective-permute-start | bytes 405512 | tf_op jit(solution)/shard_map/ppermute | solution.py:34
  11.2 0.9 collective-permute-start.2
  12.1 4.7 %collective-permute-start.3 = (bf16[528,128]{1,0:T(8,128)(2,1)}, bf16[528,128]{1,0:T(8,128)(2,1)S(1)}, u32[]{:S(2)}, u32[]{:S(2)}) collective-permute-start(bf16[528,128]{1,0:T(8,128)(2,1)} %get-tuple-element.46), channel_id=1, source_target_pairs={{0,176},{16,128},{32,144},{48,160},{64,240},{80,192},{96,208},{112... | collective-permute-start | bytes 405512 | tf_op jit(solution)/shard_map/ppermute | solution.py:34
  16.8 1.4 %collective-permute-start.4 = (bf16[528,128]{1,0:T(8,128)(2,1)}, bf16[528,128]{1,0:T(8,128)(2,1)S(1)}, u32[]{:S(2)}, u32[]{:S(2)}) collective-permute-start(bf16[528,128]{1,0:T(8,128)(2,1)} %get-tuple-element.47), channel_id=1, source_target_pairs={{0,224},{16,240},{32,192},{48,208},{64,32},{80,48},{96,0},{112,16}... | collective-permute-start | bytes 405512 | tf_op jit(solution)/shard_map/ppermute | solution.py:34
  18.2 1.5 %collective-permute-start.5 = (bf16[528,128]{1,0:T(8,128)(2,1)}, bf16[528,128]{1,0:T(8,128)(2,1)S(1)}, u32[]{:S(2)}, u32[]{:S(2)}) collective-permute-start(bf16[528,128]{1,0:T(8,128)(2,1)} %get-tuple-element.48), channel_id=1, source_target_pairs={{0,32},{16,48},{32,0},{48,16},{64,96},{80,112},{96,64},{112,80},{1... | collective-permute-start | bytes 405512 | tf_op jit(solution)/shard_map/ppermute | solution.py:34
  19.7 3.1 %collective-permute-start.6 = (bf16[528,128]{1,0:T(8,128)(2,1)}, bf16[528,128]{1,0:T(8,128)(2,1)S(1)}, u32[]{:S(2)}, u32[]{:S(2)}) collective-permute-start(bf16[528,128]{1,0:T(8,128)(2,1)} %get-tuple-element.49), channel_id=1, source_target_pairs={{0,80},{16,96},{32,112},{48,64},{64,144},{80,160},{96,176},{112,12... | collective-permute-start | bytes 405512 | tf_op jit(solution)/shard_map/ppermute | solution.py:34
  22.8 1.7 %collective-permute-start.7 = (bf16[528,128]{1,0:T(8,128)(2,1)}, bf16[528,128]{1,0:T(8,128)(2,1)S(1)}, u32[]{:S(2)}, u32[]{:S(2)}) collective-permute-start(bf16[528,128]{1,0:T(8,128)(2,1)} %get-tuple-element.50), channel_id=1, source_target_pairs={{0,112},{16,64},{32,80},{48,96},{64,176},{80,128},{96,144},{112,16... | collective-permute-start | bytes 405512 | tf_op jit(solution)/shard_map/ppermute | solution.py:34
  24.5 1.4 %collective-permute-start.8 = (bf16[528,128]{1,0:T(8,128)(2,1)}, bf16[528,128]{1,0:T(8,128)(2,1)S(1)}, u32[]{:S(2)}, u32[]{:S(2)}) collective-permute-start(bf16[528,128]{1,0:T(8,128)(2,1)} %get-tuple-element.51), channel_id=1, source_target_pairs={{0,128},{16,144},{32,160},{48,176},{64,192},{80,208},{96,224},{112... | collective-permute-start | bytes 405512 | tf_op jit(solution)/shard_map/ppermute | solution.py:34
  25.9 1.9 %collective-permute-done.4.refs_5_ = bf16[528,128]{1,0:T(8,128)(2,1)S(1)} collective-permute-done((bf16[528,128]{1,0:T(8,128)(2,1)}, bf16[528,128]{1,0:T(8,128)(2,1)S(1)}, u32[]{:S(2)}, u32[]{:S(2)}) %collective-permute-start.4) | collective-permute-done | bytes 135200 | tf_op jit(solution)/shard_map/ppermute | solution.py:34
  27.8 0.6 collective-permute-start.9
  28.4 2.1 %collective-permute-done.5.refs_6_ = bf16[528,128]{1,0:T(8,128)(2,1)S(1)} collective-permute-done((bf16[528,128]{1,0:T(8,128)(2,1)}, bf16[528,128]{1,0:T(8,128)(2,1)S(1)}, u32[]{:S(2)}, u32[]{:S(2)}) %collective-permute-start.5) | collective-permute-done | bytes 135200 | tf_op jit(solution)/shard_map/ppermute | solution.py:34
  30.6 0.9 collective-permute-start.10
  31.4 1.9 %collective-permute-start.11 = (bf16[528,128]{1,0:T(8,128)(2,1)}, bf16[528,128]{1,0:T(8,128)(2,1)S(1)}, u32[]{:S(2)}, u32[]{:S(2)}) collective-permute-start(bf16[528,128]{1,0:T(8,128)(2,1)} %get-tuple-element.54), channel_id=1, source_target_pairs={{0,16},{16,32},{32,48},{48,0},{64,80},{80,96},{96,112},{112,64},{1... | collective-permute-start | bytes 405512 | tf_op jit(solution)/shard_map/ppermute | solution.py:34
  33.3 2.7 %collective-permute-start.12 = (bf16[528,128]{1,0:T(8,128)(2,1)}, bf16[528,128]{1,0:T(8,128)(2,1)S(1)}, u32[]{:S(2)}, u32[]{:S(2)}) collective-permute-start(bf16[528,128]{1,0:T(8,128)(2,1)} %get-tuple-element.55), channel_id=1, source_target_pairs={{0,48},{16,0},{32,16},{48,32},{64,112},{80,64},{96,80},{112,96},{1... | collective-permute-start | bytes 405512 | tf_op jit(solution)/shard_map/ppermute | solution.py:34
  36.0 2.5 %collective-permute-start.13 = (bf16[528,128]{1,0:T(8,128)(2,1)}, bf16[528,128]{1,0:T(8,128)(2,1)S(1)}, u32[]{:S(2)}, u32[]{:S(2)}) collective-permute-start(bf16[528,128]{1,0:T(8,128)(2,1)} %get-tuple-element.56), channel_id=1, source_target_pairs={{0,64},{16,80},{32,96},{48,112},{64,128},{80,144},{96,160},{112,17... | collective-permute-start | bytes 405512 | tf_op jit(solution)/shard_map/ppermute | solution.py:34
  38.5 0.9 collective-permute-done.11.refs_12_
  39.4 1.0 collective-permute-done.12.refs_13_
  40.4 0.9 collective-permute-done.13.refs_14_
  41.3 3.6 %collective-permute-done.14.refs_15_ = bf16[528,128]{1,0:T(8,128)(2,1)S(1)} collective-permute-done((bf16[528,128]{1,0:T(8,128)(2,1)}, bf16[528,128]{1,0:T(8,128)(2,1)S(1)}, u32[]{:S(2)}, u32[]{:S(2)}) %collective-permute-start.14) | collective-permute-done | bytes 135200 | tf_op jit(solution)/shard_map/ppermute | solution.py:34
  45.0 0.5 copy-done.15
  45.5 16.5 %shard_map.102 = (bf16[512,128]{1,0:T(8,128)(2,1)}, bf16[512,128]{1,0:T(8,128)(2,1)}, bf16[512,128]{1,0:T(8,128)(2,1)}, bf16[512,128]{1,0:T(8,128)(2,1)}, bf16[5...) custom-call(f32[16]{0:T(128)} %temper_ref.1, ...), custom_call_target="tpu_custom_call" | custom-call | tf_op jit(solution)/shard_map/pallas_call | solution.py:273
  62.1 3.9 %collective-permute-start.16 = (bf16[512,128]{1,0:T(8,128)(2,1)}, bf16[512,128]{1,0:T(8,128)(2,1)S(1)}, u32[]{:S(2)}, u32[]{:S(2)}) collective-permute-start(bf16[512,128]{1,0:T(8,128)(2,1)} %get-tuple-element.60), channel_id=1, source_target_pairs={{0,96},{16,112},{32,64},{48,80},{64,160},{80,176},{96,128},{112,14... | collective-permute-start | bytes 393224 | tf_op jit(solution)/shard_map/ppermute | solution.py:34
  66.0 0.3 collective-permute-start.17
  66.2 5.4 %collective-permute-start.18 = (bf16[512,128]{1,0:T(8,128)(2,1)}, bf16[512,128]{1,0:T(8,128)(2,1)S(1)}, u32[]{:S(2)}, u32[]{:S(2)}) collective-permute-start(bf16[512,128]{1,0:T(8,128)(2,1)} %get-tuple-element.62), channel_id=1, source_target_pairs={{0,176},{16,128},{32,144},{48,160},{64,240},{80,192},{96,208},{112... | collective-permute-start | bytes 393224 | tf_op jit(solution)/shard_map/ppermute | solution.py:34
  72.9 3.7 %collective-permute-start.31 = (f32[1]{0:T(128)}, f32[1]{0:T(128)}, u32[]{:S(2)}, u32[]{:S(2)}) collective-permute-start(f32[1]{0:T(128)} %add.12), channel_id=1, source_target_pairs={{0,2},{1,3},{2,4},{3,5},{4,6},{5,7},{6,8},{7,9},{8,10},{9,11},{10,... | collective-permute-start | bytes 20 | tf_op jit(solution)/shard_map/ppermute | solution.py:298
  76.6 4.1 %collective-permute-done.31 = f32[1]{0:T(128)} collective-permute-done((f32[1]{0:T(128)}, f32[1]{0:T(128)}, u32[]{:S(2)}, u32[]{:S(2)}) %collective-permute-start.31) | collective-permute-done | bytes 36 | tf_op jit(solution)/shard_map/ppermute | solution.py:298
  81.4 1.4 %collective-permute-start.32 = (f32[1]{0:T(128)}, f32[1]{0:T(128)}, u32[]{:S(2)}, u32[]{:S(2)}) collective-permute-start(f32[1]{0:T(128)} %add.13), channel_id=1, source_target_pairs={{0,4},{1,5},{2,6},{3,7},{4,8},{5,9},{6,10},{7,11},{8,12},{9,13},{1... | collective-permute-start | bytes 20 | tf_op jit(solution)/shard_map/ppermute | solution.py:298
  82.8 4.3 %collective-permute-done.32 = f32[1]{0:T(128)} collective-permute-done((f32[1]{0:T(128)}, f32[1]{0:T(128)}, u32[]{:S(2)}, u32[]{:S(2)}) %collective-permute-start.32) | collective-permute-done | bytes 36 | tf_op jit(solution)/shard_map/ppermute | solution.py:298
  87.7 5.9 %collective-permute-start.33 = (f32[1]{0:T(128)}, f32[1]{0:T(128)}, u32[]{:S(2)}, u32[]{:S(2)}) collective-permute-start(f32[1]{0:T(128)} %add.14), channel_id=1, source_target_pairs={{0,8},{1,9},{2,10},{3,11},{4,12},{5,13},{6,14},{7,15},{8,0},{9,1},... | collective-permute-start | bytes 20 | tf_op jit(solution)/shard_map/ppermute | solution.py:298
  93.6 1.5 %collective-permute-done.33 = f32[1]{0:T(128)} collective-permute-done((f32[1]{0:T(128)}, f32[1]{0:T(128)}, u32[]{:S(2)}, u32[]{:S(2)}) %collective-permute-start.33) | collective-permute-done | bytes 36 | tf_op jit(solution)/shard_map/ppermute | solution.py:298
  95.2 3.3 %collective-permute-start.20 = (bf16[512,128]{1,0:T(8,128)(2,1)}, bf16[512,128]{1,0:T(8,128)(2,1)S(1)}, u32[]{:S(2)}, u32[]{:S(2)}) collective-permute-start(bf16[512,128]{1,0:T(8,128)(2,1)} %get-tuple-element.64), channel_id=1, source_target_pairs={{0,32},{16,48},{32,0},{48,16},{64,96},{80,112},{96,64},{112,80},{1... | collective-permute-start | bytes 393224 | tf_op jit(solution)/shard_map/ppermute | solution.py:34
  98.5 0.6 collective-permute-start.21
  99.1 5.4 %collective-permute-start.22 = (bf16[512,128]{1,0:T(8,128)(2,1)}, bf16[512,128]{1,0:T(8,128)(2,1)S(1)}, u32[]{:S(2)}, u32[]{:S(2)}) collective-permute-start(bf16[512,128]{1,0:T(8,128)(2,1)} %get-tuple-element.66), channel_id=1, source_target_pairs={{0,112},{16,64},{32,80},{48,96},{64,176},{80,128},{96,144},{112,16... | collective-permute-start | bytes 393224 | tf_op jit(solution)/shard_map/ppermute | solution.py:34
  104.5 0.2 collective-permute-start.23
  104.7 1.9 %collective-permute-done.19.refs_5_ = bf16[512,128]{1,0:T(8,128)(2,1)S(1)} collective-permute-done((bf16[512,128]{1,0:T(8,128)(2,1)}, bf16[512,128]{1,0:T(8,128)(2,1)S(1)}, u32[]{:S(2)}, u32[]{:S(2)}) %collective-permute-start.19) | collective-permute-done | bytes 131104 | tf_op jit(solution)/shard_map/ppermute | solution.py:34
  106.7 3.5 %collective-permute-start.25 = (bf16[512,128]{1,0:T(8,128)(2,1)}, bf16[512,128]{1,0:T(8,128)(2,1)S(1)}, u32[]{:S(2)}, u32[]{:S(2)}) collective-permute-start(bf16[512,128]{1,0:T(8,128)(2,1)} %get-tuple-element.69), channel_id=1, source_target_pairs={{0,240},{16,192},{32,208},{48,224},{64,48},{80,0},{96,16},{112,32}... | collective-permute-start | bytes 393224 | tf_op jit(solution)/shard_map/ppermute | solution.py:34
  110.1 0.3 collective-permute-start.26
  110.4 2.9 %collective-permute-start.27 = (bf16[512,128]{1,0:T(8,128)(2,1)}, bf16[512,128]{1,0:T(8,128)(2,1)S(1)}, u32[]{:S(2)}, u32[]{:S(2)}) collective-permute-start(bf16[512,128]{1,0:T(8,128)(2,1)} %get-tuple-element.71), channel_id=1, source_target_pairs={{0,48},{16,0},{32,16},{48,32},{64,112},{80,64},{96,80},{112,96},{1... | collective-permute-start | bytes 393224 | tf_op jit(solution)/shard_map/ppermute | solution.py:34
  113.4 1.4 %collective-permute-start.28 = (bf16[512,128]{1,0:T(8,128)(2,1)}, bf16[512,128]{1,0:T(8,128)(2,1)S(1)}, u32[]{:S(2)}, u32[]{:S(2)}) collective-permute-start(bf16[512,128]{1,0:T(8,128)(2,1)} %get-tuple-element.72), channel_id=1, source_target_pairs={{0,64},{16,80},{32,96},{48,112},{64,128},{80,144},{96,160},{112,17... | collective-permute-start | bytes 393224 | tf_op jit(solution)/shard_map/ppermute | solution.py:34
  114.7 0.4 collective-permute-done.24.refs_10_
  115.1 0.2 collective-permute-start.29
  116.0 0.5 collective-permute-done.26.refs_12_
  116.6 2.0 %collective-permute-done.28.refs_14_ = bf16[512,128]{1,0:T(8,128)(2,1)S(1)} collective-permute-done((bf16[512,128]{1,0:T(8,128)(2,1)}, bf16[512,128]{1,0:T(8,128)(2,1)S(1)}, u32[]{:S(2)}, u32[]{:S(2)}) %collective-permute-start.28) | collective-permute-done | bytes 131104 | tf_op jit(solution)/shard_map/ppermute | solution.py:34
  118.5 3.0 %collective-permute-done.29.refs_15_ = bf16[512,128]{1,0:T(8,128)(2,1)S(1)} collective-permute-done((bf16[512,128]{1,0:T(8,128)(2,1)}, bf16[512,128]{1,0:T(8,128)(2,1)S(1)}, u32[]{:S(2)}, u32[]{:S(2)}) %collective-permute-start.29) | collective-permute-done | bytes 131104 | tf_op jit(solution)/shard_map/ppermute | solution.py:34
  121.5 0.9 copy-done
  122.4 7.1 %shard_map.103 = (bf16[128,16,128]{2,1,0:T(8,128)(2,1)}, bf16[128,16,128]{2,1,0:T(8,128)(2,1)}, bf16[128,16,128]{2,1,0:T(8,128)(2,1)}, bf16[128,16,128]{2,1,0:T(8,128)(2,1)}) custom-call(bf16[512,128]{1,0:T(8,128)(2,1)S(1)} %copy-done, bf16[512,128]{1,0:T(8,128)(2,1)S(1)} %collective-permute-done.15.refs_1_, ...), custom_call_target="tpu_custom_call" | custom-call | tf_op jit(solution)/shard_map/pallas_call | solution.py:300
  (55 shorter events, 0.2 us)
Async XLA Ops:
  5.2 13.0 %collective-permute-start = (bf16[528,128]{1,0:T(8,128)(2,1)}, bf16[528,128]{1,0:T(8,128)(2,1)S(1)}, u32[]{:S(2)}, u32[]{:S(2)}) collective-permute-start(bf16[528,128]{1,0:T(8,128)(2,1)} %get-tuple-element.43), channel_id=1, source_target_pairs={{0,160},{16,176},{32,128},{48,144},{64,224},{80,240},{96,192},{112... | collective-permute-start | bytes 405512 | tf_op jit(solution)/shard_map/ppermute | solution.py:34
  9.3 10.4 %collective-permute-start.1 = (bf16[528,128]{1,0:T(8,128)(2,1)}, bf16[528,128]{1,0:T(8,128)(2,1)S(1)}, u32[]{:S(2)}, u32[]{:S(2)}) collective-permute-start(bf16[528,128]{1,0:T(8,128)(2,1)} %get-tuple-element.44), channel_id=1, source_target_pairs={{0,96},{16,112},{32,64},{48,80},{64,160},{80,176},{96,128},{112,14... | collective-permute-start | bytes 405512 | tf_op jit(solution)/shard_map/ppermute | solution.py:34
  11.2 11.7 %collective-permute-start.2 = (bf16[528,128]{1,0:T(8,128)(2,1)}, bf16[528,128]{1,0:T(8,128)(2,1)S(1)}, u32[]{:S(2)}, u32[]{:S(2)}) collective-permute-start(bf16[528,128]{1,0:T(8,128)(2,1)} %get-tuple-element.45), channel_id=1, source_target_pairs={{0,144},{16,160},{32,176},{48,128},{64,208},{80,224},{96,240},{112... | collective-permute-start | bytes 405512 | tf_op jit(solution)/shard_map/ppermute | solution.py:34
  12.1 12.4 %collective-permute-start.3 = (bf16[528,128]{1,0:T(8,128)(2,1)}, bf16[528,128]{1,0:T(8,128)(2,1)S(1)}, u32[]{:S(2)}, u32[]{:S(2)}) collective-permute-start(bf16[528,128]{1,0:T(8,128)(2,1)} %get-tuple-element.46), channel_id=1, source_target_pairs={{0,176},{16,128},{32,144},{48,160},{64,240},{80,192},{96,208},{112... | collective-permute-start | bytes 405512 | tf_op jit(solution)/shard_map/ppermute | solution.py:34
  16.8 11.0 %collective-permute-start.4 = (bf16[528,128]{1,0:T(8,128)(2,1)}, bf16[528,128]{1,0:T(8,128)(2,1)S(1)}, u32[]{:S(2)}, u32[]{:S(2)}) collective-permute-start(bf16[528,128]{1,0:T(8,128)(2,1)} %get-tuple-element.47), channel_id=1, source_target_pairs={{0,224},{16,240},{32,192},{48,208},{64,32},{80,48},{96,0},{112,16}... | collective-permute-start | bytes 405512 | tf_op jit(solution)/shard_map/ppermute | solution.py:34
  18.2 26.7 %copy-start.1 = (bf16[528,128]{1,0:T(8,128)(2,1)}, bf16[528,128]{1,0:T(8,128)(2,1)S(1)}, u32[]{:S(2)}) copy-start(bf16[528,128]{1,0:T(8,128)(2,1)S(1)} %collective-permute-done.refs_1_) | copy-start | bytes 405508
  18.2 12.4 %collective-permute-start.5 = (bf16[528,128]{1,0:T(8,128)(2,1)}, bf16[528,128]{1,0:T(8,128)(2,1)S(1)}, u32[]{:S(2)}, u32[]{:S(2)}) collective-permute-start(bf16[528,128]{1,0:T(8,128)(2,1)} %get-tuple-element.48), channel_id=1, source_target_pairs={{0,32},{16,48},{32,0},{48,16},{64,96},{80,112},{96,64},{112,80},{1... | collective-permute-start | bytes 405512 | tf_op jit(solution)/shard_map/ppermute | solution.py:34
  19.7 25.2 %copy-start.2 = (bf16[528,128]{1,0:T(8,128)(2,1)}, bf16[528,128]{1,0:T(8,128)(2,1)S(1)}, u32[]{:S(2)}) copy-start(bf16[528,128]{1,0:T(8,128)(2,1)S(1)} %collective-permute-done.1.refs_2_) | copy-start | bytes 405508
  19.7 11.7 %collective-permute-start.6 = (bf16[528,128]{1,0:T(8,128)(2,1)}, bf16[528,128]{1,0:T(8,128)(2,1)S(1)}, u32[]{:S(2)}, u32[]{:S(2)}) collective-permute-start(bf16[528,128]{1,0:T(8,128)(2,1)} %get-tuple-element.49), channel_id=1, source_target_pairs={{0,80},{16,96},{32,112},{48,64},{64,144},{80,160},{96,176},{112,12... | collective-permute-start | bytes 405512 | tf_op jit(solution)/shard_map/ppermute | solution.py:34
  22.8 22.0 %copy-start.3 = (bf16[528,128]{1,0:T(8,128)(2,1)}, bf16[528,128]{1,0:T(8,128)(2,1)S(1)}, u32[]{:S(2)}) copy-start(bf16[528,128]{1,0:T(8,128)(2,1)S(1)} %collective-permute-done.2.refs_3_) | copy-start | bytes 405508
  22.8 10.5 %collective-permute-start.7 = (bf16[528,128]{1,0:T(8,128)(2,1)}, bf16[528,128]{1,0:T(8,128)(2,1)S(1)}, u32[]{:S(2)}, u32[]{:S(2)}) collective-permute-start(bf16[528,128]{1,0:T(8,128)(2,1)} %get-tuple-element.50), channel_id=1, source_target_pairs={{0,112},{16,64},{32,80},{48,96},{64,176},{80,128},{96,144},{112,16... | collective-permute-start | bytes 405512 | tf_op jit(solution)/shard_map/ppermute | solution.py:34
  24.5 20.4 %copy-start.4 = (bf16[528,128]{1,0:T(8,128)(2,1)}, bf16[528,128]{1,0:T(8,128)(2,1)S(1)}, u32[]{:S(2)}) copy-start(bf16[528,128]{1,0:T(8,128)(2,1)S(1)} %collective-permute-done.3.refs_4_) | copy-start | bytes 405508
  24.5 11.4 %collective-permute-start.8 = (bf16[528,128]{1,0:T(8,128)(2,1)}, bf16[528,128]{1,0:T(8,128)(2,1)S(1)}, u32[]{:S(2)}, u32[]{:S(2)}) collective-permute-start(bf16[528,128]{1,0:T(8,128)(2,1)} %get-tuple-element.51), channel_id=1, source_target_pairs={{0,128},{16,144},{32,160},{48,176},{64,192},{80,208},{96,224},{112... | collective-permute-start | bytes 405512 | tf_op jit(solution)/shard_map/ppermute | solution.py:34
  27.8 17.1 %copy-start.5 = (bf16[528,128]{1,0:T(8,128)(2,1)}, bf16[528,128]{1,0:T(8,128)(2,1)S(1)}, u32[]{:S(2)}) copy-start(bf16[528,128]{1,0:T(8,128)(2,1)S(1)} %collective-permute-done.4.refs_5_) | copy-start | bytes 405508
  27.8 10.6 %collective-permute-start.9 = (bf16[528,128]{1,0:T(8,128)(2,1)}, bf16[528,128]{1,0:T(8,128)(2,1)S(1)}, u32[]{:S(2)}, u32[]{:S(2)}) collective-permute-start(bf16[528,128]{1,0:T(8,128)(2,1)} %get-tuple-element.52), channel_id=1, source_target_pairs={{0,208},{16,224},{32,240},{48,192},{64,16},{80,32},{96,48},{112,0}... | collective-permute-start | bytes 405512 | tf_op jit(solution)/shard_map/ppermute | solution.py:34
  30.6 14.3 %copy-start.6 = (bf16[528,128]{1,0:T(8,128)(2,1)}, bf16[528,128]{1,0:T(8,128)(2,1)S(1)}, u32[]{:S(2)}) copy-start(bf16[528,128]{1,0:T(8,128)(2,1)S(1)} %collective-permute-done.5.refs_6_) | copy-start | bytes 405508
  30.6 7.9 %collective-permute-start.10 = (bf16[528,128]{1,0:T(8,128)(2,1)}, bf16[528,128]{1,0:T(8,128)(2,1)S(1)}, u32[]{:S(2)}, u32[]{:S(2)}) collective-permute-start(bf16[528,128]{1,0:T(8,128)(2,1)} %get-tuple-element.53), channel_id=1, source_target_pairs={{0,240},{16,192},{32,208},{48,224},{64,48},{80,0},{96,16},{112,32}... | collective-permute-start | bytes 405512 | tf_op jit(solution)/shard_map/ppermute | solution.py:34
  31.4 13.5 %copy-start.7 = (bf16[528,128]{1,0:T(8,128)(2,1)}, bf16[528,128]{1,0:T(8,128)(2,1)S(1)}, u32[]{:S(2)}) copy-start(bf16[528,128]{1,0:T(8,128)(2,1)S(1)} %collective-permute-done.6.refs_7_) | copy-start | bytes 405508
  31.4 7.9 %collective-permute-start.11 = (bf16[528,128]{1,0:T(8,128)(2,1)}, bf16[528,128]{1,0:T(8,128)(2,1)S(1)}, u32[]{:S(2)}, u32[]{:S(2)}) collective-permute-start(bf16[528,128]{1,0:T(8,128)(2,1)} %get-tuple-element.54), channel_id=1, source_target_pairs={{0,16},{16,32},{32,48},{48,0},{64,80},{80,96},{96,112},{112,64},{1... | collective-permute-start | bytes 405512 | tf_op jit(solution)/shard_map/ppermute | solution.py:34
  33.3 11.6 %copy-start.8 = (bf16[528,128]{1,0:T(8,128)(2,1)}, bf16[528,128]{1,0:T(8,128)(2,1)S(1)}, u32[]{:S(2)}) copy-start(bf16[528,128]{1,0:T(8,128)(2,1)S(1)} %collective-permute-done.7.refs_8_) | copy-start | bytes 405508
  33.3 7.1 %collective-permute-start.12 = (bf16[528,128]{1,0:T(8,128)(2,1)}, bf16[528,128]{1,0:T(8,128)(2,1)S(1)}, u32[]{:S(2)}, u32[]{:S(2)}) collective-permute-start(bf16[528,128]{1,0:T(8,128)(2,1)} %get-tuple-element.55), channel_id=1, source_target_pairs={{0,48},{16,0},{32,16},{48,32},{64,112},{80,64},{96,80},{112,96},{1... | collective-permute-start | bytes 405512 | tf_op jit(solution)/shard_map/ppermute | solution.py:34
  36.0 9.0 %copy-start.9 = (bf16[528,128]{1,0:T(8,128)(2,1)}, bf16[528,128]{1,0:T(8,128)(2,1)S(1)}, u32[]{:S(2)}) copy-start(bf16[528,128]{1,0:T(8,128)(2,1)S(1)} %collective-permute-done.8.refs_9_) | copy-start | bytes 405508
  36.0 5.3 %collective-permute-start.13 = (bf16[528,128]{1,0:T(8,128)(2,1)}, bf16[528,128]{1,0:T(8,128)(2,1)S(1)}, u32[]{:S(2)}, u32[]{:S(2)}) collective-permute-start(bf16[528,128]{1,0:T(8,128)(2,1)} %get-tuple-element.56), channel_id=1, source_target_pairs={{0,64},{16,80},{32,96},{48,112},{64,128},{80,144},{96,160},{112,17... | collective-permute-start | bytes 405512 | tf_op jit(solution)/shard_map/ppermute | solution.py:34
  38.4 6.5 %copy-start.10 = (bf16[528,128]{1,0:T(8,128)(2,1)}, bf16[528,128]{1,0:T(8,128)(2,1)S(1)}, u32[]{:S(2)}) copy-start(bf16[528,128]{1,0:T(8,128)(2,1)S(1)} %collective-permute-done.9.refs_10_) | copy-start | bytes 405508
  38.4 6.4 %collective-permute-start.14 = (bf16[528,128]{1,0:T(8,128)(2,1)}, bf16[528,128]{1,0:T(8,128)(2,1)S(1)}, u32[]{:S(2)}, u32[]{:S(2)}) collective-permute-start(bf16[528,128]{1,0:T(8,128)(2,1)} %get-tuple-element.57), channel_id=1, source_target_pairs={{0,192},{16,208},{32,224},{48,240},{64,0},{80,16},{96,32},{112,48}... | collective-permute-start | bytes 405512 | tf_op jit(solution)/shard_map/ppermute | solution.py:34
  38.5 6.5 %copy-start.11 = (bf16[528,128]{1,0:T(8,128)(2,1)}, bf16[528,128]{1,0:T(8,128)(2,1)S(1)}, u32[]{:S(2)}) copy-start(bf16[528,128]{1,0:T(8,128)(2,1)S(1)} %collective-permute-done.10.refs_11_) | copy-start | bytes 405508
  39.4 5.6 %copy-start.12 = (bf16[528,128]{1,0:T(8,128)(2,1)}, bf16[528,128]{1,0:T(8,128)(2,1)S(1)}, u32[]{:S(2)}) copy-start(bf16[528,128]{1,0:T(8,128)(2,1)S(1)} %collective-permute-done.11.refs_12_) | copy-start | bytes 405508
  40.4 4.6 %copy-start.13 = (bf16[528,128]{1,0:T(8,128)(2,1)}, bf16[528,128]{1,0:T(8,128)(2,1)S(1)}, u32[]{:S(2)}) copy-start(bf16[528,128]{1,0:T(8,128)(2,1)S(1)} %collective-permute-done.12.refs_13_) | copy-start | bytes 405508
  41.3 3.7 %copy-start.14 = (bf16[528,128]{1,0:T(8,128)(2,1)}, bf16[528,128]{1,0:T(8,128)(2,1)S(1)}, u32[]{:S(2)}) copy-start(bf16[528,128]{1,0:T(8,128)(2,1)S(1)} %collective-permute-done.13.refs_14_) | copy-start | bytes 405508
  62.0 9.6 %collective-permute-start.30 = (f32[1]{0:T(128)}, f32[1]{0:T(128)}, u32[]{:S(2)}, u32[]{:S(2)}) collective-permute-start(f32[1]{0:T(128)} %get-tuple-element.78), channel_id=1, source_target_pairs={{0,1},{1,2},{2,3},{3,4},{4,5},{5,6},{6,7},{7,8},{8,9},{9,10},{10,1... | collective-permute-start | bytes 20 | tf_op jit(solution)/shard_map/ppermute | solution.py:298
  62.0 33.2 %collective-permute-start.15 = (bf16[512,128]{1,0:T(8,128)(2,1)}, bf16[512,128]{1,0:T(8,128)(2,1)S(1)}, u32[]{:S(2)}, u32[]{:S(2)}) collective-permute-start(bf16[512,128]{1,0:T(8,128)(2,1)} %get-tuple-element.59), channel_id=1, source_target_pairs={{0,160},{16,176},{32,128},{48,144},{64,224},{80,240},{96,192},{112... | collective-permute-start | bytes 393224 | tf_op jit(solution)/shard_map/ppermute | solution.py:34
  62.1 36.4 %collective-permute-start.16 = (bf16[512,128]{1,0:T(8,128)(2,1)}, bf16[512,128]{1,0:T(8,128)(2,1)S(1)}, u32[]{:S(2)}, u32[]{:S(2)}) collective-permute-start(bf16[512,128]{1,0:T(8,128)(2,1)} %get-tuple-element.60), channel_id=1, source_target_pairs={{0,96},{16,112},{32,64},{48,80},{64,160},{80,176},{96,128},{112,14... | collective-permute-start | bytes 393224 | tf_op jit(solution)/shard_map/ppermute | solution.py:34
  66.0 33.1 %collective-permute-start.17 = (bf16[512,128]{1,0:T(8,128)(2,1)}, bf16[512,128]{1,0:T(8,128)(2,1)S(1)}, u32[]{:S(2)}, u32[]{:S(2)}) collective-permute-start(bf16[512,128]{1,0:T(8,128)(2,1)} %get-tuple-element.61), channel_id=1, source_target_pairs={{0,144},{16,160},{32,176},{48,128},{64,208},{80,224},{96,240},{112... | collective-permute-start | bytes 393224 | tf_op jit(solution)/shard_map/ppermute | solution.py:34
  66.2 38.3 %collective-permute-start.18 = (bf16[512,128]{1,0:T(8,128)(2,1)}, bf16[512,128]{1,0:T(8,128)(2,1)S(1)}, u32[]{:S(2)}, u32[]{:S(2)}) collective-permute-start(bf16[512,128]{1,0:T(8,128)(2,1)} %get-tuple-element.62), channel_id=1, source_target_pairs={{0,176},{16,128},{32,144},{48,160},{64,240},{80,192},{96,208},{112... | collective-permute-start | bytes 393224 | tf_op jit(solution)/shard_map/ppermute | solution.py:34
  72.9 7.8 %collective-permute-start.31 = (f32[1]{0:T(128)}, f32[1]{0:T(128)}, u32[]{:S(2)}, u32[]{:S(2)}) collective-permute-start(f32[1]{0:T(128)} %add.12), channel_id=1, source_target_pairs={{0,2},{1,3},{2,4},{3,5},{4,6},{5,7},{6,8},{7,9},{8,10},{9,11},{10,... | collective-permute-start | bytes 20 | tf_op jit(solution)/shard_map/ppermute | solution.py:298
  81.4 5.7 %collective-permute-start.32 = (f32[1]{0:T(128)}, f32[1]{0:T(128)}, u32[]{:S(2)}, u32[]{:S(2)}) collective-permute-start(f32[1]{0:T(128)} %add.13), channel_id=1, source_target_pairs={{0,4},{1,5},{2,6},{3,7},{4,8},{5,9},{6,10},{7,11},{8,12},{9,13},{1... | collective-permute-start | bytes 20 | tf_op jit(solution)/shard_map/ppermute | solution.py:298
  87.7 7.5 %collective-permute-start.33 = (f32[1]{0:T(128)}, f32[1]{0:T(128)}, u32[]{:S(2)}, u32[]{:S(2)}) collective-permute-start(f32[1]{0:T(128)} %add.14), channel_id=1, source_target_pairs={{0,8},{1,9},{2,10},{3,11},{4,12},{5,13},{6,14},{7,15},{8,0},{9,1},... | collective-permute-start | bytes 20 | tf_op jit(solution)/shard_map/ppermute | solution.py:298
  95.2 11.5 %collective-permute-start.19 = (bf16[512,128]{1,0:T(8,128)(2,1)}, bf16[512,128]{1,0:T(8,128)(2,1)S(1)}, u32[]{:S(2)}, u32[]{:S(2)}) collective-permute-start(bf16[512,128]{1,0:T(8,128)(2,1)} %get-tuple-element.63), channel_id=1, source_target_pairs={{0,224},{16,240},{32,192},{48,208},{64,32},{80,48},{96,0},{112,16}... | collective-permute-start | bytes 393224 | tf_op jit(solution)/shard_map/ppermute | solution.py:34
  95.2 11.5 %collective-permute-start.20 = (bf16[512,128]{1,0:T(8,128)(2,1)}, bf16[512,128]{1,0:T(8,128)(2,1)S(1)}, u32[]{:S(2)}, u32[]{:S(2)}) collective-permute-start(bf16[512,128]{1,0:T(8,128)(2,1)} %get-tuple-element.64), channel_id=1, source_target_pairs={{0,32},{16,48},{32,0},{48,16},{64,96},{80,112},{96,64},{112,80},{1... | collective-permute-start | bytes 393224 | tf_op jit(solution)/shard_map/ppermute | solution.py:34
  98.5 11.6 %collective-permute-start.21 = (bf16[512,128]{1,0:T(8,128)(2,1)}, bf16[512,128]{1,0:T(8,128)(2,1)S(1)}, u32[]{:S(2)}, u32[]{:S(2)}) collective-permute-start(bf16[512,128]{1,0:T(8,128)(2,1)} %get-tuple-element.65), channel_id=1, source_target_pairs={{0,80},{16,96},{32,112},{48,64},{64,144},{80,160},{96,176},{112,12... | collective-permute-start | bytes 393224 | tf_op jit(solution)/shard_map/ppermute | solution.py:34
  99.1 11.4 %collective-permute-start.22 = (bf16[512,128]{1,0:T(8,128)(2,1)}, bf16[512,128]{1,0:T(8,128)(2,1)S(1)}, u32[]{:S(2)}, u32[]{:S(2)}) collective-permute-start(bf16[512,128]{1,0:T(8,128)(2,1)} %get-tuple-element.66), channel_id=1, source_target_pairs={{0,112},{16,64},{32,80},{48,96},{64,176},{80,128},{96,144},{112,16... | collective-permute-start | bytes 393224 | tf_op jit(solution)/shard_map/ppermute | solution.py:34
  104.5 8.9 %collective-permute-start.23 = (bf16[512,128]{1,0:T(8,128)(2,1)}, bf16[512,128]{1,0:T(8,128)(2,1)S(1)}, u32[]{:S(2)}, u32[]{:S(2)}) collective-permute-start(bf16[512,128]{1,0:T(8,128)(2,1)} %get-tuple-element.67), channel_id=1, source_target_pairs={{0,128},{16,144},{32,160},{48,176},{64,192},{80,208},{96,224},{112... | collective-permute-start | bytes 393224 | tf_op jit(solution)/shard_map/ppermute | solution.py:34
  106.7 8.5 %collective-permute-start.24 = (bf16[512,128]{1,0:T(8,128)(2,1)}, bf16[512,128]{1,0:T(8,128)(2,1)S(1)}, u32[]{:S(2)}, u32[]{:S(2)}) collective-permute-start(bf16[512,128]{1,0:T(8,128)(2,1)} %get-tuple-element.68), channel_id=1, source_target_pairs={{0,208},{16,224},{32,240},{48,192},{64,16},{80,32},{96,48},{112,0}... | collective-permute-start | bytes 393224 | tf_op jit(solution)/shard_map/ppermute | solution.py:34
  106.7 9.4 %collective-permute-start.25 = (bf16[512,128]{1,0:T(8,128)(2,1)}, bf16[512,128]{1,0:T(8,128)(2,1)S(1)}, u32[]{:S(2)}, u32[]{:S(2)}) collective-permute-start(bf16[512,128]{1,0:T(8,128)(2,1)} %get-tuple-element.69), channel_id=1, source_target_pairs={{0,240},{16,192},{32,208},{48,224},{64,48},{80,0},{96,16},{112,32}... | collective-permute-start | bytes 393224 | tf_op jit(solution)/shard_map/ppermute | solution.py:34
  110.1 6.4 %collective-permute-start.26 = (bf16[512,128]{1,0:T(8,128)(2,1)}, bf16[512,128]{1,0:T(8,128)(2,1)S(1)}, u32[]{:S(2)}, u32[]{:S(2)}) collective-permute-start(bf16[512,128]{1,0:T(8,128)(2,1)} %get-tuple-element.70), channel_id=1, source_target_pairs={{0,16},{16,32},{32,48},{48,0},{64,80},{80,96},{96,112},{112,64},{1... | collective-permute-start | bytes 393224 | tf_op jit(solution)/shard_map/ppermute | solution.py:34
  110.4 6.1 %collective-permute-start.27 = (bf16[512,128]{1,0:T(8,128)(2,1)}, bf16[512,128]{1,0:T(8,128)(2,1)S(1)}, u32[]{:S(2)}, u32[]{:S(2)}) collective-permute-start(bf16[512,128]{1,0:T(8,128)(2,1)} %get-tuple-element.71), channel_id=1, source_target_pairs={{0,48},{16,0},{32,16},{48,32},{64,112},{80,64},{96,80},{112,96},{1... | collective-permute-start | bytes 393224 | tf_op jit(solution)/shard_map/ppermute | solution.py:34
  113.4 5.2 %collective-permute-start.28 = (bf16[512,128]{1,0:T(8,128)(2,1)}, bf16[512,128]{1,0:T(8,128)(2,1)S(1)}, u32[]{:S(2)}, u32[]{:S(2)}) collective-permute-start(bf16[512,128]{1,0:T(8,128)(2,1)} %get-tuple-element.72), channel_id=1, source_target_pairs={{0,64},{16,80},{32,96},{48,112},{64,128},{80,144},{96,160},{112,17... | collective-permute-start | bytes 393224 | tf_op jit(solution)/shard_map/ppermute | solution.py:34
  115.1 6.4 %collective-permute-start.29 = (bf16[512,128]{1,0:T(8,128)(2,1)}, bf16[512,128]{1,0:T(8,128)(2,1)S(1)}, u32[]{:S(2)}, u32[]{:S(2)}) collective-permute-start(bf16[512,128]{1,0:T(8,128)(2,1)} %get-tuple-element.73), channel_id=1, source_target_pairs={{0,192},{16,208},{32,224},{48,240},{64,0},{80,16},{96,32},{112,48}... | collective-permute-start | bytes 393224 | tf_op jit(solution)/shard_map/ppermute | solution.py:34
  (2 other events, 1.6 us)

commit v2 on v0

v2 whole, which is shorter than its diff:
```python
import functools

import jax
import jax.numpy as jnp
from jax import lax
from jax.experimental import pallas as pl
from jax.experimental.pallas import tpu as pltpu
from jax.sharding import PartitionSpec as P

NT = (((1,), (1,)), ((), ()))
NN = (((1,), (0,)), ((), ()))
LOG2E = 1.4426950408889634
HIDE = -1e30
BLK = 256
PAD = 16
MIB = 1024 * 1024


def dot(a, b, dims):
    return lax.dot_general(a, b, dims, preferred_element_type=jnp.float32)


def pack_body(q_hbm, k_hbm, v_hbm, c_hbm, hist_ref, out_hbm, held, wide, packed, in_sem, out_sem):
    _, rows, heads, hd = held.shape
    loads = [
        pltpu.make_async_copy(ref, held.at[place], in_sem.at[place])
        for place, ref in enumerate((q_hbm, k_hbm, v_hbm, c_hbm))
    ]
    for load in loads:
        load.start()
    ids = jnp.broadcast_to(hist_ref[...].astype(jnp.float32), (PAD, rows)).astype(jnp.bfloat16)
    for head in range(heads):
        packed[head, 4 * rows :, :] = ids
    stores = []
    for place, load in enumerate(loads):
        load.wait()
        wide[place % 2] = held[place].astype(jnp.float32).reshape(rows * heads, hd)
        for head in range(heads):
            part = wide[place % 2, pl.ds(head, rows, stride=heads), :]
            packed[head, place * rows : (place + 1) * rows, :] = part.astype(jnp.bfloat16)
        span = pl.ds(place * rows, rows if place < 3 else rows + PAD)
        store = pltpu.make_async_copy(
            packed.at[:, span, :], out_hbm.at[:, span, :], out_sem.at[place]
        )
        store.start()
        stores.append(store)
    for store in stores:
        store.wait()


def unpack_body(in_hbm, a_hbm, b_hbm, c_hbm, d_hbm, held, wide, packed, in_sem, out_sem):
    _, rows, heads, hd = packed.shape
    loads = []
    for place in range(4):
        span = pl.ds(place * rows, rows)
        load = pltpu.make_async_copy(
            in_hbm.at[:, span, :], held.at[:, span, :], in_sem.at[place]
        )
        load.start()
        loads.append(load)
    stores = []
    for place, ref in enumerate((a_hbm, b_hbm, c_hbm, d_hbm)):
        loads[place].wait()
        for head in range(heads):
            part = held[head, place * rows : (place + 1) * rows, :]
            wide[place % 2, pl.ds(head, rows, stride=heads), :] = part.astype(jnp.float32)
        packed[place] = wide[place % 2].reshape(rows, heads, hd).astype(jnp.bfloat16)
        store = pltpu.make_async_copy(packed.at[place], ref, out_sem.at[place])
        store.start()
        stores.append(store)
    for store in stores:
        store.wait()


def attend_body(
    temper_ref,
    in_hbm,
    out_hbm,
    gt_ref,
    held,
    done,
    logit,
    pgrad,
    k_t,
    v_t,
    dk_acc,
    dv_acc,
    in_sem,
    out_sem,
):
    shards, hd = held.shape[0], held.shape[2]
    rows = done.shape[1] // 4
    per = BLK // rows
    blocks = shards // per
    group = blocks // 4
    loads = [
        pltpu.make_async_copy(in_hbm.at[span], held.at[span], in_sem.at[n])
        for n, span in enumerate(
            (pl.ds(0, group * per), pl.ds(group * per, shards - group * per))
        )
    ]
    for load in loads:
        load.start()
    temper = temper_ref[lax.axis_index("ctx")]
    scale = temper * hd ** (-0.5)
    logit_scale = scale * LOG2E

    def identity(size):
        return (
            lax.broadcasted_iota(jnp.int32, (size, size), 0)
            == lax.broadcasted_iota(jnp.int32, (size, size), 1)
        ).astype(jnp.bfloat16)

    eye_hd = identity(hd)
    eye_blk = identity(BLK)

    def span_of(place, low, high):
        part = held[low * per : high * per, place * rows : (place + 1) * rows, :]
        return part.reshape((high - low) * BLK, hd)

    def put(place, block, value):
        done[block * per : (block + 1) * per, place * rows : (place + 1) * rows, :] = value.astype(
            jnp.bfloat16
        ).reshape(per, rows, hd)

    def store(first, last, kind):
        span, part = pl.ds(first * per, (last - first) * per), pl.ds(2 * kind * rows, 2 * rows)
        return pltpu.make_async_copy(
            done.at[span, part, :], out_hbm.at[span, part, :], out_sem.at[kind, first // group]
        )

    def turn(low, high):
        span = slice(low * BLK, high * BLK)
        k_t[:, span] = dot(eye_hd, span_of(1, low, high), NT).astype(jnp.bfloat16)
        v_t[:, span] = dot(eye_hd, span_of(2, low, high), NT).astype(jnp.bfloat16)

    def folded(x):
        return x.reshape(x.shape[0] // 8, 8, x.shape[1])

    edge_low, edge_high = blocks // 4, 3 * blocks // 4

    def first_key(i):
        return edge_low if i >= edge_high else 0

    def scores(i, bound):
        low, high = first_key(i), i + 1
        s = dot(span_of(1, low, high), span_of(0, i, i + 1), NT) * logit_scale
        g = dot(span_of(2, low, high), span_of(3, i, i + 1), NT)
        pgrad[i, low * BLK : high * BLK, :] = g
        cols = i * BLK + lax.broadcasted_iota(jnp.int32, (1, BLK), 1)
        lowest = jnp.where(cols >= bound, bound, 0)
        top = None
        for j in range(low, high):
            part = s[(j - low) * BLK : (j - low + 1) * BLK]
            row = lax.broadcasted_iota(jnp.int32, (BLK, BLK), 0)
            if i >= edge_low and j < edge_high:
                part = jnp.where(row >= lowest - j * BLK, part, HIDE)
            if j == i:
                part = jnp.where(
                    row <= lax.broadcasted_iota(jnp.int32, (BLK, BLK), 1), part, HIDE
                )
            logit[i, j * BLK : (j + 1) * BLK, :] = part
            part = jnp.max(folded(part), axis=0)
            top = part if top is None else jnp.maximum(top, part)
        return jnp.max(top, axis=0, keepdims=True)

    def settle(i, top):
        total = delta = jnp.zeros((8, BLK), jnp.float32)
        for j in range(first_key(i), i + 1):
            span = slice(j * BLK, (j + 1) * BLK)
            e = jnp.exp2(logit[i, span, :] - top)
            total = total + jnp.sum(folded(e), axis=0)
            delta = delta + jnp.sum(folded(e * pgrad[i, span, :]), axis=0)
        total = jnp.sum(total, axis=0, keepdims=True)
        delta = jnp.sum(delta, axis=0, keepdims=True) / total
        return top + jnp.log2(total), delta

    def gradients(i, norm, delta, gt):
        low, high = first_key(i), i + 1
        weights, grads = [], []
        for j in range(low, high):
            span = slice(j * BLK, (j + 1) * BLK)
            s = logit[i, span, :]
            p = jnp.exp2(s - norm)
            ds = p * (pgrad[i, span, :] - delta)
            gt = gt + jnp.sum(folded(ds * s), axis=0)
            weights.append(p.astype(jnp.bfloat16))
            grads.append(ds.astype(jnp.bfloat16))
        p, ds = jnp.concatenate(weights, axis=0), jnp.concatenate(grads, axis=0)
        dv = dot(p, span_of(3, i, i + 1), NN)
        dk = dot(ds, span_of(0, i, i + 1), NN)
        if low < i:
            span = slice(low * BLK, i * BLK)
            dv_acc[span, :] += dv[: (i - low) * BLK]
            dk_acc[span, :] += dk[: (i - low) * BLK]
        span = slice(i * BLK, high * BLK)
        dv_acc[span, :] = dv[(i - low) * BLK :]
        dk_acc[span, :] = dk[(i - low) * BLK :]
        span = slice(low * BLK, high * BLK)
        o = dot(v_t[:, span], p, NN).astype(jnp.bfloat16)
        dq = (dot(k_t[:, span], ds, NN) * scale).astype(jnp.bfloat16)
        put(0, i, dot(eye_blk, o, NT))
        put(1, i, dot(eye_blk, dq, NT))
        return gt

    loads[0].wait()
    turn(0, group)
    tops = {0: scores(0, shards * rows)}
    gt = jnp.zeros((8, BLK), jnp.float32)
    bound = None
    for i in range(blocks):
        if i + 1 == group:
            loads[1].wait()
            ids = held[:, 4 * rows :, :].astype(jnp.float32)
            bound = shards * rows - (jnp.sum(ids) * (1.0 / PAD)).astype(jnp.int32)
            turn(group, blocks)
        if i + 1 < blocks:
            tops[i + 1] = scores(i + 1, shards * rows if bound is None else bound)
        norm, delta = settle(i, tops[i])
        gt = gradients(i, norm, delta, gt)
        if (i + 1) % group == 0:
            store(i + 1 - group, i + 1, 0).start()
    for i in range(blocks):
        span = slice(i * BLK, (i + 1) * BLK)
        put(2, i, dk_acc[span, :] * scale)
        put(3, i, dv_acc[span, :])
        if (i + 1) % group == 0:
            store(i + 1 - group, i + 1, 1).start()
    gt_ref[0] = jnp.sum(gt) / (temper * LOG2E)
    for first in range(0, blocks, group):
        store(first, first + group, 0).wait()
        store(first, first + group, 1).wait()


def vmem_spec():
    return pl.BlockSpec(memory_space=pltpu.VMEM)


def any_spec():
    return pl.BlockSpec(memory_space=pl.ANY)


def grant(mib):
    return pltpu.CompilerParams(vmem_limit_bytes=mib * MIB)


def body(queries, keys, values, cotangent, history, temper):
    _, rows, heads, hd = queries.shape
    shards = lax.axis_size("ctx")
    blocks = shards * rows // BLK
    low, f32 = jnp.bfloat16, jnp.float32

    send = pl.pallas_call(
        pack_body,
        out_shape=jax.ShapeDtypeStruct((heads, 4 * rows + PAD, hd), low),
        in_specs=[any_spec()] * 4 + [vmem_spec()],
        out_specs=any_spec(),
        scratch_shapes=[
            pltpu.VMEM((4, rows, heads, hd), low),
            pltpu.VMEM((2, rows * heads, hd), f32),
            pltpu.VMEM((heads, 4 * rows + PAD, hd), low),
            pltpu.SemaphoreType.DMA((4,)),
            pltpu.SemaphoreType.DMA((4,)),
        ],
        compiler_params=grant(56),
    )(queries[0], keys[0], values[0], cotangent[0], history)
    recv = lax.all_to_all(send, "ctx", split_axis=0, concat_axis=0, tiled=True)
    results, gt = pl.pallas_call(
        attend_body,
        out_shape=(
            jax.ShapeDtypeStruct((shards, 4 * rows, hd), low),
            jax.ShapeDtypeStruct((1,), f32),
        ),
        in_specs=[pl.BlockSpec(memory_space=pltpu.SMEM), any_spec()],
        out_specs=(any_spec(), pl.BlockSpec(memory_space=pltpu.SMEM)),
        scratch_shapes=[
            pltpu.VMEM((shards, 4 * rows + PAD, hd), low),
            pltpu.VMEM((shards, 4 * rows, hd), low),
            pltpu.VMEM((blocks, blocks * BLK, BLK), f32),
            pltpu.VMEM((blocks, blocks * BLK, BLK), f32),
            pltpu.VMEM((hd, blocks * BLK), low),
            pltpu.VMEM((hd, blocks * BLK), low),
            pltpu.VMEM((blocks * BLK, hd), f32),
            pltpu.VMEM((blocks * BLK, hd), f32),
            pltpu.SemaphoreType.DMA((2,)),
            pltpu.SemaphoreType.DMA((2, 4)),
        ],
        compiler_params=grant(60),
    )(temper, recv)
    back = lax.all_to_all(results, "ctx", split_axis=0, concat_axis=0, tiled=True)
    exp_size = lax.axis_size("exp")
    step = 1
    while step < exp_size:
        gt = gt + lax.ppermute(gt, "exp", [(n, (n + step) % exp_size) for n in range(exp_size)])
        step *= 2
    outs = pl.pallas_call(
        unpack_body,
        out_shape=[jax.ShapeDtypeStruct((rows, heads, hd), low)] * 4,
        in_specs=[any_spec()],
        out_specs=[any_spec()] * 4,
        scratch_shapes=[
            pltpu.VMEM((heads, 4 * rows, hd), low),
            pltpu.VMEM((2, rows * heads, hd), f32),
            pltpu.VMEM((4, rows, heads, hd), low),
            pltpu.SemaphoreType.DMA((4,)),
            pltpu.SemaphoreType.DMA((4,)),
        ],
        compiler_params=grant(16),
    )(back)
    attn_out, grad_q, grad_k, grad_v = [part[None] for part in outs]
    return attn_out, grad_q, grad_k, grad_v, gt


def solution(mesh):
    placed = P("exp", "ctx", None, None)
    return jax.shard_map(
        body,
        mesh=mesh,
        in_specs=(placed, placed, placed, placed, P("exp", "ctx"), P()),
        out_specs=(placed, placed, placed, placed, P("ctx")),
        check_vma=False,
    )
```

time: 108 us -> 92.7 us (0.86)
  Pallas kernels: 35.1 us -> 21.6 us
  local copies, waits for them, and re-layouts: 1.34 us -> 0 us
    pallas_call x1, Pallas kernels: 26 us -> 14.1 us  [body(): pl.pallas_call(attend_body, out_shape=(jax.ShapeDtypeStruct((shards, 4 *...]
    pallas_call x1, Pallas kernels: 4.71 us -> 3.33 us  [body(): pl.pallas_call(unpack_body, out_shape=[jax.ShapeDtypeStruct((rows, heads,...]
    unnamed x2 -> x0, local copies, waits for them, and re-layouts: 1.34 us -> none
    ppermute x4, waiting for transfers between devices: 8.78 us -> 10 us  [body(): lax.ppermute(gt, 'exp', [(n, (n + step) % exp_size) for n in range(exp_si...]
where the time goes in v2:
time: 92.7 us; the launch traced here: 92.4 us
  blocking collectives  36.5 us (39%)
  Pallas kernels  21.6 us (23%)
  waiting for transfers between devices  15.5 us (17%)
  starting transfers between devices  14 us (15%)
  between operations  4.71 us (5%)
    all_to_all x1, blocking collectives, body(): recv = lax.all_to_all(send, 'ctx', split_axis=0, concat_axis=0, tiled=True)  36.5 us
    pallas_call x1, Pallas kernels, body(): pl.pallas_call(attend_body, out_shape=(jax.ShapeDtypeStruct((shards, 4 *...  14.1 us
    ppermute x4, starting transfers between devices, body(): lax.ppermute(gt, 'exp', [(n, (n + step) % exp_size) for n in range(exp_si...  10.1 us
    ppermute x4, waiting for transfers between devices, body(): lax.ppermute(gt, 'exp', [(n, (n + step) % exp_size) for n in range(exp_si...  10 us
    all_to_all x1, waiting for transfers between devices, body(): lax.all_to_all(results, 'ctx', split_axis=0, concat_axis=0, tiled=True)  5.53 us
    pallas_call x1, Pallas kernels, body(): pl.pallas_call(pack_body, out_shape=jax.ShapeDtypeStruct((heads, 4 * rows...  4.12 us
    all_to_all x1, starting transfers between devices, body(): lax.all_to_all(results, 'ctx', split_axis=0, concat_axis=0, tiled=True)  3.91 us
    pallas_call x1, Pallas kernels, body(): pl.pallas_call(unpack_body, out_shape=[jax.ShapeDtypeStruct((rows, heads,...  3.33 us
  transfers between devices with their start and end apart: 5, of which 5 were waited for; matrix products, arithmetic and copies ran while one was open for 0% of the time, Pallas kernels for 0%

profile of v2, /device:TPU:192, one launch (start us, length us, event | category | flops | bytes accessed | tf_op | source)
XLA Modules:
  0.0 92.4 jit_solution(9567267398124948063)
XLA Ops:
  0.6 4.1 %shard_map.101 = bf16[16,528,128]{2,1,0:T(8,128)(2,1)} custom-call(bf16[128,16,128]{2,1,0:T(8,128)(2,1)} %bitcast.8, bf16[128,16,128]{2,1,0:T(8,128)(2,1)} %bitcast.9, bf16[128,16,128]{2,1,0:T(8,128)(2,1)} %bitcast.10, bf16[128,16,128]{2,1,0:T(8,128)(2,1)} %bitcast.11, s32[1,128]{1,0:T(1,128)} %hist_ref.1), custom_call_target="tpu_custom_call" | custom-call | tf_op jit(solution)/shard_map/pallas_call | solution.py:253
  4.8 36.5 %all_to_all.10.in_hbm = bf16[16,528,128]{2,1,0:T(8,128)(2,1)} all-to-all(bf16[16,528,128]{2,1,0:T(8,128)(2,1)} %shard_map.101), channel_id=1, replica_groups=mesh['ctx'=16,'exp'=16] {'ctx'}, dimensions={0} | all-to-all | bytes 4325376 | tf_op jit(solution)/shard_map/all_to_all | solution.py:267
  41.3 14.1 %shard_map.102 = (bf16[16,512,128]{2,1,0:T(8,128)(2,1)}, f32[1]{0:T(128)}) custom-call(f32[16]{0:T(128)} %temper_ref.1, bf16[16,528,128]{2,1,0:T(8,128)(2,1)} %all_to_all.10.in_hbm), custom_call_target="tpu_custom_call" | custom-call | tf_op jit(solution)/shard_map/pallas_call | solution.py:268
  55.4 3.9 %all-to-all-start.1 = ((bf16[16,512,128]{2,1,0:T(8,128)(2,1)}), bf16[16,512,128]{2,1,0:T(8,128)(2,1)S(1)}, u32[]{:S(2)}, u32[]{:S(2)}) async-start(bf16[16,512,128]{2,1,0:T(8,128)(2,1)} %get-tuple-element.11), calls=%async_computation.1 | async-start | bytes 4194304 | tf_op jit(solution)/shard_map/all_to_all | solution.py:290
  59.3 0.0 collective-permute-start
  59.3 3.2 %collective-permute-done = f32[1]{0:T(128)} collective-permute-done((f32[1]{0:T(128)}, f32[1]{0:T(128)}, u32[]{:S(2)}, u32[]{:S(2)}) %collective-permute-start) | collective-permute-done | bytes 36 | tf_op jit(solution)/shard_map/ppermute | solution.py:294
  63.7 2.4 %collective-permute-start.1 = (f32[1]{0:T(128)}, f32[1]{0:T(128)}, u32[]{:S(2)}, u32[]{:S(2)}) collective-permute-start(f32[1]{0:T(128)} %add.12), channel_id=1, source_target_pairs={{0,2},{1,3},{2,4},{3,5},{4,6},{5,7},{6,8},{7,9},{8,10},{9,11},{10,... | collective-permute-start | bytes 20 | tf_op jit(solution)/shard_map/ppermute | solution.py:294
  66.1 1.3 %collective-permute-done.1 = f32[1]{0:T(128)} collective-permute-done((f32[1]{0:T(128)}, f32[1]{0:T(128)}, u32[]{:S(2)}, u32[]{:S(2)}) %collective-permute-start.1) | collective-permute-done | bytes 36 | tf_op jit(solution)/shard_map/ppermute | solution.py:294
  68.0 3.1 %collective-permute-start.2 = (f32[1]{0:T(128)}, f32[1]{0:T(128)}, u32[]{:S(2)}, u32[]{:S(2)}) collective-permute-start(f32[1]{0:T(128)} %add.13), channel_id=1, source_target_pairs={{0,4},{1,5},{2,6},{3,7},{4,8},{5,9},{6,10},{7,11},{8,12},{9,13},{1... | collective-permute-start | bytes 20 | tf_op jit(solution)/shard_map/ppermute | solution.py:294
  71.1 2.5 %collective-permute-done.2 = f32[1]{0:T(128)} collective-permute-done((f32[1]{0:T(128)}, f32[1]{0:T(128)}, u32[]{:S(2)}, u32[]{:S(2)}) %collective-permute-start.2) | collective-permute-done | bytes 36 | tf_op jit(solution)/shard_map/ppermute | solution.py:294
  74.2 4.6 %collective-permute-start.3 = (f32[1]{0:T(128)}, f32[1]{0:T(128)}, u32[]{:S(2)}, u32[]{:S(2)}) collective-permute-start(f32[1]{0:T(128)} %add.14), channel_id=1, source_target_pairs={{0,8},{1,9},{2,10},{3,11},{4,12},{5,13},{6,14},{7,15},{8,0},{9,1},... | collective-permute-start | bytes 20 | tf_op jit(solution)/shard_map/ppermute | solution.py:294
  78.8 3.0 %collective-permute-done.3 = f32[1]{0:T(128)} collective-permute-done((f32[1]{0:T(128)}, f32[1]{0:T(128)}, u32[]{:S(2)}, u32[]{:S(2)}) %collective-permute-start.3) | collective-permute-done | bytes 36 | tf_op jit(solution)/shard_map/ppermute | solution.py:294
  82.4 5.5 %all-to-all-done.1.in_hbm = bf16[16,512,128]{2,1,0:T(8,128)(2,1)S(1)} async-done(((bf16[16,512,128]{2,1,0:T(8,128)(2,1)}), bf16[16,512,128]{2,1,0:T(8,128)(2,1)S(1)}, u32[]{:S(2)}, u32[]{:S(2)}) %all-to-all-start.1) | async-done | bytes 2097184 | tf_op jit(solution)/shard_map/all_to_all | solution.py:290
  87.9 3.3 %shard_map.103 = (bf16[128,16,128]{2,1,0:T(8,128)(2,1)}, bf16[128,16,128]{2,1,0:T(8,128)(2,1)}, bf16[128,16,128]{2,1,0:T(8,128)(2,1)}, bf16[128,16,128]{2,1,0:T(8,128)(2,1)}) custom-call(bf16[16,512,128]{2,1,0:T(8,128)(2,1)S(1)} %all-to-all-done.1.in_hbm), custom_call_target="tpu_custom_call" | custom-call | tf_op jit(solution)/shard_map/pallas_call | solution.py:296
Async XLA Ops:
  55.4 32.5 %all-to-all-start.1 = ((bf16[16,512,128]{2,1,0:T(8,128)(2,1)}), bf16[16,512,128]{2,1,0:T(8,128)(2,1)S(1)}, u32[]{:S(2)}, u32[]{:S(2)}) async-start(bf16[16,512,128]{2,1,0:T(8,128)(2,1)} %get-tuple-element.11), calls=%async_computation.1 | async-start | bytes 4194304 | tf_op jit(solution)/shard_map/all_to_all | solution.py:290
  59.3 3.2 %collective-permute-start = (f32[1]{0:T(128)}, f32[1]{0:T(128)}, u32[]{:S(2)}, u32[]{:S(2)}) collective-permute-start(f32[1]{0:T(128)} %get-tuple-element.16), channel_id=1, source_target_pairs={{0,1},{1,2},{2,3},{3,4},{4,5},{5,6},{6,7},{7,8},{8,9},{9,10},{10,1... | collective-permute-start | bytes 20 | tf_op jit(solution)/shard_map/ppermute | solution.py:294
  63.7 3.7 %collective-permute-start.1 = (f32[1]{0:T(128)}, f32[1]{0:T(128)}, u32[]{:S(2)}, u32[]{:S(2)}) collective-permute-start(f32[1]{0:T(128)} %add.12), channel_id=1, source_target_pairs={{0,2},{1,3},{2,4},{3,5},{4,6},{5,7},{6,8},{7,9},{8,10},{9,11},{10,... | collective-permute-start | bytes 20 | tf_op jit(solution)/shard_map/ppermute | solution.py:294
  68.0 5.6 %collective-permute-start.2 = (f32[1]{0:T(128)}, f32[1]{0:T(128)}, u32[]{:S(2)}, u32[]{:S(2)}) collective-permute-start(f32[1]{0:T(128)} %add.13), channel_id=1, source_target_pairs={{0,4},{1,5},{2,6},{3,7},{4,8},{5,9},{6,10},{7,11},{8,12},{9,13},{1... | collective-permute-start | bytes 20 | tf_op jit(solution)/shard_map/ppermute | solution.py:294
  74.2 7.6 %collective-permute-start.3 = (f32[1]{0:T(128)}, f32[1]{0:T(128)}, u32[]{:S(2)}, u32[]{:S(2)}) collective-permute-start(f32[1]{0:T(128)} %add.14), channel_id=1, source_target_pairs={{0,8},{1,9},{2,10},{3,11},{4,12},{5,13},{6,14},{7,15},{8,0},{9,1},... | collective-permute-start | bytes 20 | tf_op jit(solution)/shard_map/ppermute | solution.py:294

commit v3 on v0

v3 whole, which is shorter than its diff:
```python
import functools

import jax
import jax.numpy as jnp
from jax import lax
from jax.experimental import pallas as pl
from jax.experimental.pallas import tpu as pltpu
from jax.sharding import PartitionSpec as P

NT = (((1,), (1,)), ((), ()))
NN = (((1,), (0,)), ((), ()))
LOG2E = 1.4426950408889634
HIDE = -1e30
BLK = 512
PAD = 16
PARTS = 2
MIB = 1024 * 1024


def dot(a, b, dims):
    return lax.dot_general(a, b, dims, preferred_element_type=jnp.float32)


def pack_body(q_hbm, k_hbm, v_hbm, c_hbm, hist_ref, out_hbm, held, wide, packed, in_sem, out_sem):
    _, rows, heads, hd = held.shape
    size = rows // PARTS
    loads, stores = [], []
    for stage in range(4 * PARTS):
        place, span = stage // PARTS, pl.ds(stage % PARTS * size, size)
        ref = (q_hbm, k_hbm, v_hbm, c_hbm)[place]
        load = pltpu.make_async_copy(ref.at[span], held.at[place, span], in_sem.at[stage])
        load.start()
        loads.append(load)
    ids = jnp.broadcast_to(hist_ref[...].astype(jnp.float32), (PAD, rows)).astype(jnp.bfloat16)
    for head in range(heads):
        packed[head, 4 * rows :, :] = ids
    for stage, load in enumerate(loads):
        load.wait()
        place, first, slot = stage // PARTS, stage % PARTS * size, stage % 4
        part = held[place, first : first + size]
        wide[slot] = part.astype(jnp.float32).reshape(size * heads, hd)
        for head in range(heads):
            part = wide[slot, pl.ds(head, size, stride=heads), :]
            packed[head, stage * size : (stage + 1) * size, :] = part.astype(jnp.bfloat16)
        span = pl.ds(stage * size, size if stage + 1 < len(loads) else size + PAD)
        store = pltpu.make_async_copy(
            packed.at[:, span, :], out_hbm.at[:, span, :], out_sem.at[stage]
        )
        store.start()
        stores.append(store)
    for store in stores:
        store.wait()


def unpack_body(in_hbm, a_hbm, b_hbm, c_hbm, d_hbm, held, wide, packed, in_sem, out_sem):
    _, rows, heads, hd = packed.shape
    size = rows // PARTS
    loads, stores = [], []
    for stage in range(4 * PARTS):
        span = pl.ds(stage * size, size)
        load = pltpu.make_async_copy(
            in_hbm.at[:, span, :], held.at[:, span, :], in_sem.at[stage]
        )
        load.start()
        loads.append(load)
    for stage, load in enumerate(loads):
        load.wait()
        place, span, slot = stage // PARTS, pl.ds(stage % PARTS * size, size), stage % 4
        for head in range(heads):
            part = held[head, stage * size : (stage + 1) * size, :]
            wide[slot, pl.ds(head, size, stride=heads), :] = part.astype(jnp.float32)
        packed[place, span] = wide[slot].reshape(size, heads, hd).astype(jnp.bfloat16)
        ref = (a_hbm, b_hbm, c_hbm, d_hbm)[place]
        store = pltpu.make_async_copy(packed.at[place, span], ref.at[span], out_sem.at[stage])
        store.start()
        stores.append(store)
    for store in stores:
        store.wait()


def attend_body(
    temper_ref,
    in_hbm,
    out_hbm,
    gt_ref,
    held,
    ids,
    done,
    logit,
    pgrad,
    k_t,
    v_t,
    dk_acc,
    dv_acc,
    o_acc,
    dq_acc,
    in_sem,
    out_sem,
):
    shards, rows, hd = held.shape[0], held.shape[1] // 4, held.shape[2]
    per = BLK // rows
    blocks = shards // per
    half = BLK // 2
    data = pl.ds(0, 4 * rows)

    def load(block):
        span = pl.ds(block * per, per)
        return pltpu.make_async_copy(
            in_hbm.at[span, data, :], held.at[span, data, :], in_sem.at[block]
        )

    def store(block, kind):
        span, part = pl.ds(block * per, per), pl.ds(2 * kind * rows, 2 * rows)
        return pltpu.make_async_copy(
            done.at[span, part, :], out_hbm.at[span, part, :], out_sem.at[kind, block]
        )

    load_ids = pltpu.make_async_copy(in_hbm.at[:, pl.ds(4 * rows, PAD), :], ids, in_sem.at[blocks])
    load_ids.start()
    for block in range(blocks):
        load(block).start()
    temper = temper_ref[lax.axis_index("ctx")]
    scale = temper * hd ** (-0.5)
    logit_scale = scale * LOG2E
    load_ids.wait()
    bound = shards * rows - (jnp.sum(ids[...].astype(jnp.float32)) * (1.0 / PAD)).astype(jnp.int32)

    def rows_of(place, block):
        part = held[pl.ds(block * per, per), place * rows : (place + 1) * rows, :]
        return part.reshape(BLK, hd)

    def identity(size):
        return (
            lax.broadcasted_iota(jnp.int32, (size, size), 0)
            == lax.broadcasted_iota(jnp.int32, (size, size), 1)
        ).astype(jnp.bfloat16)

    eye_hd = identity(hd)
    eye_half = identity(half)

    def turned(part):
        return dot(eye_hd, part, NT).astype(jnp.bfloat16)

    def put(place, block, value):
        value = value.astype(jnp.bfloat16)
        value = jnp.concatenate(
            [dot(eye_half, value[:, n * half : (n + 1) * half], NT) for n in range(2)], axis=0
        )
        done[pl.ds(block * per, per), place * rows : (place + 1) * rows, :] = value.astype(
            jnp.bfloat16
        ).reshape(per, rows, hd)

    def folded(x):
        return x.reshape(x.shape[0] // 8, 8, x.shape[1])

    def query_block(i, gt):
        load(i).wait()
        q_i, k_i, v_i, c_i = [rows_of(place, i) for place in range(4)]
        k_t[i] = turned(k_i)
        v_t[i] = turned(v_i)
        q_t, c_t = turned(q_i), turned(c_i)
        dk_acc[i] = jnp.zeros((hd, BLK), jnp.float32)
        dv_acc[i] = jnp.zeros((hd, BLK), jnp.float32)
        first_i = i * BLK
        cols = first_i + lax.broadcasted_iota(jnp.int32, (1, BLK), 1)
        low = jnp.where(cols >= bound, bound, 0)
        start = jnp.where(first_i >= bound, bound // BLK, 0)

        def scan_keys(j, carry):
            top, total, delta = carry
            first_j = j * BLK
            s = dot(rows_of(1, j), q_i, NT) * logit_scale
            row = lax.broadcasted_iota(jnp.int32, (BLK, BLK), 0)
            s = jnp.where((row <= cols - first_j) & (row >= low - first_j), s, HIDE)
            logit[j] = s
            s = folded(s)
            g = dot(rows_of(2, j), c_i, NT)
            pgrad[j] = g
            new_top = jnp.maximum(top, jnp.max(s, axis=0))
            keep = jnp.exp2(top - new_top)
            e = jnp.exp2(s - new_top[None])
            total = total * keep + jnp.sum(e, axis=0)
            delta = delta * keep + jnp.sum(e * folded(g), axis=0)
            return new_top, total, delta

        zero = jnp.zeros((8, BLK), jnp.float32)
        top, total, delta = lax.fori_loop(
            start, i + 1, scan_keys, (jnp.full((8, BLK), HIDE, jnp.float32), zero, zero)
        )
        top_all = jnp.max(top, axis=0, keepdims=True)
        part = jnp.exp2(top - top_all)
        total = jnp.sum(total * part, axis=0, keepdims=True)
        delta = jnp.sum(delta * part, axis=0, keepdims=True) / total
        norm = top_all + jnp.log2(total)
        o_acc[...] = jnp.zeros((hd, BLK), jnp.float32)
        dq_acc[...] = jnp.zeros((hd, BLK), jnp.float32)

        def gradients(j, gt):
            s = logit[j]
            p = jnp.exp2(s - norm)
            ds = p * (pgrad[j] - delta)
            gt = gt + jnp.sum(folded(ds * s), axis=0)
            p, ds = p.astype(jnp.bfloat16), ds.astype(jnp.bfloat16)
            dv_acc[j] += dot(c_t, p, NT)
            dk_acc[j] += dot(q_t, ds, NT)
            o_acc[...] += dot(v_t[j], p, NN)
            dq_acc[...] += dot(k_t[j], ds, NN)
            return gt

        gt = lax.fori_loop(start, i + 1, gradients, gt)
        put(0, i, o_acc[...])
        put(1, i, dq_acc[...] * scale)
        store(i, 0).start()
        return gt

    gt = lax.fori_loop(0, blocks, query_block, jnp.zeros((8, BLK), jnp.float32))
    for block in range(blocks):
        put(2, block, dk_acc[block] * scale)
        put(3, block, dv_acc[block])
        store(block, 1).start()
    gt_ref[0] = jnp.sum(gt) / (temper * LOG2E)
    for block in range(blocks):
        store(block, 0).wait()
        store(block, 1).wait()


def vmem_spec():
    return pl.BlockSpec(memory_space=pltpu.VMEM)


def any_spec():
    return pl.BlockSpec(memory_space=pl.ANY)


def grant(mib):
    return pltpu.CompilerParams(vmem_limit_bytes=mib * MIB)


def body(queries, keys, values, cotangent, history, temper):
    _, rows, heads, hd = queries.shape
    shards = lax.axis_size("ctx")
    blocks = shards * rows // BLK
    low, f32 = jnp.bfloat16, jnp.float32

    send = pl.pallas_call(
        pack_body,
        out_shape=jax.ShapeDtypeStruct((heads, 4 * rows + PAD, hd), low),
        in_specs=[any_spec()] * 4 + [vmem_spec()],
        out_specs=any_spec(),
        scratch_shapes=[
            pltpu.VMEM((4, rows, heads, hd), low),
            pltpu.VMEM((4, rows // PARTS * heads, hd), f32),
            pltpu.VMEM((heads, 4 * rows + PAD, hd), low),
            pltpu.SemaphoreType.DMA((4 * PARTS,)),
            pltpu.SemaphoreType.DMA((4 * PARTS,)),
        ],
        compiler_params=grant(56),
    )(queries[0], keys[0], values[0], cotangent[0], history)
    recv = lax.all_to_all(send, "ctx", split_axis=0, concat_axis=0, tiled=True)
    results, gt = pl.pallas_call(
        attend_body,
        out_shape=(
            jax.ShapeDtypeStruct((shards, 4 * rows, hd), low),
            jax.ShapeDtypeStruct((1,), f32),
        ),
        in_specs=[pl.BlockSpec(memory_space=pltpu.SMEM), any_spec()],
        out_specs=(any_spec(), pl.BlockSpec(memory_space=pltpu.SMEM)),
        scratch_shapes=[
            pltpu.VMEM((shards, 4 * rows, hd), low),
            pltpu.VMEM((shards, PAD, hd), low),
            pltpu.VMEM((shards, 4 * rows, hd), low),
            pltpu.VMEM((blocks, BLK, BLK), f32),
            pltpu.VMEM((blocks, BLK, BLK), f32),
            pltpu.VMEM((blocks, hd, BLK), low),
            pltpu.VMEM((blocks, hd, BLK), low),
            pltpu.VMEM((blocks, hd, BLK), f32),
            pltpu.VMEM((blocks, hd, BLK), f32),
            pltpu.VMEM((hd, BLK), f32),
            pltpu.VMEM((hd, BLK), f32),
            pltpu.SemaphoreType.DMA((blocks + 1,)),
            pltpu.SemaphoreType.DMA((2, blocks)),
        ],
        compiler_params=grant(60),
    )(temper, recv)
    back = lax.all_to_all(results, "ctx", split_axis=0, concat_axis=0, tiled=True)
    exp_size = lax.axis_size("exp")
    step = 1
    while step < exp_size:
        gt = gt + lax.ppermute(gt, "exp", [(n, (n + step) % exp_size) for n in range(exp_size)])
        step *= 2
    outs = pl.pallas_call(
        unpack_body,
        out_shape=[jax.ShapeDtypeStruct((rows, heads, hd), low)] * 4,
        in_specs=[any_spec()],
        out_specs=[any_spec()] * 4,
        scratch_shapes=[
            pltpu.VMEM((heads, 4 * rows, hd), low),
            pltpu.VMEM((4, rows // PARTS * heads, hd), f32),
            pltpu.VMEM((4, rows, heads, hd), low),
            pltpu.SemaphoreType.DMA((4 * PARTS,)),
            pltpu.SemaphoreType.DMA((4 * PARTS,)),
        ],
        compiler_params=grant(16),
    )(back)
    attn_out, grad_q, grad_k, grad_v = [part[None] for part in outs]
    return attn_out, grad_q, grad_k, grad_v, gt


def solution(mesh):
    placed = P("exp", "ctx", None, None)
    return jax.shard_map(
        body,
        mesh=mesh,
        in_specs=(placed, placed, placed, placed, P("exp", "ctx"), P()),
        out_specs=(placed, placed, placed, placed, P("ctx")),
        check_vma=False,
    )
```

time: 108 us -> 95 us (0.88)
  Pallas kernels: 35.1 us -> 24.1 us
  local copies, waits for them, and re-layouts: 1.34 us -> 0 us
    pallas_call x1, Pallas kernels: 26 us -> 16.9 us  [body(): pl.pallas_call(attend_body, out_shape=(jax.ShapeDtypeStruct((shards, 4 *...]
    pallas_call x1, Pallas kernels: 4.71 us -> 3.2 us  [body(): pl.pallas_call(unpack_body, out_shape=[jax.ShapeDtypeStruct((rows, heads,...]
    unnamed x2 -> x0, local copies, waits for them, and re-layouts: 1.34 us -> none
    ppermute x4, waiting for transfers between devices: 8.78 us -> 10.1 us  [body(): lax.ppermute(gt, 'exp', [(n, (n + step) % exp_size) for n in range(exp_si...]
where the time goes in v3:
time: 95 us; the launch traced here: 94.7 us
  blocking collectives  36.5 us (38%)
  Pallas kernels  24.1 us (25%)
  waiting for transfers between devices  15.6 us (16%)
  starting transfers between devices  13.8 us (15%)
  between operations  4.71 us (5%)
    all_to_all x1, blocking collectives, body(): recv = lax.all_to_all(send, 'ctx', split_axis=0, concat_axis=0, tiled=True)  36.5 us
    pallas_call x1, Pallas kernels, body(): pl.pallas_call(attend_body, out_shape=(jax.ShapeDtypeStruct((shards, 4 *...  16.9 us
    ppermute x4, starting transfers between devices, body(): lax.ppermute(gt, 'exp', [(n, (n + step) % exp_size) for n in range(exp_si...  10.1 us
    ppermute x4, waiting for transfers between devices, body(): lax.ppermute(gt, 'exp', [(n, (n + step) % exp_size) for n in range(exp_si...  10.1 us
    all_to_all x1, waiting for transfers between devices, body(): lax.all_to_all(results, 'ctx', split_axis=0, concat_axis=0, tiled=True)  5.53 us
    pallas_call x1, Pallas kernels, body(): pl.pallas_call(pack_body, out_shape=jax.ShapeDtypeStruct((heads, 4 * rows...  4.01 us
    all_to_all x1, starting transfers between devices, body(): lax.all_to_all(results, 'ctx', split_axis=0, concat_axis=0, tiled=True)  3.73 us
    pallas_call x1, Pallas kernels, body(): pl.pallas_call(unpack_body, out_shape=[jax.ShapeDtypeStruct((rows, heads,...  3.2 us
  transfers between devices with their start and end apart: 5, of which 5 were waited for; matrix products, arithmetic and copies ran while one was open for 0% of the time, Pallas kernels for 0%

profile of v3, /device:TPU:192, one launch (start us, length us, event | category | flops | bytes accessed | tf_op | source)
XLA Modules:
  0.0 94.7 jit_solution(14005030583155516052)
XLA Ops:
  0.6 4.0 %shard_map.101 = bf16[16,528,128]{2,1,0:T(8,128)(2,1)} custom-call(bf16[128,16,128]{2,1,0:T(8,128)(2,1)} %bitcast.8, bf16[128,16,128]{2,1,0:T(8,128)(2,1)} %bitcast.9, bf16[128,16,128]{2,1,0:T(8,128)(2,1)} %bitcast.10, bf16[128,16,128]{2,1,0:T(8,128)(2,1)} %bitcast.11, s32[1,128]{1,0:T(1,128)} %hist_ref.1), custom_call_target="tpu_custom_call" | custom-call | tf_op jit(solution)/shard_map/pallas_call | solution.py:245
  4.6 36.5 %all_to_all.10.in_hbm = bf16[16,528,128]{2,1,0:T(8,128)(2,1)} all-to-all(bf16[16,528,128]{2,1,0:T(8,128)(2,1)} %shard_map.101), channel_id=1, replica_groups=mesh['ctx'=16,'exp'=16] {'ctx'}, dimensions={0} | all-to-all | bytes 4325376 | tf_op jit(solution)/shard_map/all_to_all | solution.py:259
  41.1 16.9 %shard_map.102 = (bf16[16,512,128]{2,1,0:T(8,128)(2,1)}, f32[1]{0:T(128)}) custom-call(f32[16]{0:T(128)} %temper_ref.1, bf16[16,528,128]{2,1,0:T(8,128)(2,1)} %all_to_all.10.in_hbm), custom_call_target="tpu_custom_call" | custom-call | tf_op jit(solution)/shard_map/pallas_call | solution.py:260
  58.0 3.7 %all-to-all-start.1 = ((bf16[16,512,128]{2,1,0:T(8,128)(2,1)}), bf16[16,512,128]{2,1,0:T(8,128)(2,1)S(1)}, u32[]{:S(2)}, u32[]{:S(2)}) async-start(bf16[16,512,128]{2,1,0:T(8,128)(2,1)} %get-tuple-element.11), calls=%async_computation.1 | async-start | bytes 4194304 | tf_op jit(solution)/shard_map/all_to_all | solution.py:285
  61.8 0.0 collective-permute-start
  61.8 3.2 %collective-permute-done = f32[1]{0:T(128)} collective-permute-done((f32[1]{0:T(128)}, f32[1]{0:T(128)}, u32[]{:S(2)}, u32[]{:S(2)}) %collective-permute-start) | collective-permute-done | bytes 36 | tf_op jit(solution)/shard_map/ppermute | solution.py:289
  66.2 2.4 %collective-permute-start.1 = (f32[1]{0:T(128)}, f32[1]{0:T(128)}, u32[]{:S(2)}, u32[]{:S(2)}) collective-permute-start(f32[1]{0:T(128)} %add.12), channel_id=1, source_target_pairs={{0,2},{1,3},{2,4},{3,5},{4,6},{5,7},{6,8},{7,9},{8,10},{9,11},{10,... | collective-permute-start | bytes 20 | tf_op jit(solution)/shard_map/ppermute | solution.py:289
  68.6 1.3 %collective-permute-done.1 = f32[1]{0:T(128)} collective-permute-done((f32[1]{0:T(128)}, f32[1]{0:T(128)}, u32[]{:S(2)}, u32[]{:S(2)}) %collective-permute-start.1) | collective-permute-done | bytes 36 | tf_op jit(solution)/shard_map/ppermute | solution.py:289
  70.5 3.0 %collective-permute-start.2 = (f32[1]{0:T(128)}, f32[1]{0:T(128)}, u32[]{:S(2)}, u32[]{:S(2)}) collective-permute-start(f32[1]{0:T(128)} %add.13), channel_id=1, source_target_pairs={{0,4},{1,5},{2,6},{3,7},{4,8},{5,9},{6,10},{7,11},{8,12},{9,13},{1... | collective-permute-start | bytes 20 | tf_op jit(solution)/shard_map/ppermute | solution.py:289
  73.5 2.5 %collective-permute-done.2 = f32[1]{0:T(128)} collective-permute-done((f32[1]{0:T(128)}, f32[1]{0:T(128)}, u32[]{:S(2)}, u32[]{:S(2)}) %collective-permute-start.2) | collective-permute-done | bytes 36 | tf_op jit(solution)/shard_map/ppermute | solution.py:289
  76.6 4.6 %collective-permute-start.3 = (f32[1]{0:T(128)}, f32[1]{0:T(128)}, u32[]{:S(2)}, u32[]{:S(2)}) collective-permute-start(f32[1]{0:T(128)} %add.14), channel_id=1, source_target_pairs={{0,8},{1,9},{2,10},{3,11},{4,12},{5,13},{6,14},{7,15},{8,0},{9,1},... | collective-permute-start | bytes 20 | tf_op jit(solution)/shard_map/ppermute | solution.py:289
  81.3 3.0 %collective-permute-done.3 = f32[1]{0:T(128)} collective-permute-done((f32[1]{0:T(128)}, f32[1]{0:T(128)}, u32[]{:S(2)}, u32[]{:S(2)}) %collective-permute-start.3) | collective-permute-done | bytes 36 | tf_op jit(solution)/shard_map/ppermute | solution.py:289
  84.8 5.5 %all-to-all-done.1.in_hbm = bf16[16,512,128]{2,1,0:T(8,128)(2,1)S(1)} async-done(((bf16[16,512,128]{2,1,0:T(8,128)(2,1)}), bf16[16,512,128]{2,1,0:T(8,128)(2,1)S(1)}, u32[]{:S(2)}, u32[]{:S(2)}) %all-to-all-start.1) | async-done | bytes 2097184 | tf_op jit(solution)/shard_map/all_to_all | solution.py:285
  90.4 3.2 %shard_map.103 = (bf16[128,16,128]{2,1,0:T(8,128)(2,1)}, bf16[128,16,128]{2,1,0:T(8,128)(2,1)}, bf16[128,16,128]{2,1,0:T(8,128)(2,1)}, bf16[128,16,128]{2,1,0:T(8,128)(2,1)}) custom-call(bf16[16,512,128]{2,1,0:T(8,128)(2,1)S(1)} %all-to-all-done.1.in_hbm), custom_call_target="tpu_custom_call" | custom-call | tf_op jit(solution)/shard_map/pallas_call | solution.py:291
Async XLA Ops:
  58.0 32.3 %all-to-all-start.1 = ((bf16[16,512,128]{2,1,0:T(8,128)(2,1)}), bf16[16,512,128]{2,1,0:T(8,128)(2,1)S(1)}, u32[]{:S(2)}, u32[]{:S(2)}) async-start(bf16[16,512,128]{2,1,0:T(8,128)(2,1)} %get-tuple-element.11), calls=%async_computation.1 | async-start | bytes 4194304 | tf_op jit(solution)/shard_map/all_to_all | solution.py:285
  61.8 3.2 %collective-permute-start = (f32[1]{0:T(128)}, f32[1]{0:T(128)}, u32[]{:S(2)}, u32[]{:S(2)}) collective-permute-start(f32[1]{0:T(128)} %get-tuple-element.16), channel_id=1, source_target_pairs={{0,1},{1,2},{2,3},{3,4},{4,5},{5,6},{6,7},{7,8},{8,9},{9,10},{10,1... | collective-permute-start | bytes 20 | tf_op jit(solution)/shard_map/ppermute | solution.py:289
  66.2 3.7 %collective-permute-start.1 = (f32[1]{0:T(128)}, f32[1]{0:T(128)}, u32[]{:S(2)}, u32[]{:S(2)}) collective-permute-start(f32[1]{0:T(128)} %add.12), channel_id=1, source_target_pairs={{0,2},{1,3},{2,4},{3,5},{4,6},{5,7},{6,8},{7,9},{8,10},{9,11},{10,... | collective-permute-start | bytes 20 | tf_op jit(solution)/shard_map/ppermute | solution.py:289
  70.5 5.6 %collective-permute-start.2 = (f32[1]{0:T(128)}, f32[1]{0:T(128)}, u32[]{:S(2)}, u32[]{:S(2)}) collective-permute-start(f32[1]{0:T(128)} %add.13), channel_id=1, source_target_pairs={{0,4},{1,5},{2,6},{3,7},{4,8},{5,9},{6,10},{7,11},{8,12},{9,13},{1... | collective-permute-start | bytes 20 | tf_op jit(solution)/shard_map/ppermute | solution.py:289
  76.6 7.6 %collective-permute-start.3 = (f32[1]{0:T(128)}, f32[1]{0:T(128)}, u32[]{:S(2)}, u32[]{:S(2)}) collective-permute-start(f32[1]{0:T(128)} %add.14), channel_id=1, source_target_pairs={{0,8},{1,9},{2,10},{3,11},{4,12},{5,13},{6,14},{7,15},{8,0},{9,1},... | collective-permute-start | bytes 20 | tf_op jit(solution)/shard_map/ppermute | solution.py:289

commit v4 on v3

--- a/solution.py
+++ b/solution.py
@@ -9,6 +9,7 @@
 
 NT = (((1,), (1,)), ((), ()))
 NN = (((1,), (0,)), ((), ()))
+TN = (((0,), (0,)), ((), ()))
 LOG2E = 1.4426950408889634
 HIDE = -1e30
 BLK = 512
@@ -88,8 +89,6 @@
     done,
     logit,
     pgrad,
-    k_t,
-    v_t,
     dk_acc,
     dv_acc,
     o_acc,
@@ -100,7 +99,6 @@
     shards, rows, hd = held.shape[0], held.shape[1] // 4, held.shape[2]
     per = BLK // rows
     blocks = shards // per
-    half = BLK // 2
     data = pl.ds(0, 4 * rows)
 
     def load(block):
@@ -129,23 +127,7 @@
         part = held[pl.ds(block * per, per), place * rows : (place + 1) * rows, :]
         return part.reshape(BLK, hd)
 
-    def identity(size):
-        return (
-            lax.broadcasted_iota(jnp.int32, (size, size), 0)
-            == lax.broadcasted_iota(jnp.int32, (size, size), 1)
-        ).astype(jnp.bfloat16)
-
-    eye_hd = identity(hd)
-    eye_half = identity(half)
-
-    def turned(part):
-        return dot(eye_hd, part, NT).astype(jnp.bfloat16)
-
     def put(place, block, value):
-        value = value.astype(jnp.bfloat16)
-        value = jnp.concatenate(
-            [dot(eye_half, value[:, n * half : (n + 1) * half], NT) for n in range(2)], axis=0
-        )
         done[pl.ds(block * per, per), place * rows : (place + 1) * rows, :] = value.astype(
             jnp.bfloat16
         ).reshape(per, rows, hd)
@@ -155,12 +137,9 @@
 
     def query_block(i, gt):
         load(i).wait()
-        q_i, k_i, v_i, c_i = [rows_of(place, i) for place in range(4)]
-        k_t[i] = turned(k_i)
-        v_t[i] = turned(v_i)
-        q_t, c_t = turned(q_i), turned(c_i)
-        dk_acc[i] = jnp.zeros((hd, BLK), jnp.float32)
-        dv_acc[i] = jnp.zeros((hd, BLK), jnp.float32)
+        q_i, c_i = rows_of(0, i), rows_of(3, i)
+        dk_acc[i] = jnp.zeros((BLK, hd), jnp.float32)
+        dv_acc[i] = jnp.zeros((BLK, hd), jnp.float32)
         first_i = i * BLK
         cols = first_i + lax.broadcasted_iota(jnp.int32, (1, BLK), 1)
         low = jnp.where(cols >= bound, bound, 0)
@@ -192,8 +171,8 @@
         total = jnp.sum(total * part, axis=0, keepdims=True)
         delta = jnp.sum(delta * part, axis=0, keepdims=True) / total
         norm = top_all + jnp.log2(total)
-        o_acc[...] = jnp.zeros((hd, BLK), jnp.float32)
-        dq_acc[...] = jnp.zeros((hd, BLK), jnp.float32)
+        o_acc[...] = jnp.zeros((BLK, hd), jnp.float32)
+        dq_acc[...] = jnp.zeros((BLK, hd), jnp.float32)
 
         def gradients(j, gt):
             s = logit[j]
@@ -201,10 +180,10 @@
             ds = p * (pgrad[j] - delta)
             gt = gt + jnp.sum(folded(ds * s), axis=0)
             p, ds = p.astype(jnp.bfloat16), ds.astype(jnp.bfloat16)
-            dv_acc[j] += dot(c_t, p, NT)
-            dk_acc[j] += dot(q_t, ds, NT)
-            o_acc[...] += dot(v_t[j], p, NN)
-            dq_acc[...] += dot(k_t[j], ds, NN)
+            dv_acc[j] += dot(p, c_i, NN)
+            dk_acc[j] += dot(ds, q_i, NN)
+            o_acc[...] += dot(p, rows_of(2, j), TN)
+            dq_acc[...] += dot(ds, rows_of(1, j), TN)
             return gt
 
         gt = lax.fori_loop(start, i + 1, gradients, gt)
@@ -271,12 +250,10 @@
             pltpu.VMEM((shards, 4 * rows, hd), low),
             pltpu.VMEM((blocks, BLK, BLK), f32),
             pltpu.VMEM((blocks, BLK, BLK), f32),
-            pltpu.VMEM((blocks, hd, BLK), low),
-            pltpu.VMEM((blocks, hd, BLK), low),
-            pltpu.VMEM((blocks, hd, BLK), f32),
-            pltpu.VMEM((blocks, hd, BLK), f32),
-            pltpu.VMEM((hd, BLK), f32),
-            pltpu.VMEM((hd, BLK), f32),
+            pltpu.VMEM((blocks, BLK, hd), f32),
+            pltpu.VMEM((blocks, BLK, hd), f32),
+            pltpu.VMEM((BLK, hd), f32),
+            pltpu.VMEM((BLK, hd), f32),
             pltpu.SemaphoreType.DMA((blocks + 1,)),
             pltpu.SemaphoreType.DMA((2, blocks)),
         ],

time: 95 us -> 93.2 us (0.981)
  Pallas kernels: 24.1 us -> 22.2 us
    pallas_call x1, Pallas kernels: 16.9 us -> 15 us  [body(): pl.pallas_call(attend_body, out_shape=(jax.ShapeDtypeStruct((shards, 4 *...]
where the time goes in v4:
time: 93.2 us; the launch traced here: 92.9 us
  blocking collectives  36.5 us (39%)
  Pallas kernels  22.2 us (24%)
  waiting for transfers between devices  15.6 us (17%)
  starting transfers between devices  13.8 us (15%)
  between operations  4.71 us (5%)
    all_to_all x1, blocking collectives, body(): recv = lax.all_to_all(send, 'ctx', split_axis=0, concat_axis=0, tiled=True)  36.5 us
    pallas_call x1, Pallas kernels, body(): pl.pallas_call(attend_body, out_shape=(jax.ShapeDtypeStruct((shards, 4 *...  15 us
    ppermute x4, starting transfers between devices, body(): lax.ppermute(gt, 'exp', [(n, (n + step) % exp_size) for n in range(exp_si...  10.1 us
    ppermute x4, waiting for transfers between devices, body(): lax.ppermute(gt, 'exp', [(n, (n + step) % exp_size) for n in range(exp_si...  10.1 us
    all_to_all x1, waiting for transfers between devices, body(): lax.all_to_all(results, 'ctx', split_axis=0, concat_axis=0, tiled=True)  5.54 us
    pallas_call x1, Pallas kernels, body(): pl.pallas_call(pack_body, out_shape=jax.ShapeDtypeStruct((heads, 4 * rows...  4.01 us
    all_to_all x1, starting transfers between devices, body(): lax.all_to_all(results, 'ctx', split_axis=0, concat_axis=0, tiled=True)  3.73 us
    pallas_call x1, Pallas kernels, body(): pl.pallas_call(unpack_body, out_shape=[jax.ShapeDtypeStruct((rows, heads,...  3.2 us
  transfers between devices with their start and end apart: 5, of which 5 were waited for; matrix products, arithmetic and copies ran while one was open for 0% of the time, Pallas kernels for 0%

profile of v4, /device:TPU:192, one launch (start us, length us, event | category | flops | bytes accessed | tf_op | source)
XLA Modules:
  0.0 92.9 jit_solution(4325512918850777198)
XLA Ops:
  0.6 4.0 %shard_map.101 = bf16[16,528,128]{2,1,0:T(8,128)(2,1)} custom-call(bf16[128,16,128]{2,1,0:T(8,128)(2,1)} %bitcast.8, bf16[128,16,128]{2,1,0:T(8,128)(2,1)} %bitcast.9, bf16[128,16,128]{2,1,0:T(8,128)(2,1)} %bitcast.10, bf16[128,16,128]{2,1,0:T(8,128)(2,1)} %bitcast.11, s32[1,128]{1,0:T(1,128)} %hist_ref.1), custom_call_target="tpu_custom_call" | custom-call | tf_op jit(solution)/shard_map/pallas_call | solution.py:224
  4.6 36.5 %all_to_all.10.in_hbm = bf16[16,528,128]{2,1,0:T(8,128)(2,1)} all-to-all(bf16[16,528,128]{2,1,0:T(8,128)(2,1)} %shard_map.101), channel_id=1, replica_groups=mesh['ctx'=16,'exp'=16] {'ctx'}, dimensions={0} | all-to-all | bytes 4325376 | tf_op jit(solution)/shard_map/all_to_all | solution.py:238
  41.1 15.0 %shard_map.102 = (bf16[16,512,128]{2,1,0:T(8,128)(2,1)}, f32[1]{0:T(128)}) custom-call(f32[16]{0:T(128)} %temper_ref.1, bf16[16,528,128]{2,1,0:T(8,128)(2,1)} %all_to_all.10.in_hbm), custom_call_target="tpu_custom_call" | custom-call | tf_op jit(solution)/shard_map/pallas_call | solution.py:239
  56.2 3.7 %all-to-all-start.1 = ((bf16[16,512,128]{2,1,0:T(8,128)(2,1)}), bf16[16,512,128]{2,1,0:T(8,128)(2,1)S(1)}, u32[]{:S(2)}, u32[]{:S(2)}) async-start(bf16[16,512,128]{2,1,0:T(8,128)(2,1)} %get-tuple-element.11), calls=%async_computation.1 | async-start | bytes 4194304 | tf_op jit(solution)/shard_map/all_to_all | solution.py:262
  59.9 0.0 collective-permute-start
  59.9 3.2 %collective-permute-done = f32[1]{0:T(128)} collective-permute-done((f32[1]{0:T(128)}, f32[1]{0:T(128)}, u32[]{:S(2)}, u32[]{:S(2)}) %collective-permute-start) | collective-permute-done | bytes 36 | tf_op jit(solution)/shard_map/ppermute | solution.py:266
  64.3 2.4 %collective-permute-start.1 = (f32[1]{0:T(128)}, f32[1]{0:T(128)}, u32[]{:S(2)}, u32[]{:S(2)}) collective-permute-start(f32[1]{0:T(128)} %add.12), channel_id=1, source_target_pairs={{0,2},{1,3},{2,4},{3,5},{4,6},{5,7},{6,8},{7,9},{8,10},{9,11},{10,... | collective-permute-start | bytes 20 | tf_op jit(solution)/shard_map/ppermute | solution.py:266
  66.7 1.3 %collective-permute-done.1 = f32[1]{0:T(128)} collective-permute-done((f32[1]{0:T(128)}, f32[1]{0:T(128)}, u32[]{:S(2)}, u32[]{:S(2)}) %collective-permute-start.1) | collective-permute-done | bytes 36 | tf_op jit(solution)/shard_map/ppermute | solution.py:266
  68.6 3.1 %collective-permute-start.2 = (f32[1]{0:T(128)}, f32[1]{0:T(128)}, u32[]{:S(2)}, u32[]{:S(2)}) collective-permute-start(f32[1]{0:T(128)} %add.13), channel_id=1, source_target_pairs={{0,4},{1,5},{2,6},{3,7},{4,8},{5,9},{6,10},{7,11},{8,12},{9,13},{1... | collective-permute-start | bytes 20 | tf_op jit(solution)/shard_map/ppermute | solution.py:266
  71.7 2.5 %collective-permute-done.2 = f32[1]{0:T(128)} collective-permute-done((f32[1]{0:T(128)}, f32[1]{0:T(128)}, u32[]{:S(2)}, u32[]{:S(2)}) %collective-permute-start.2) | collective-permute-done | bytes 36 | tf_op jit(solution)/shard_map/ppermute | solution.py:266
  74.8 4.6 %collective-permute-start.3 = (f32[1]{0:T(128)}, f32[1]{0:T(128)}, u32[]{:S(2)}, u32[]{:S(2)}) collective-permute-start(f32[1]{0:T(128)} %add.14), channel_id=1, source_target_pairs={{0,8},{1,9},{2,10},{3,11},{4,12},{5,13},{6,14},{7,15},{8,0},{9,1},... | collective-permute-start | bytes 20 | tf_op jit(solution)/shard_map/ppermute | solution.py:266
  79.4 3.0 %collective-permute-done.3 = f32[1]{0:T(128)} collective-permute-done((f32[1]{0:T(128)}, f32[1]{0:T(128)}, u32[]{:S(2)}, u32[]{:S(2)}) %collective-permute-start.3) | collective-permute-done | bytes 36 | tf_op jit(solution)/shard_map/ppermute | solution.py:266
  83.0 5.5 %all-to-all-done.1.in_hbm = bf16[16,512,128]{2,1,0:T(8,128)(2,1)S(1)} async-done(((bf16[16,512,128]{2,1,0:T(8,128)(2,1)}), bf16[16,512,128]{2,1,0:T(8,128)(2,1)S(1)}, u32[]{:S(2)}, u32[]{:S(2)}) %all-to-all-start.1) | async-done | bytes 2097184 | tf_op jit(solution)/shard_map/all_to_all | solution.py:262
  88.5 3.2 %shard_map.103 = (bf16[128,16,128]{2,1,0:T(8,128)(2,1)}, bf16[128,16,128]{2,1,0:T(8,128)(2,1)}, bf16[128,16,128]{2,1,0:T(8,128)(2,1)}, bf16[128,16,128]{2,1,0:T(8,128)(2,1)}) custom-call(bf16[16,512,128]{2,1,0:T(8,128)(2,1)S(1)} %all-to-all-done.1.in_hbm), custom_call_target="tpu_custom_call" | custom-call | tf_op jit(solution)/shard_map/pallas_call | solution.py:268
Async XLA Ops:
  56.2 32.3 %all-to-all-start.1 = ((bf16[16,512,128]{2,1,0:T(8,128)(2,1)}), bf16[16,512,128]{2,1,0:T(8,128)(2,1)S(1)}, u32[]{:S(2)}, u32[]{:S(2)}) async-start(bf16[16,512,128]{2,1,0:T(8,128)(2,1)} %get-tuple-element.11), calls=%async_computation.1 | async-start | bytes 4194304 | tf_op jit(solution)/shard_map/all_to_all | solution.py:262
  59.9 3.2 %collective-permute-start = (f32[1]{0:T(128)}, f32[1]{0:T(128)}, u32[]{:S(2)}, u32[]{:S(2)}) collective-permute-start(f32[1]{0:T(128)} %get-tuple-element.16), channel_id=1, source_target_pairs={{0,1},{1,2},{2,3},{3,4},{4,5},{5,6},{6,7},{7,8},{8,9},{9,10},{10,1... | collective-permute-start | bytes 20 | tf_op jit(solution)/shard_map/ppermute | solution.py:266
  64.3 3.7 %collective-permute-start.1 = (f32[1]{0:T(128)}, f32[1]{0:T(128)}, u32[]{:S(2)}, u32[]{:S(2)}) collective-permute-start(f32[1]{0:T(128)} %add.12), channel_id=1, source_target_pairs={{0,2},{1,3},{2,4},{3,5},{4,6},{5,7},{6,8},{7,9},{8,10},{9,11},{10,... | collective-permute-start | bytes 20 | tf_op jit(solution)/shard_map/ppermute | solution.py:266
  68.6 5.6 %collective-permute-start.2 = (f32[1]{0:T(128)}, f32[1]{0:T(128)}, u32[]{:S(2)}, u32[]{:S(2)}) collective-permute-start(f32[1]{0:T(128)} %add.13), channel_id=1, source_target_pairs={{0,4},{1,5},{2,6},{3,7},{4,8},{5,9},{6,10},{7,11},{8,12},{9,13},{1... | collective-permute-start | bytes 20 | tf_op jit(solution)/shard_map/ppermute | solution.py:266
  74.8 7.6 %collective-permute-start.3 = (f32[1]{0:T(128)}, f32[1]{0:T(128)}, u32[]{:S(2)}, u32[]{:S(2)}) collective-permute-start(f32[1]{0:T(128)} %add.14), channel_id=1, source_target_pairs={{0,8},{1,9},{2,10},{3,11},{4,12},{5,13},{6,14},{7,15},{8,0},{9,1},... | collective-permute-start | bytes 20 | tf_op jit(solution)/shard_map/ppermute | solution.py:266

commit v5 on v2

--- a/solution.py
+++ b/solution.py
@@ -9,10 +9,12 @@
 
 NT = (((1,), (1,)), ((), ()))
 NN = (((1,), (0,)), ((), ()))
+TN = (((0,), (0,)), ((), ()))
 LOG2E = 1.4426950408889634
 HIDE = -1e30
 BLK = 256
 PAD = 16
+PARTS = 2
 MIB = 1024 * 1024
 
 
@@ -22,25 +24,28 @@
 
 def pack_body(q_hbm, k_hbm, v_hbm, c_hbm, hist_ref, out_hbm, held, wide, packed, in_sem, out_sem):
     _, rows, heads, hd = held.shape
-    loads = [
-        pltpu.make_async_copy(ref, held.at[place], in_sem.at[place])
-        for place, ref in enumerate((q_hbm, k_hbm, v_hbm, c_hbm))
-    ]
-    for load in loads:
+    size = rows // PARTS
+    loads, stores = [], []
+    for stage in range(4 * PARTS):
+        place, span = stage // PARTS, pl.ds(stage % PARTS * size, size)
+        ref = (q_hbm, k_hbm, v_hbm, c_hbm)[place]
+        load = pltpu.make_async_copy(ref.at[span], held.at[place, span], in_sem.at[stage])
         load.start()
+        loads.append(load)
     ids = jnp.broadcast_to(hist_ref[...].astype(jnp.float32), (PAD, rows)).astype(jnp.bfloat16)
     for head in range(heads):
         packed[head, 4 * rows :, :] = ids
-    stores = []
-    for place, load in enumerate(loads):
+    for stage, load in enumerate(loads):
         load.wait()
-        wide[place % 2] = held[place].astype(jnp.float32).reshape(rows * heads, hd)
+        place, first, slot = stage // PARTS, stage % PARTS * size, stage % 4
+        part = held[place, first : first + size]
+        wide[slot] = part.astype(jnp.float32).reshape(size * heads, hd)
         for head in range(heads):
-            part = wide[place % 2, pl.ds(head, rows, stride=heads), :]
-            packed[head, place * rows : (place + 1) * rows, :] = part.astype(jnp.bfloat16)
-        span = pl.ds(place * rows, rows if place < 3 else rows + PAD)
+            part = wide[slot, pl.ds(head, size, stride=heads), :]
+            packed[head, stage * size : (stage + 1) * size, :] = part.astype(jnp.bfloat16)
+        span = pl.ds(stage * size, size if stage + 1 < len(loads) else size + PAD)
         store = pltpu.make_async_copy(
-            packed.at[:, span, :], out_hbm.at[:, span, :], out_sem.at[place]
+            packed.at[:, span, :], out_hbm.at[:, span, :], out_sem.at[stage]
         )
         store.start()
         stores.append(store)
@@ -50,22 +55,24 @@
 
 def unpack_body(in_hbm, a_hbm, b_hbm, c_hbm, d_hbm, held, wide, packed, in_sem, out_sem):
     _, rows, heads, hd = packed.shape
-    loads = []
-    for place in range(4):
-        span = pl.ds(place * rows, rows)
+    size = rows // PARTS
+    loads, stores = [], []
+    for stage in range(4 * PARTS):
+        span = pl.ds(stage * size, size)
         load = pltpu.make_async_copy(
-            in_hbm.at[:, span, :], held.at[:, span, :], in_sem.at[place]
+            in_hbm.at[:, span, :], held.at[:, span, :], in_sem.at[stage]
         )
         load.start()
         loads.append(load)
-    stores = []
-    for place, ref in enumerate((a_hbm, b_hbm, c_hbm, d_hbm)):
-        loads[place].wait()
+    for stage, load in enumerate(loads):
+        load.wait()
+        place, span, slot = stage // PARTS, pl.ds(stage % PARTS * size, size), stage % 4
         for head in range(heads):
-            part = held[head, place * rows : (place + 1) * rows, :]
-            wide[place % 2, pl.ds(head, rows, stride=heads), :] = part.astype(jnp.float32)
-        packed[place] = wide[place % 2].reshape(rows, heads, hd).astype(jnp.bfloat16)
-        store = pltpu.make_async_copy(packed.at[place], ref, out_sem.at[place])
+            part = held[head, stage * size : (stage + 1) * size, :]
+            wide[slot, pl.ds(head, size, stride=heads), :] = part.astype(jnp.float32)
+        packed[place, span] = wide[slot].reshape(size, heads, hd).astype(jnp.bfloat16)
+        ref = (a_hbm, b_hbm, c_hbm, d_hbm)[place]
+        store = pltpu.make_async_copy(packed.at[place, span], ref.at[span], out_sem.at[stage])
         store.start()
         stores.append(store)
     for store in stores:
@@ -81,7 +88,6 @@
     done,
     logit,
     pgrad,
-    k_t,
     v_t,
     dk_acc,
     dv_acc,
@@ -131,7 +137,6 @@
 
     def turn(low, high):
         span = slice(low * BLK, high * BLK)
-        k_t[:, span] = dot(eye_hd, span_of(1, low, high), NT).astype(jnp.bfloat16)
         v_t[:, span] = dot(eye_hd, span_of(2, low, high), NT).astype(jnp.bfloat16)
 
     def folded(x):
@@ -198,9 +203,9 @@
         dk_acc[span, :] = dk[(i - low) * BLK :]
         span = slice(low * BLK, high * BLK)
         o = dot(v_t[:, span], p, NN).astype(jnp.bfloat16)
-        dq = (dot(k_t[:, span], ds, NN) * scale).astype(jnp.bfloat16)
+        dq = dot(ds, span_of(1, low, high), TN) * scale
         put(0, i, dot(eye_blk, o, NT))
-        put(1, i, dot(eye_blk, dq, NT))
+        put(1, i, dq)
         return gt
 
     loads[0].wait()
@@ -257,10 +262,10 @@
         out_specs=any_spec(),
         scratch_shapes=[
             pltpu.VMEM((4, rows, heads, hd), low),
-            pltpu.VMEM((2, rows * heads, hd), f32),
+            pltpu.VMEM((4, rows // PARTS * heads, hd), f32),
             pltpu.VMEM((heads, 4 * rows + PAD, hd), low),
-            pltpu.SemaphoreType.DMA((4,)),
-            pltpu.SemaphoreType.DMA((4,)),
+            pltpu.SemaphoreType.DMA((4 * PARTS,)),
+            pltpu.SemaphoreType.DMA((4 * PARTS,)),
         ],
         compiler_params=grant(56),
     )(queries[0], keys[0], values[0], cotangent[0], history)
@@ -278,7 +283,6 @@
             pltpu.VMEM((shards, 4 * rows, hd), low),
             pltpu.VMEM((blocks, blocks * BLK, BLK), f32),
             pltpu.VMEM((blocks, blocks * BLK, BLK), f32),
-            pltpu.VMEM((hd, blocks * BLK), low),
             pltpu.VMEM((hd, blocks * BLK), low),
             pltpu.VMEM((blocks * BLK, hd), f32),
             pltpu.VMEM((blocks * BLK, hd), f32),
@@ -300,10 +304,10 @@
         out_specs=[any_spec()] * 4,
         scratch_shapes=[
             pltpu.VMEM((heads, 4 * rows, hd), low),
-            pltpu.VMEM((2, rows * heads, hd), f32),
+            pltpu.VMEM((4, rows // PARTS * heads, hd), f32),
             pltpu.VMEM((4, rows, heads, hd), low),
-            pltpu.SemaphoreType.DMA((4,)),
-            pltpu.SemaphoreType.DMA((4,)),
+            pltpu.SemaphoreType.DMA((4 * PARTS,)),
+            pltpu.SemaphoreType.DMA((4 * PARTS,)),
         ],
         compiler_params=grant(16),
     )(back)

time: 92.7 us -> 91.6 us (0.988)
  Pallas kernels: 21.6 us -> 20.6 us
where the time goes in v5:
time: 91.6 us; the launch traced here: 91.2 us
  blocking collectives  36.5 us (40%)
  Pallas kernels  20.6 us (22%)
  waiting for transfers between devices  15.6 us (17%)
  starting transfers between devices  13.8 us (15%)
  between operations  4.71 us (5%)
    all_to_all x1, blocking collectives, body(): recv = lax.all_to_all(send, 'ctx', split_axis=0, concat_axis=0, tiled=True)  36.5 us
    pallas_call x1, Pallas kernels, body(): pl.pallas_call(attend_body, out_shape=(jax.ShapeDtypeStruct((shards, 4 *...  13.4 us
    ppermute x4, starting transfers between devices, body(): lax.ppermute(gt, 'exp', [(n, (n + step) % exp_size) for n in range(exp_si...  10.1 us
    ppermute x4, waiting for transfers between devices, body(): lax.ppermute(gt, 'exp', [(n, (n + step) % exp_size) for n in range(exp_si...  10.1 us
    all_to_all x1, waiting for transfers between devices, body(): lax.all_to_all(results, 'ctx', split_axis=0, concat_axis=0, tiled=True)  5.53 us
    pallas_call x1, Pallas kernels, body(): pl.pallas_call(pack_body, out_shape=jax.ShapeDtypeStruct((heads, 4 * rows...  4.01 us
    all_to_all x1, starting transfers between devices, body(): lax.all_to_all(results, 'ctx', split_axis=0, concat_axis=0, tiled=True)  3.73 us
    pallas_call x1, Pallas kernels, body(): pl.pallas_call(unpack_body, out_shape=[jax.ShapeDtypeStruct((rows, heads,...  3.2 us
  transfers between devices with their start and end apart: 5, of which 5 were waited for; matrix products, arithmetic and copies ran while one was open for 0% of the time, Pallas kernels for 0%

profile of v5, /device:TPU:192, one launch (start us, length us, event | category | flops | bytes accessed | tf_op | source)
XLA Modules:
  0.0 91.2 jit_solution(11736923336572954620)
XLA Ops:
  0.6 4.0 %shard_map.101 = bf16[16,528,128]{2,1,0:T(8,128)(2,1)} custom-call(bf16[128,16,128]{2,1,0:T(8,128)(2,1)} %bitcast.8, bf16[128,16,128]{2,1,0:T(8,128)(2,1)} %bitcast.9, bf16[128,16,128]{2,1,0:T(8,128)(2,1)} %bitcast.10, bf16[128,16,128]{2,1,0:T(8,128)(2,1)} %bitcast.11, s32[1,128]{1,0:T(1,128)} %hist_ref.1), custom_call_target="tpu_custom_call" | custom-call | tf_op jit(solution)/shard_map/pallas_call | solution.py:258
  4.6 36.5 %all_to_all.10.in_hbm = bf16[16,528,128]{2,1,0:T(8,128)(2,1)} all-to-all(bf16[16,528,128]{2,1,0:T(8,128)(2,1)} %shard_map.101), channel_id=1, replica_groups=mesh['ctx'=16,'exp'=16] {'ctx'}, dimensions={0} | all-to-all | bytes 4325376 | tf_op jit(solution)/shard_map/all_to_all | solution.py:272
  41.1 13.4 %shard_map.102 = (bf16[16,512,128]{2,1,0:T(8,128)(2,1)}, f32[1]{0:T(128)}) custom-call(f32[16]{0:T(128)} %temper_ref.1, bf16[16,528,128]{2,1,0:T(8,128)(2,1)} %all_to_all.10.in_hbm), custom_call_target="tpu_custom_call" | custom-call | tf_op jit(solution)/shard_map/pallas_call | solution.py:273
  54.6 3.7 %all-to-all-start.1 = ((bf16[16,512,128]{2,1,0:T(8,128)(2,1)}), bf16[16,512,128]{2,1,0:T(8,128)(2,1)S(1)}, u32[]{:S(2)}, u32[]{:S(2)}) async-start(bf16[16,512,128]{2,1,0:T(8,128)(2,1)} %get-tuple-element.11), calls=%async_computation.1 | async-start | bytes 4194304 | tf_op jit(solution)/shard_map/all_to_all | solution.py:294
  58.3 0.0 collective-permute-start
  58.3 3.2 %collective-permute-done = f32[1]{0:T(128)} collective-permute-done((f32[1]{0:T(128)}, f32[1]{0:T(128)}, u32[]{:S(2)}, u32[]{:S(2)}) %collective-permute-start) | collective-permute-done | bytes 36 | tf_op jit(solution)/shard_map/ppermute | solution.py:298
  62.7 2.4 %collective-permute-start.1 = (f32[1]{0:T(128)}, f32[1]{0:T(128)}, u32[]{:S(2)}, u32[]{:S(2)}) collective-permute-start(f32[1]{0:T(128)} %add.12), channel_id=1, source_target_pairs={{0,2},{1,3},{2,4},{3,5},{4,6},{5,7},{6,8},{7,9},{8,10},{9,11},{10,... | collective-permute-start | bytes 20 | tf_op jit(solution)/shard_map/ppermute | solution.py:298
  65.1 1.3 %collective-permute-done.1 = f32[1]{0:T(128)} collective-permute-done((f32[1]{0:T(128)}, f32[1]{0:T(128)}, u32[]{:S(2)}, u32[]{:S(2)}) %collective-permute-start.1) | collective-permute-done | bytes 36 | tf_op jit(solution)/shard_map/ppermute | solution.py:298
  67.0 3.0 %collective-permute-start.2 = (f32[1]{0:T(128)}, f32[1]{0:T(128)}, u32[]{:S(2)}, u32[]{:S(2)}) collective-permute-start(f32[1]{0:T(128)} %add.13), channel_id=1, source_target_pairs={{0,4},{1,5},{2,6},{3,7},{4,8},{5,9},{6,10},{7,11},{8,12},{9,13},{1... | collective-permute-start | bytes 20 | tf_op jit(solution)/shard_map/ppermute | solution.py:298
  70.1 2.5 %collective-permute-done.2 = f32[1]{0:T(128)} collective-permute-done((f32[1]{0:T(128)}, f32[1]{0:T(128)}, u32[]{:S(2)}, u32[]{:S(2)}) %collective-permute-start.2) | collective-permute-done | bytes 36 | tf_op jit(solution)/shard_map/ppermute | solution.py:298
  73.2 4.6 %collective-permute-start.3 = (f32[1]{0:T(128)}, f32[1]{0:T(128)}, u32[]{:S(2)}, u32[]{:S(2)}) collective-permute-start(f32[1]{0:T(128)} %add.14), channel_id=1, source_target_pairs={{0,8},{1,9},{2,10},{3,11},{4,12},{5,13},{6,14},{7,15},{8,0},{9,1},... | collective-permute-start | bytes 20 | tf_op jit(solution)/shard_map/ppermute | solution.py:298
  77.8 3.0 %collective-permute-done.3 = f32[1]{0:T(128)} collective-permute-done((f32[1]{0:T(128)}, f32[1]{0:T(128)}, u32[]{:S(2)}, u32[]{:S(2)}) %collective-permute-start.3) | collective-permute-done | bytes 36 | tf_op jit(solution)/shard_map/ppermute | solution.py:298
  81.4 5.5 %all-to-all-done.1.in_hbm = bf16[16,512,128]{2,1,0:T(8,128)(2,1)S(1)} async-done(((bf16[16,512,128]{2,1,0:T(8,128)(2,1)}), bf16[16,512,128]{2,1,0:T(8,128)(2,1)S(1)}, u32[]{:S(2)}, u32[]{:S(2)}) %all-to-all-start.1) | async-done | bytes 2097184 | tf_op jit(solution)/shard_map/all_to_all | solution.py:294
  86.9 3.2 %shard_map.103 = (bf16[128,16,128]{2,1,0:T(8,128)(2,1)}, bf16[128,16,128]{2,1,0:T(8,128)(2,1)}, bf16[128,16,128]{2,1,0:T(8,128)(2,1)}, bf16[128,16,128]{2,1,0:T(8,128)(2,1)}) custom-call(bf16[16,512,128]{2,1,0:T(8,128)(2,1)S(1)} %all-to-all-done.1.in_hbm), custom_call_target="tpu_custom_call" | custom-call | tf_op jit(solution)/shard_map/pallas_call | solution.py:300
Async XLA Ops:
  54.6 32.3 %all-to-all-start.1 = ((bf16[16,512,128]{2,1,0:T(8,128)(2,1)}), bf16[16,512,128]{2,1,0:T(8,128)(2,1)S(1)}, u32[]{:S(2)}, u32[]{:S(2)}) async-start(bf16[16,512,128]{2,1,0:T(8,128)(2,1)} %get-tuple-element.11), calls=%async_computation.1 | async-start | bytes 4194304 | tf_op jit(solution)/shard_map/all_to_all | solution.py:294
  58.3 3.2 %collective-permute-start = (f32[1]{0:T(128)}, f32[1]{0:T(128)}, u32[]{:S(2)}, u32[]{:S(2)}) collective-permute-start(f32[1]{0:T(128)} %get-tuple-element.16), channel_id=1, source_target_pairs={{0,1},{1,2},{2,3},{3,4},{4,5},{5,6},{6,7},{7,8},{8,9},{9,10},{10,1... | collective-permute-start | bytes 20 | tf_op jit(solution)/shard_map/ppermute | solution.py:298
  62.7 3.7 %collective-permute-start.1 = (f32[1]{0:T(128)}, f32[1]{0:T(128)}, u32[]{:S(2)}, u32[]{:S(2)}) collective-permute-start(f32[1]{0:T(128)} %add.12), channel_id=1, source_target_pairs={{0,2},{1,3},{2,4},{3,5},{4,6},{5,7},{6,8},{7,9},{8,10},{9,11},{10,... | collective-permute-start | bytes 20 | tf_op jit(solution)/shard_map/ppermute | solution.py:298
  67.0 5.6 %collective-permute-start.2 = (f32[1]{0:T(128)}, f32[1]{0:T(128)}, u32[]{:S(2)}, u32[]{:S(2)}) collective-permute-start(f32[1]{0:T(128)} %add.13), channel_id=1, source_target_pairs={{0,4},{1,5},{2,6},{3,7},{4,8},{5,9},{6,10},{7,11},{8,12},{9,13},{1... | collective-permute-start | bytes 20 | tf_op jit(solution)/shard_map/ppermute | solution.py:298
  73.2 7.6 %collective-permute-start.3 = (f32[1]{0:T(128)}, f32[1]{0:T(128)}, u32[]{:S(2)}, u32[]{:S(2)}) collective-permute-start(f32[1]{0:T(128)} %add.14), channel_id=1, source_target_pairs={{0,8},{1,9},{2,10},{3,11},{4,12},{5,13},{6,14},{7,15},{8,0},{9,1},... | collective-permute-start | bytes 20 | tf_op jit(solution)/shard_map/ppermute | solution.py:298

commit v6 on v5

--- a/solution.py
+++ b/solution.py
@@ -144,11 +144,11 @@
 
     edge_low, edge_high = blocks // 4, 3 * blocks // 4
 
-    def first_key(i):
-        return edge_low if i >= edge_high else 0
-
-    def scores(i, bound):
-        low, high = first_key(i), i + 1
+    def first_key(i, edge):
+        return edge if i > edge else 0
+
+    def scores(i, edge, bound):
+        low, high = first_key(i, edge), i + 1
         s = dot(span_of(1, low, high), span_of(0, i, i + 1), NT) * logit_scale
         g = dot(span_of(2, low, high), span_of(3, i, i + 1), NT)
         pgrad[i, low * BLK : high * BLK, :] = g
@@ -158,7 +158,7 @@
         for j in range(low, high):
             part = s[(j - low) * BLK : (j - low + 1) * BLK]
             row = lax.broadcasted_iota(jnp.int32, (BLK, BLK), 0)
-            if i >= edge_low and j < edge_high:
+            if i == edge or j == edge:
                 part = jnp.where(row >= lowest - j * BLK, part, HIDE)
             if j == i:
                 part = jnp.where(
@@ -169,9 +169,9 @@
             top = part if top is None else jnp.maximum(top, part)
         return jnp.max(top, axis=0, keepdims=True)
 
-    def settle(i, top):
+    def settle(i, edge, top):
         total = delta = jnp.zeros((8, BLK), jnp.float32)
-        for j in range(first_key(i), i + 1):
+        for j in range(first_key(i, edge), i + 1):
             span = slice(j * BLK, (j + 1) * BLK)
             e = jnp.exp2(logit[i, span, :] - top)
             total = total + jnp.sum(folded(e), axis=0)
@@ -180,8 +180,8 @@
         delta = jnp.sum(delta, axis=0, keepdims=True) / total
         return top + jnp.log2(total), delta
 
-    def gradients(i, norm, delta, gt):
-        low, high = first_key(i), i + 1
+    def gradients(i, edge, norm, delta, gt):
+        low, high = first_key(i, edge), i + 1
         weights, grads = [], []
         for j in range(low, high):
             span = slice(j * BLK, (j + 1) * BLK)
@@ -208,30 +208,45 @@
         put(1, i, dq)
         return gt
 
+    def leave(first, last):
+        for j in range(first, last):
+            span = slice(j * BLK, (j + 1) * BLK)
+            put(2, j, dk_acc[span, :] * scale)
+            put(3, j, dv_acc[span, :])
+            if (j + 1) % group == 0:
+                store(j + 1 - group, j + 1, 1).start()
+
     loads[0].wait()
     turn(0, group)
-    tops = {0: scores(0, shards * rows)}
-    gt = jnp.zeros((8, BLK), jnp.float32)
-    bound = None
-    for i in range(blocks):
-        if i + 1 == group:
-            loads[1].wait()
-            ids = held[:, 4 * rows :, :].astype(jnp.float32)
-            bound = shards * rows - (jnp.sum(ids) * (1.0 / PAD)).astype(jnp.int32)
-            turn(group, blocks)
-        if i + 1 < blocks:
-            tops[i + 1] = scores(i + 1, shards * rows if bound is None else bound)
-        norm, delta = settle(i, tops[i])
-        gt = gradients(i, norm, delta, gt)
-        if (i + 1) % group == 0:
-            store(i + 1 - group, i + 1, 0).start()
-    for i in range(blocks):
-        span = slice(i * BLK, (i + 1) * BLK)
-        put(2, i, dk_acc[span, :] * scale)
-        put(3, i, dv_acc[span, :])
-        if (i + 1) % group == 0:
-            store(i + 1 - group, i + 1, 1).start()
-    gt_ref[0] = jnp.sum(gt) / (temper * LOG2E)
+    everything = shards * rows
+    top = scores(0, edge_high, everything)
+    next_top = scores(1, edge_high, everything)
+    norm, delta = settle(0, edge_high, top)
+    first_gt = gradients(0, edge_high, norm, delta, jnp.zeros((8, BLK), jnp.float32))
+    loads[1].wait()
+    ids = held[:, 4 * rows :, :].astype(jnp.float32)
+    bound = everything - (jnp.sum(ids) * (1.0 / PAD)).astype(jnp.int32)
+    turn(group, blocks)
+    edge_at = jnp.clip(bound // BLK, edge_low, edge_high - 1)
+
+    def rest(edge):
+        gt, top, left = first_gt, next_top, 0
+        for i in range(1, blocks):
+            if i + 1 < blocks:
+                following = scores(i + 1, edge, bound)
+            norm, delta = settle(i, edge, top)
+            top = following
+            gt = gradients(i, edge, norm, delta, gt)
+            if (i + 1) % group == 0:
+                store(i + 1 - group, i + 1, 0).start()
+            if i == edge:
+                left = edge // group * group
+                leave(0, left)
+        leave(left, blocks)
+        gt_ref[0] = jnp.sum(gt) / (temper * LOG2E)
+
+    for edge in range(edge_low, edge_high):
+        pl.when(edge_at == edge)(functools.partial(rest, edge))
     for first in range(0, blocks, group):
         store(first, first + group, 0).wait()
         store(first, first + group, 1).wait()

time: 91.6 us -> 89.7 us (0.979)
  Pallas kernels: 20.6 us -> 17.4 us
  starting transfers between devices: 13.8 us -> 14.8 us
    pallas_call x1, Pallas kernels: 13.4 us -> 10.1 us  [body(): pl.pallas_call(attend_body, out_shape=(jax.ShapeDtypeStruct((shards, 4 *...]
    ppermute x4, starting transfers between devices: 10.1 us -> 11.1 us  [body(): lax.ppermute(gt, 'exp', [(n, (n + step) % exp_size) for n in range(exp_si...]
where the time goes in v6:
time: 89.7 us; the launch traced here: 88.5 us
  blocking collectives  36.5 us (41%)
  Pallas kernels  17.4 us (19%)
  waiting for transfers between devices  15.1 us (17%)
  starting transfers between devices  14.8 us (16%)
  between operations  4.71 us (5%)
    all_to_all x1, blocking collectives, body(): recv = lax.all_to_all(send, 'ctx', split_axis=0, concat_axis=0, tiled=True)  36.5 us
    ppermute x4, starting transfers between devices, body(): lax.ppermute(gt, 'exp', [(n, (n + step) % exp_size) for n in range(exp_si...  11.1 us
    pallas_call x1, Pallas kernels, body(): pl.pallas_call(attend_body, out_shape=(jax.ShapeDtypeStruct((shards, 4 *...  10.1 us
    ppermute x4, waiting for transfers between devices, body(): lax.ppermute(gt, 'exp', [(n, (n + step) % exp_size) for n in range(exp_si...  9.17 us
    all_to_all x1, waiting for transfers between devices, body(): lax.all_to_all(results, 'ctx', split_axis=0, concat_axis=0, tiled=True)  5.92 us
    pallas_call x1, Pallas kernels, body(): pl.pallas_call(pack_body, out_shape=jax.ShapeDtypeStruct((heads, 4 * rows...  4.01 us
    all_to_all x1, starting transfers between devices, body(): lax.all_to_all(results, 'ctx', split_axis=0, concat_axis=0, tiled=True)  3.73 us
    pallas_call x1, Pallas kernels, body(): pl.pallas_call(unpack_body, out_shape=[jax.ShapeDtypeStruct((rows, heads,...  3.2 us
  transfers between devices with their start and end apart: 5, of which 5 were waited for; matrix products, arithmetic and copies ran while one was open for 0% of the time, Pallas kernels for 0%

profile of v6, /device:TPU:192, one launch (start us, length us, event | category | flops | bytes accessed | tf_op | source)
XLA Modules:
  0.0 88.5 jit_solution(9615006354695638528)
XLA Ops:
  0.6 4.0 %shard_map.101 = bf16[16,528,128]{2,1,0:T(8,128)(2,1)} custom-call(bf16[128,16,128]{2,1,0:T(8,128)(2,1)} %bitcast.8, bf16[128,16,128]{2,1,0:T(8,128)(2,1)} %bitcast.9, bf16[128,16,128]{2,1,0:T(8,128)(2,1)} %bitcast.10, bf16[128,16,128]{2,1,0:T(8,128)(2,1)} %bitcast.11, s32[1,128]{1,0:T(1,128)} %hist_ref.1), custom_call_target="tpu_custom_call" | custom-call | tf_op jit(solution)/shard_map/pallas_call | solution.py:273
  4.6 36.5 %all_to_all.10.in_hbm = bf16[16,528,128]{2,1,0:T(8,128)(2,1)} all-to-all(bf16[16,528,128]{2,1,0:T(8,128)(2,1)} %shard_map.101), channel_id=1, replica_groups=mesh['ctx'=16,'exp'=16] {'ctx'}, dimensions={0} | all-to-all | bytes 4325376 | tf_op jit(solution)/shard_map/all_to_all | solution.py:287
  41.1 10.1 %shard_map.102 = (bf16[16,512,128]{2,1,0:T(8,128)(2,1)}, f32[1]{0:T(128)}) custom-call(f32[16]{0:T(128)} %temper_ref.1, bf16[16,528,128]{2,1,0:T(8,128)(2,1)} %all_to_all.10.in_hbm), custom_call_target="tpu_custom_call" | custom-call | tf_op jit(solution)/shard_map/pallas_call | solution.py:288
  51.3 3.7 %all-to-all-start.1 = ((bf16[16,512,128]{2,1,0:T(8,128)(2,1)}), bf16[16,512,128]{2,1,0:T(8,128)(2,1)S(1)}, u32[]{:S(2)}, u32[]{:S(2)}) async-start(bf16[16,512,128]{2,1,0:T(8,128)(2,1)} %get-tuple-element.11), calls=%async_computation.1 | async-start | bytes 4194304 | tf_op jit(solution)/shard_map/all_to_all | solution.py:309
  55.0 0.0 collective-permute-start
  55.1 3.2 %collective-permute-done = f32[1]{0:T(128)} collective-permute-done((f32[1]{0:T(128)}, f32[1]{0:T(128)}, u32[]{:S(2)}, u32[]{:S(2)}) %collective-permute-start) | collective-permute-done | bytes 36 | tf_op jit(solution)/shard_map/ppermute | solution.py:313
  59.5 2.9 %collective-permute-start.1 = (f32[1]{0:T(128)}, f32[1]{0:T(128)}, u32[]{:S(2)}, u32[]{:S(2)}) collective-permute-start(f32[1]{0:T(128)} %add.12), channel_id=1, source_target_pairs={{0,2},{1,3},{2,4},{3,5},{4,6},{5,7},{6,8},{7,9},{8,10},{9,11},{10,... | collective-permute-start | bytes 20 | tf_op jit(solution)/shard_map/ppermute | solution.py:313
  62.4 0.8 collective-permute-done.1
  63.7 3.6 %collective-permute-start.2 = (f32[1]{0:T(128)}, f32[1]{0:T(128)}, u32[]{:S(2)}, u32[]{:S(2)}) collective-permute-start(f32[1]{0:T(128)} %add.13), channel_id=1, source_target_pairs={{0,4},{1,5},{2,6},{3,7},{4,8},{5,9},{6,10},{7,11},{8,12},{9,13},{1... | collective-permute-start | bytes 20 | tf_op jit(solution)/shard_map/ppermute | solution.py:313
  67.3 2.2 %collective-permute-done.2 = f32[1]{0:T(128)} collective-permute-done((f32[1]{0:T(128)}, f32[1]{0:T(128)}, u32[]{:S(2)}, u32[]{:S(2)}) %collective-permute-start.2) | collective-permute-done | bytes 36 | tf_op jit(solution)/shard_map/ppermute | solution.py:313
  70.0 4.6 %collective-permute-start.3 = (f32[1]{0:T(128)}, f32[1]{0:T(128)}, u32[]{:S(2)}, u32[]{:S(2)}) collective-permute-start(f32[1]{0:T(128)} %add.14), channel_id=1, source_target_pairs={{0,8},{1,9},{2,10},{3,11},{4,12},{5,13},{6,14},{7,15},{8,0},{9,1},... | collective-permute-start | bytes 20 | tf_op jit(solution)/shard_map/ppermute | solution.py:313
  74.7 3.0 %collective-permute-done.3 = f32[1]{0:T(128)} collective-permute-done((f32[1]{0:T(128)}, f32[1]{0:T(128)}, u32[]{:S(2)}, u32[]{:S(2)}) %collective-permute-start.3) | collective-permute-done | bytes 36 | tf_op jit(solution)/shard_map/ppermute | solution.py:313
  78.2 5.9 %all-to-all-done.1.in_hbm = bf16[16,512,128]{2,1,0:T(8,128)(2,1)S(1)} async-done(((bf16[16,512,128]{2,1,0:T(8,128)(2,1)}), bf16[16,512,128]{2,1,0:T(8,128)(2,1)S(1)}, u32[]{:S(2)}, u32[]{:S(2)}) %all-to-all-start.1) | async-done | bytes 2097184 | tf_op jit(solution)/shard_map/all_to_all | solution.py:309
  84.2 3.2 %shard_map.103 = (bf16[128,16,128]{2,1,0:T(8,128)(2,1)}, bf16[128,16,128]{2,1,0:T(8,128)(2,1)}, bf16[128,16,128]{2,1,0:T(8,128)(2,1)}, bf16[128,16,128]{2,1,0:T(8,128)(2,1)}) custom-call(bf16[16,512,128]{2,1,0:T(8,128)(2,1)S(1)} %all-to-all-done.1.in_hbm), custom_call_target="tpu_custom_call" | custom-call | tf_op jit(solution)/shard_map/pallas_call | solution.py:315
Async XLA Ops:
  51.3 32.9 %all-to-all-start.1 = ((bf16[16,512,128]{2,1,0:T(8,128)(2,1)}), bf16[16,512,128]{2,1,0:T(8,128)(2,1)S(1)}, u32[]{:S(2)}, u32[]{:S(2)}) async-start(bf16[16,512,128]{2,1,0:T(8,128)(2,1)} %get-tuple-element.11), calls=%async_computation.1 | async-start | bytes 4194304 | tf_op jit(solution)/shard_map/all_to_all | solution.py:309
  55.0 3.2 %collective-permute-start = (f32[1]{0:T(128)}, f32[1]{0:T(128)}, u32[]{:S(2)}, u32[]{:S(2)}) collective-permute-start(f32[1]{0:T(128)} %get-tuple-element.16), channel_id=1, source_target_pairs={{0,1},{1,2},{2,3},{3,4},{4,5},{5,6},{6,7},{7,8},{8,9},{9,10},{10,1... | collective-permute-start | bytes 20 | tf_op jit(solution)/shard_map/ppermute | solution.py:313
  59.5 3.7 %collective-permute-start.1 = (f32[1]{0:T(128)}, f32[1]{0:T(128)}, u32[]{:S(2)}, u32[]{:S(2)}) collective-permute-start(f32[1]{0:T(128)} %add.12), channel_id=1, source_target_pairs={{0,2},{1,3},{2,4},{3,5},{4,6},{5,7},{6,8},{7,9},{8,10},{9,11},{10,... | collective-permute-start | bytes 20 | tf_op jit(solution)/shard_map/ppermute | solution.py:313
  63.7 5.7 %collective-permute-start.2 = (f32[1]{0:T(128)}, f32[1]{0:T(128)}, u32[]{:S(2)}, u32[]{:S(2)}) collective-permute-start(f32[1]{0:T(128)} %add.13), channel_id=1, source_target_pairs={{0,4},{1,5},{2,6},{3,7},{4,8},{5,9},{6,10},{7,11},{8,12},{9,13},{1... | collective-permute-start | bytes 20 | tf_op jit(solution)/shard_map/ppermute | solution.py:313
  70.0 7.6 %collective-permute-start.3 = (f32[1]{0:T(128)}, f32[1]{0:T(128)}, u32[]{:S(2)}, u32[]{:S(2)}) collective-permute-start(f32[1]{0:T(128)} %add.14), channel_id=1, source_target_pairs={{0,8},{1,9},{2,10},{3,11},{4,12},{5,13},{6,14},{7,15},{8,0},{9,1},... | collective-permute-start | bytes 20 | tf_op jit(solution)/shard_map/ppermute | solution.py:313

commit v7 on v6

--- a/solution.py
+++ b/solution.py
@@ -14,7 +14,7 @@
 HIDE = -1e30
 BLK = 256
 PAD = 16
-PARTS = 2
+PARTS = 4
 MIB = 1024 * 1024
 
 
@@ -100,10 +100,7 @@
     blocks = shards // per
     group = blocks // 4
     loads = [
-        pltpu.make_async_copy(in_hbm.at[span], held.at[span], in_sem.at[n])
-        for n, span in enumerate(
-            (pl.ds(0, group * per), pl.ds(group * per, shards - group * per))
-        )
+        pltpu.make_async_copy(in_hbm.at[n], held.at[n], in_sem.at[n]) for n in range(shards)
     ]
     for load in loads:
         load.start()
@@ -129,11 +126,18 @@
             jnp.bfloat16
         ).reshape(per, rows, hd)
 
-    def store(first, last, kind):
-        span, part = pl.ds(first * per, (last - first) * per), pl.ds(2 * kind * rows, 2 * rows)
-        return pltpu.make_async_copy(
-            done.at[span, part, :], out_hbm.at[span, part, :], out_sem.at[kind, first // group]
-        )
+    def stores(block, kind):
+        part = pl.ds(2 * kind * rows, 2 * rows)
+        return [
+            pltpu.make_async_copy(
+                done.at[n, part, :], out_hbm.at[n, part, :], out_sem.at[kind, n]
+            )
+            for n in range(block * per, (block + 1) * per)
+        ]
+
+    def send(block, kind):
+        for copy in stores(block, kind):
+            copy.start()
 
     def turn(low, high):
         span = slice(low * BLK, high * BLK)
@@ -213,17 +217,19 @@
             span = slice(j * BLK, (j + 1) * BLK)
             put(2, j, dk_acc[span, :] * scale)
             put(3, j, dv_acc[span, :])
-            if (j + 1) % group == 0:
-                store(j + 1 - group, j + 1, 1).start()
-
-    loads[0].wait()
+            send(j, 1)
+
+    for load in loads[: group * per]:
+        load.wait()
     turn(0, group)
     everything = shards * rows
     top = scores(0, edge_high, everything)
     next_top = scores(1, edge_high, everything)
     norm, delta = settle(0, edge_high, top)
     first_gt = gradients(0, edge_high, norm, delta, jnp.zeros((8, BLK), jnp.float32))
-    loads[1].wait()
+    send(0, 0)
+    for load in loads[group * per :]:
+        load.wait()
     ids = held[:, 4 * rows :, :].astype(jnp.float32)
     bound = everything - (jnp.sum(ids) * (1.0 / PAD)).astype(jnp.int32)
     turn(group, blocks)
@@ -237,19 +243,19 @@
             norm, delta = settle(i, edge, top)
             top = following
             gt = gradients(i, edge, norm, delta, gt)
-            if (i + 1) % group == 0:
-                store(i + 1 - group, i + 1, 0).start()
+            send(i, 0)
             if i == edge:
-                left = edge // group * group
+                left = edge
                 leave(0, left)
         leave(left, blocks)
         gt_ref[0] = jnp.sum(gt) / (temper * LOG2E)
 
     for edge in range(edge_low, edge_high):
         pl.when(edge_at == edge)(functools.partial(rest, edge))
-    for first in range(0, blocks, group):
-        store(first, first + group, 0).wait()
-        store(first, first + group, 1).wait()
+    for block in range(blocks):
+        for kind in range(2):
+            for copy in stores(block, kind):
+                copy.wait()
 
 
 def vmem_spec():
@@ -301,8 +307,8 @@
             pltpu.VMEM((hd, blocks * BLK), low),
             pltpu.VMEM((blocks * BLK, hd), f32),
             pltpu.VMEM((blocks * BLK, hd), f32),
-            pltpu.SemaphoreType.DMA((2,)),
-            pltpu.SemaphoreType.DMA((2, 4)),
+            pltpu.SemaphoreType.DMA((shards,)),
+            pltpu.SemaphoreType.DMA((2, shards)),
         ],
         compiler_params=grant(60),
     )(temper, recv)

time: 89.7 us -> 90 us (level)
  Pallas kernels: 17.4 us -> 18.5 us
    pallas_call x1, Pallas kernels: 10.1 us -> 11.1 us  [body(): pl.pallas_call(attend_body, out_shape=(jax.ShapeDtypeStruct((shards, 4 *...]
where the time goes in v7:
time: 90 us; the launch traced here: 88.7 us
  blocking collectives  36.5 us (41%)
  Pallas kernels  18.5 us (21%)
  starting transfers between devices  14.6 us (16%)
  waiting for transfers between devices  14.3 us (16%)
  between operations  4.71 us (5%)
    all_to_all x1, blocking collectives, body(): recv = lax.all_to_all(send, 'ctx', split_axis=0, concat_axis=0, tiled=True)  36.5 us
    pallas_call x1, Pallas kernels, body(): pl.pallas_call(attend_body, out_shape=(jax.ShapeDtypeStruct((shards, 4 *...  11.1 us
    ppermute x4, starting transfers between devices, body(): lax.ppermute(gt, 'exp', [(n, (n + step) % exp_size) for n in range(exp_si...  10.9 us
    ppermute x4, waiting for transfers between devices, body(): lax.ppermute(gt, 'exp', [(n, (n + step) % exp_size) for n in range(exp_si...  8.81 us
    all_to_all x1, waiting for transfers between devices, body(): lax.all_to_all(results, 'ctx', split_axis=0, concat_axis=0, tiled=True)  5.53 us
    pallas_call x1, Pallas kernels, body(): pl.pallas_call(pack_body, out_shape=jax.ShapeDtypeStruct((heads, 4 * rows...  4.06 us
    all_to_all x1, starting transfers between devices, body(): lax.all_to_all(results, 'ctx', split_axis=0, concat_axis=0, tiled=True)  3.73 us
    pallas_call x1, Pallas kernels, body(): pl.pallas_call(unpack_body, out_shape=[jax.ShapeDtypeStruct((rows, heads,...  3.36 us
  transfers between devices with their start and end apart: 5, of which 5 were waited for; matrix products, arithmetic and copies ran while one was open for 0% of the time, Pallas kernels for 0%

profile of v7, /device:TPU:192, one launch (start us, length us, event | category | flops | bytes accessed | tf_op | source)
XLA Modules:
  0.0 88.7 jit_solution(10215421154978884828)
XLA Ops:
  0.6 4.1 %shard_map.101 = bf16[16,528,128]{2,1,0:T(8,128)(2,1)} custom-call(bf16[128,16,128]{2,1,0:T(8,128)(2,1)} %bitcast.8, bf16[128,16,128]{2,1,0:T(8,128)(2,1)} %bitcast.9, bf16[128,16,128]{2,1,0:T(8,128)(2,1)} %bitcast.10, bf16[128,16,128]{2,1,0:T(8,128)(2,1)} %bitcast.11, s32[1,128]{1,0:T(1,128)} %hist_ref.1), custom_call_target="tpu_custom_call" | custom-call | tf_op jit(solution)/shard_map/pallas_call | solution.py:279
  4.7 36.5 %all_to_all.10.in_hbm = bf16[16,528,128]{2,1,0:T(8,128)(2,1)} all-to-all(bf16[16,528,128]{2,1,0:T(8,128)(2,1)} %shard_map.101), channel_id=1, replica_groups=mesh['ctx'=16,'exp'=16] {'ctx'}, dimensions={0} | all-to-all | bytes 4325376 | tf_op jit(solution)/shard_map/all_to_all | solution.py:293
  41.2 11.1 %shard_map.102 = (bf16[16,512,128]{2,1,0:T(8,128)(2,1)}, f32[1]{0:T(128)}) custom-call(f32[16]{0:T(128)} %temper_ref.1, bf16[16,528,128]{2,1,0:T(8,128)(2,1)} %all_to_all.10.in_hbm), custom_call_target="tpu_custom_call" | custom-call | tf_op jit(solution)/shard_map/pallas_call | solution.py:294
  52.3 3.7 %all-to-all-start.1 = ((bf16[16,512,128]{2,1,0:T(8,128)(2,1)}), bf16[16,512,128]{2,1,0:T(8,128)(2,1)S(1)}, u32[]{:S(2)}, u32[]{:S(2)}) async-start(bf16[16,512,128]{2,1,0:T(8,128)(2,1)} %get-tuple-element.11), calls=%async_computation.1 | async-start | bytes 4194304 | tf_op jit(solution)/shard_map/all_to_all | solution.py:315
  56.0 0.0 collective-permute-start
  56.1 3.2 %collective-permute-done = f32[1]{0:T(128)} collective-permute-done((f32[1]{0:T(128)}, f32[1]{0:T(128)}, u32[]{:S(2)}, u32[]{:S(2)}) %collective-permute-start) | collective-permute-done | bytes 36 | tf_op jit(solution)/shard_map/ppermute | solution.py:319
  60.5 2.8 %collective-permute-start.1 = (f32[1]{0:T(128)}, f32[1]{0:T(128)}, u32[]{:S(2)}, u32[]{:S(2)}) collective-permute-start(f32[1]{0:T(128)} %add.12), channel_id=1, source_target_pairs={{0,2},{1,3},{2,4},{3,5},{4,6},{5,7},{6,8},{7,9},{8,10},{9,11},{10,... | collective-permute-start | bytes 20 | tf_op jit(solution)/shard_map/ppermute | solution.py:319
  63.2 0.9 %collective-permute-done.1 = f32[1]{0:T(128)} collective-permute-done((f32[1]{0:T(128)}, f32[1]{0:T(128)}, u32[]{:S(2)}, u32[]{:S(2)}) %collective-permute-start.1) | collective-permute-done | bytes 36 | tf_op jit(solution)/shard_map/ppermute | solution.py:319
  64.7 3.4 %collective-permute-start.2 = (f32[1]{0:T(128)}, f32[1]{0:T(128)}, u32[]{:S(2)}, u32[]{:S(2)}) collective-permute-start(f32[1]{0:T(128)} %add.13), channel_id=1, source_target_pairs={{0,4},{1,5},{2,6},{3,7},{4,8},{5,9},{6,10},{7,11},{8,12},{9,13},{1... | collective-permute-start | bytes 20 | tf_op jit(solution)/shard_map/ppermute | solution.py:319
  68.2 1.7 %collective-permute-done.2 = f32[1]{0:T(128)} collective-permute-done((f32[1]{0:T(128)}, f32[1]{0:T(128)}, u32[]{:S(2)}, u32[]{:S(2)}) %collective-permute-start.2) | collective-permute-done | bytes 36 | tf_op jit(solution)/shard_map/ppermute | solution.py:319
  70.4 4.6 %collective-permute-start.3 = (f32[1]{0:T(128)}, f32[1]{0:T(128)}, u32[]{:S(2)}, u32[]{:S(2)}) collective-permute-start(f32[1]{0:T(128)} %add.14), channel_id=1, source_target_pairs={{0,8},{1,9},{2,10},{3,11},{4,12},{5,13},{6,14},{7,15},{8,0},{9,1},... | collective-permute-start | bytes 20 | tf_op jit(solution)/shard_map/ppermute | solution.py:319
  75.1 3.0 %collective-permute-done.3 = f32[1]{0:T(128)} collective-permute-done((f32[1]{0:T(128)}, f32[1]{0:T(128)}, u32[]{:S(2)}, u32[]{:S(2)}) %collective-permute-start.3) | collective-permute-done | bytes 36 | tf_op jit(solution)/shard_map/ppermute | solution.py:319
  78.6 5.5 %all-to-all-done.1.in_hbm = bf16[16,512,128]{2,1,0:T(8,128)(2,1)S(1)} async-done(((bf16[16,512,128]{2,1,0:T(8,128)(2,1)}), bf16[16,512,128]{2,1,0:T(8,128)(2,1)S(1)}, u32[]{:S(2)}, u32[]{:S(2)}) %all-to-all-start.1) | async-done | bytes 2097184 | tf_op jit(solution)/shard_map/all_to_all | solution.py:315
  84.2 3.4 %shard_map.103 = (bf16[128,16,128]{2,1,0:T(8,128)(2,1)}, bf16[128,16,128]{2,1,0:T(8,128)(2,1)}, bf16[128,16,128]{2,1,0:T(8,128)(2,1)}, bf16[128,16,128]{2,1,0:T(8,128)(2,1)}) custom-call(bf16[16,512,128]{2,1,0:T(8,128)(2,1)S(1)} %all-to-all-done.1.in_hbm), custom_call_target="tpu_custom_call" | custom-call | tf_op jit(solution)/shard_map/pallas_call | solution.py:321
Async XLA Ops:
  52.3 31.9 %all-to-all-start.1 = ((bf16[16,512,128]{2,1,0:T(8,128)(2,1)}), bf16[16,512,128]{2,1,0:T(8,128)(2,1)S(1)}, u32[]{:S(2)}, u32[]{:S(2)}) async-start(bf16[16,512,128]{2,1,0:T(8,128)(2,1)} %get-tuple-element.11), calls=%async_computation.1 | async-start | bytes 4194304 | tf_op jit(solution)/shard_map/all_to_all | solution.py:315
  56.0 3.2 %collective-permute-start = (f32[1]{0:T(128)}, f32[1]{0:T(128)}, u32[]{:S(2)}, u32[]{:S(2)}) collective-permute-start(f32[1]{0:T(128)} %get-tuple-element.16), channel_id=1, source_target_pairs={{0,1},{1,2},{2,3},{3,4},{4,5},{5,6},{6,7},{7,8},{8,9},{9,10},{10,1... | collective-permute-start | bytes 20 | tf_op jit(solution)/shard_map/ppermute | solution.py:319
  60.5 3.7 %collective-permute-start.1 = (f32[1]{0:T(128)}, f32[1]{0:T(128)}, u32[]{:S(2)}, u32[]{:S(2)}) collective-permute-start(f32[1]{0:T(128)} %add.12), channel_id=1, source_target_pairs={{0,2},{1,3},{2,4},{3,5},{4,6},{5,7},{6,8},{7,9},{8,10},{9,11},{10,... | collective-permute-start | bytes 20 | tf_op jit(solution)/shard_map/ppermute | solution.py:319
  64.7 5.1 %collective-permute-start.2 = (f32[1]{0:T(128)}, f32[1]{0:T(128)}, u32[]{:S(2)}, u32[]{:S(2)}) collective-permute-start(f32[1]{0:T(128)} %add.13), channel_id=1, source_target_pairs={{0,4},{1,5},{2,6},{3,7},{4,8},{5,9},{6,10},{7,11},{8,12},{9,13},{1... | collective-permute-start | bytes 20 | tf_op jit(solution)/shard_map/ppermute | solution.py:319
  70.4 7.6 %collective-permute-start.3 = (f32[1]{0:T(128)}, f32[1]{0:T(128)}, u32[]{:S(2)}, u32[]{:S(2)}) collective-permute-start(f32[1]{0:T(128)} %add.14), channel_id=1, source_target_pairs={{0,8},{1,9},{2,10},{3,11},{4,12},{5,13},{6,14},{7,15},{8,0},{9,1},... | collective-permute-start | bytes 20 | tf_op jit(solution)/shard_map/ppermute | solution.py:319

commit v8 on v6

--- a/solution.py
+++ b/solution.py
@@ -53,19 +53,11 @@
         store.wait()
 
 
-def unpack_body(in_hbm, a_hbm, b_hbm, c_hbm, d_hbm, held, wide, packed, in_sem, out_sem):
+def unpack_body(held, a_hbm, b_hbm, c_hbm, d_hbm, wide, packed, out_sem):
     _, rows, heads, hd = packed.shape
     size = rows // PARTS
-    loads, stores = [], []
+    stores = []
     for stage in range(4 * PARTS):
-        span = pl.ds(stage * size, size)
-        load = pltpu.make_async_copy(
-            in_hbm.at[:, span, :], held.at[:, span, :], in_sem.at[stage]
-        )
-        load.start()
-        loads.append(load)
-    for stage, load in enumerate(loads):
-        load.wait()
         place, span, slot = stage // PARTS, pl.ds(stage % PARTS * size, size), stage % 4
         for head in range(heads):
             part = held[head, stage * size : (stage + 1) * size, :]
@@ -81,17 +73,15 @@
 
 def attend_body(
     temper_ref,
-    in_hbm,
+    held,
     out_hbm,
     gt_ref,
-    held,
     done,
     logit,
     pgrad,
     v_t,
     dk_acc,
     dv_acc,
-    in_sem,
     out_sem,
 ):
     shards, hd = held.shape[0], held.shape[2]
@@ -99,14 +89,6 @@
     per = BLK // rows
     blocks = shards // per
     group = blocks // 4
-    loads = [
-        pltpu.make_async_copy(in_hbm.at[span], held.at[span], in_sem.at[n])
-        for n, span in enumerate(
-            (pl.ds(0, group * per), pl.ds(group * per, shards - group * per))
-        )
-    ]
-    for load in loads:
-        load.start()
     temper = temper_ref[lax.axis_index("ctx")]
     scale = temper * hd ** (-0.5)
     logit_scale = scale * LOG2E
@@ -216,14 +198,12 @@
             if (j + 1) % group == 0:
                 store(j + 1 - group, j + 1, 1).start()
 
-    loads[0].wait()
     turn(0, group)
     everything = shards * rows
     top = scores(0, edge_high, everything)
     next_top = scores(1, edge_high, everything)
     norm, delta = settle(0, edge_high, top)
     first_gt = gradients(0, edge_high, norm, delta, jnp.zeros((8, BLK), jnp.float32))
-    loads[1].wait()
     ids = held[:, 4 * rows :, :].astype(jnp.float32)
     bound = everything - (jnp.sum(ids) * (1.0 / PAD)).astype(jnp.int32)
     turn(group, blocks)
@@ -291,21 +271,19 @@
             jax.ShapeDtypeStruct((shards, 4 * rows, hd), low),
             jax.ShapeDtypeStruct((1,), f32),
         ),
-        in_specs=[pl.BlockSpec(memory_space=pltpu.SMEM), any_spec()],
+        in_specs=[pl.BlockSpec(memory_space=pltpu.SMEM), vmem_spec()],
         out_specs=(any_spec(), pl.BlockSpec(memory_space=pltpu.SMEM)),
         scratch_shapes=[
-            pltpu.VMEM((shards, 4 * rows + PAD, hd), low),
             pltpu.VMEM((shards, 4 * rows, hd), low),
             pltpu.VMEM((blocks, blocks * BLK, BLK), f32),
             pltpu.VMEM((blocks, blocks * BLK, BLK), f32),
             pltpu.VMEM((hd, blocks * BLK), low),
             pltpu.VMEM((blocks * BLK, hd), f32),
             pltpu.VMEM((blocks * BLK, hd), f32),
-            pltpu.SemaphoreType.DMA((2,)),
             pltpu.SemaphoreType.DMA((2, 4)),
         ],
-        compiler_params=grant(60),
-    )(temper, recv)
+        compiler_params=grant(50),
+    )(temper, pltpu.with_memory_space_constraint(recv, pltpu.VMEM))
     back = lax.all_to_all(results, "ctx", split_axis=0, concat_axis=0, tiled=True)
     exp_size = lax.axis_size("exp")
     step = 1
@@ -315,17 +293,15 @@
     outs = pl.pallas_call(
         unpack_body,
         out_shape=[jax.ShapeDtypeStruct((rows, heads, hd), low)] * 4,
-        in_specs=[any_spec()],
+        in_specs=[vmem_spec()],
         out_specs=[any_spec()] * 4,
         scratch_shapes=[
-            pltpu.VMEM((heads, 4 * rows, hd), low),
             pltpu.VMEM((4, rows // PARTS * heads, hd), f32),
             pltpu.VMEM((4, rows, heads, hd), low),
             pltpu.SemaphoreType.DMA((4 * PARTS,)),
-            pltpu.SemaphoreType.DMA((4 * PARTS,)),
         ],
         compiler_params=grant(16),
-    )(back)
+    )(pltpu.with_memory_space_constraint(back, pltpu.VMEM))
     attn_out, grad_q, grad_k, grad_v = [part[None] for part in outs]
     return attn_out, grad_q, grad_k, grad_v, gt
 

time: 89.7 us -> 87.7 us (0.978)
  no operation moved by 1% of the time
where the time goes in v8:
time: 87.7 us; the launch traced here: 86.5 us
  blocking collectives  36.4 us (42%)
  Pallas kernels  16.8 us (19%)
  waiting for transfers between devices  14.3 us (16%)
  starting transfers between devices  14 us (16%)
  between operations  5.02 us (6%)
    all_to_all x1, blocking collectives, body(): recv = lax.all_to_all(send, 'ctx', split_axis=0, concat_axis=0, tiled=True)  36.4 us
    ppermute x4, starting transfers between devices, body(): lax.ppermute(gt, 'exp', [(n, (n + step) % exp_size) for n in range(exp_si...  10.2 us
    pallas_call x1, Pallas kernels, body(): pl.pallas_call(attend_body, out_shape=(jax.ShapeDtypeStruct((shards, 4 *...  9.79 us
    ppermute x4, waiting for transfers between devices, body(): lax.ppermute(gt, 'exp', [(n, (n + step) % exp_size) for n in range(exp_si...  8.8 us
    all_to_all x1, waiting for transfers between devices, body(): lax.all_to_all(results, 'ctx', split_axis=0, concat_axis=0, tiled=True)  5.54 us
    pallas_call x1, Pallas kernels, body(): pl.pallas_call(pack_body, out_shape=jax.ShapeDtypeStruct((heads, 4 * rows...  4.01 us
    all_to_all x1, starting transfers between devices, body(): lax.all_to_all(results, 'ctx', split_axis=0, concat_axis=0, tiled=True)  3.73 us
    pallas_call x1, Pallas kernels, body(): pl.pallas_call(unpack_body, out_shape=[jax.ShapeDtypeStruct((rows, heads,...  2.96 us
  transfers between devices with their start and end apart: 5, of which 5 were waited for; matrix products, arithmetic and copies ran while one was open for 0% of the time, Pallas kernels for 0%

profile of v8, /device:TPU:192, one launch (start us, length us, event | category | flops | bytes accessed | tf_op | source)
XLA Modules:
  0.0 86.5 jit_solution(6511608786530574303)
XLA Ops:
  0.6 4.0 %shard_map.101 = bf16[16,528,128]{2,1,0:T(8,128)(2,1)} custom-call(bf16[128,16,128]{2,1,0:T(8,128)(2,1)} %bitcast.8, bf16[128,16,128]{2,1,0:T(8,128)(2,1)} %bitcast.9, bf16[128,16,128]{2,1,0:T(8,128)(2,1)} %bitcast.10, bf16[128,16,128]{2,1,0:T(8,128)(2,1)} %bitcast.11, s32[1,128]{1,0:T(1,128)} %hist_ref.1), custom_call_target="tpu_custom_call" | custom-call | tf_op jit(solution)/shard_map/pallas_call | solution.py:253
  4.7 0.0 copy-start
  4.7 36.4 %all_to_all.10.held = bf16[16,528,128]{2,1,0:T(8,128)(2,1)S(1)} all-to-all(bf16[16,528,128]{2,1,0:T(8,128)(2,1)} %shard_map.101), channel_id=1, replica_groups=mesh['ctx'=16,'exp'=16] {'ctx'}, dimensions={0} | all-to-all | bytes 4325376 | tf_op jit(solution)/shard_map/all_to_all | solution.py:267
  41.1 0.0 copy-done
  41.1 9.8 %shard_map.102 = (bf16[16,512,128]{2,1,0:T(8,128)(2,1)}, f32[1]{0:T(128)}) custom-call(f32[16]{0:T(128)S(1)} %copy-done, bf16[16,528,128]{2,1,0:T(8,128)(2,1)S(1)} %all_to_all.10.held), custom_call_target="tpu_custom_call" | custom-call | tf_op jit(solution)/shard_map/pallas_call | solution.py:268
  50.9 3.7 %all-to-all-start.1 = ((bf16[16,512,128]{2,1,0:T(8,128)(2,1)}), bf16[16,512,128]{2,1,0:T(8,128)(2,1)S(1)}, u32[]{:S(2)}, u32[]{:S(2)}) async-start(bf16[16,512,128]{2,1,0:T(8,128)(2,1)} %get-tuple-element.11), calls=%async_computation.1 | async-start | bytes 4194304 | tf_op jit(solution)/shard_map/all_to_all | solution.py:287
  54.6 0.0 collective-permute-start
  54.6 3.0 %collective-permute-done = f32[1]{0:T(128)} collective-permute-done((f32[1]{0:T(128)}, f32[1]{0:T(128)}, u32[]{:S(2)}, u32[]{:S(2)}) %collective-permute-start) | collective-permute-done | bytes 36 | tf_op jit(solution)/shard_map/ppermute | solution.py:291
  58.9 2.4 %collective-permute-start.1 = (f32[1]{0:T(128)}, f32[1]{0:T(128)}, u32[]{:S(2)}, u32[]{:S(2)}) collective-permute-start(f32[1]{0:T(128)} %add.12), channel_id=1, source_target_pairs={{0,2},{1,3},{2,4},{3,5},{4,6},{5,7},{6,8},{7,9},{8,10},{9,11},{10,... | collective-permute-start | bytes 20 | tf_op jit(solution)/shard_map/ppermute | solution.py:291
  61.3 1.2 %collective-permute-done.1 = f32[1]{0:T(128)} collective-permute-done((f32[1]{0:T(128)}, f32[1]{0:T(128)}, u32[]{:S(2)}, u32[]{:S(2)}) %collective-permute-start.1) | collective-permute-done | bytes 36 | tf_op jit(solution)/shard_map/ppermute | solution.py:291
  63.1 3.0 %collective-permute-start.2 = (f32[1]{0:T(128)}, f32[1]{0:T(128)}, u32[]{:S(2)}, u32[]{:S(2)}) collective-permute-start(f32[1]{0:T(128)} %add.13), channel_id=1, source_target_pairs={{0,4},{1,5},{2,6},{3,7},{4,8},{5,9},{6,10},{7,11},{8,12},{9,13},{1... | collective-permute-start | bytes 20 | tf_op jit(solution)/shard_map/ppermute | solution.py:291
  66.2 1.9 %collective-permute-done.2 = f32[1]{0:T(128)} collective-permute-done((f32[1]{0:T(128)}, f32[1]{0:T(128)}, u32[]{:S(2)}, u32[]{:S(2)}) %collective-permute-start.2) | collective-permute-done | bytes 36 | tf_op jit(solution)/shard_map/ppermute | solution.py:291
  68.7 4.8 %collective-permute-start.3 = (f32[1]{0:T(128)}, f32[1]{0:T(128)}, u32[]{:S(2)}, u32[]{:S(2)}) collective-permute-start(f32[1]{0:T(128)} %add.14), channel_id=1, source_target_pairs={{0,8},{1,9},{2,10},{3,11},{4,12},{5,13},{6,14},{7,15},{8,0},{9,1},... | collective-permute-start | bytes 20 | tf_op jit(solution)/shard_map/ppermute | solution.py:291
  73.5 2.7 %collective-permute-done.3 = f32[1]{0:T(128)} collective-permute-done((f32[1]{0:T(128)}, f32[1]{0:T(128)}, u32[]{:S(2)}, u32[]{:S(2)}) %collective-permute-start.3) | collective-permute-done | bytes 36 | tf_op jit(solution)/shard_map/ppermute | solution.py:291
  76.8 5.5 %all-to-all-done.1.held = bf16[16,512,128]{2,1,0:T(8,128)(2,1)S(1)} async-done(((bf16[16,512,128]{2,1,0:T(8,128)(2,1)}), bf16[16,512,128]{2,1,0:T(8,128)(2,1)S(1)}, u32[]{:S(2)}, u32[]{:S(2)}) %all-to-all-start.1) | async-done | bytes 2097184 | tf_op jit(solution)/shard_map/all_to_all | solution.py:287
  82.4 3.0 %shard_map.103 = (bf16[128,16,128]{2,1,0:T(8,128)(2,1)}, bf16[128,16,128]{2,1,0:T(8,128)(2,1)}, bf16[128,16,128]{2,1,0:T(8,128)(2,1)}, bf16[128,16,128]{2,1,0:T(8,128)(2,1)}) custom-call(bf16[16,512,128]{2,1,0:T(8,128)(2,1)S(1)} %all-to-all-done.1.held), custom_call_target="tpu_custom_call" | custom-call | tf_op jit(solution)/shard_map/pallas_call | solution.py:293
Async XLA Ops:
  4.7 36.4 %copy-start = (f32[16]{0:T(128)S(1)}, f32[16]{0:T(128)}, u32[]{:S(2)}) copy-start(f32[16]{0:T(128)} %temper_ref.1) | copy-start | bytes 196
  50.9 31.5 %all-to-all-start.1 = ((bf16[16,512,128]{2,1,0:T(8,128)(2,1)}), bf16[16,512,128]{2,1,0:T(8,128)(2,1)S(1)}, u32[]{:S(2)}, u32[]{:S(2)}) async-start(bf16[16,512,128]{2,1,0:T(8,128)(2,1)} %get-tuple-element.11), calls=%async_computation.1 | async-start | bytes 4194304 | tf_op jit(solution)/shard_map/all_to_all | solution.py:287
  54.6 3.1 %collective-permute-start = (f32[1]{0:T(128)}, f32[1]{0:T(128)}, u32[]{:S(2)}, u32[]{:S(2)}) collective-permute-start(f32[1]{0:T(128)} %get-tuple-element.16), channel_id=1, source_target_pairs={{0,1},{1,2},{2,3},{3,4},{4,5},{5,6},{6,7},{7,8},{8,9},{9,10},{10,1... | collective-permute-start | bytes 20 | tf_op jit(solution)/shard_map/ppermute | solution.py:291
  58.9 3.6 %collective-permute-start.1 = (f32[1]{0:T(128)}, f32[1]{0:T(128)}, u32[]{:S(2)}, u32[]{:S(2)}) collective-permute-start(f32[1]{0:T(128)} %add.12), channel_id=1, source_target_pairs={{0,2},{1,3},{2,4},{3,5},{4,6},{5,7},{6,8},{7,9},{8,10},{9,11},{10,... | collective-permute-start | bytes 20 | tf_op jit(solution)/shard_map/ppermute | solution.py:291
  63.1 4.9 %collective-permute-start.2 = (f32[1]{0:T(128)}, f32[1]{0:T(128)}, u32[]{:S(2)}, u32[]{:S(2)}) collective-permute-start(f32[1]{0:T(128)} %add.13), channel_id=1, source_target_pairs={{0,4},{1,5},{2,6},{3,7},{4,8},{5,9},{6,10},{7,11},{8,12},{9,13},{1... | collective-permute-start | bytes 20 | tf_op jit(solution)/shard_map/ppermute | solution.py:291
  68.7 7.5 %collective-permute-start.3 = (f32[1]{0:T(128)}, f32[1]{0:T(128)}, u32[]{:S(2)}, u32[]{:S(2)}) collective-permute-start(f32[1]{0:T(128)} %add.14), channel_id=1, source_target_pairs={{0,8},{1,9},{2,10},{3,11},{4,12},{5,13},{6,14},{7,15},{8,0},{9,1},... | collective-permute-start | bytes 20 | tf_op jit(solution)/shard_map/ppermute | solution.py:291

commit v9 on v8

--- a/solution.py
+++ b/solution.py
@@ -114,7 +114,7 @@
     def store(first, last, kind):
         span, part = pl.ds(first * per, (last - first) * per), pl.ds(2 * kind * rows, 2 * rows)
         return pltpu.make_async_copy(
-            done.at[span, part, :], out_hbm.at[span, part, :], out_sem.at[kind, first // group]
+            done.at[span, part, :], out_hbm.at[span, part, :], out_sem.at[kind, first]
         )
 
     def turn(low, high):
@@ -195,17 +195,17 @@
             span = slice(j * BLK, (j + 1) * BLK)
             put(2, j, dk_acc[span, :] * scale)
             put(3, j, dv_acc[span, :])
-            if (j + 1) % group == 0:
-                store(j + 1 - group, j + 1, 1).start()
-
+            store(j, j + 1, 1).start()
+
+    everything = shards * rows
+    ids = held[:, 4 * rows :, :].astype(jnp.float32)
+    bound = everything - (jnp.sum(ids) * (1.0 / PAD)).astype(jnp.int32)
     turn(0, group)
-    everything = shards * rows
     top = scores(0, edge_high, everything)
     next_top = scores(1, edge_high, everything)
     norm, delta = settle(0, edge_high, top)
     first_gt = gradients(0, edge_high, norm, delta, jnp.zeros((8, BLK), jnp.float32))
-    ids = held[:, 4 * rows :, :].astype(jnp.float32)
-    bound = everything - (jnp.sum(ids) * (1.0 / PAD)).astype(jnp.int32)
+    store(0, 1, 0).start()
     turn(group, blocks)
     edge_at = jnp.clip(bound // BLK, edge_low, edge_high - 1)
 
@@ -217,19 +217,18 @@
             norm, delta = settle(i, edge, top)
             top = following
             gt = gradients(i, edge, norm, delta, gt)
-            if (i + 1) % group == 0:
-                store(i + 1 - group, i + 1, 0).start()
+            store(i, i + 1, 0).start()
             if i == edge:
-                left = edge // group * group
+                left = edge
                 leave(0, left)
         leave(left, blocks)
         gt_ref[0] = jnp.sum(gt) / (temper * LOG2E)
 
     for edge in range(edge_low, edge_high):
         pl.when(edge_at == edge)(functools.partial(rest, edge))
-    for first in range(0, blocks, group):
-        store(first, first + group, 0).wait()
-        store(first, first + group, 1).wait()
+    for block in range(blocks):
+        store(block, block + 1, 0).wait()
+        store(block, block + 1, 1).wait()
 
 
 def vmem_spec():
@@ -280,7 +279,7 @@
             pltpu.VMEM((hd, blocks * BLK), low),
             pltpu.VMEM((blocks * BLK, hd), f32),
             pltpu.VMEM((blocks * BLK, hd), f32),
-            pltpu.SemaphoreType.DMA((2, 4)),
+            pltpu.SemaphoreType.DMA((2, blocks)),
         ],
         compiler_params=grant(50),
     )(temper, pltpu.with_memory_space_constraint(recv, pltpu.VMEM))

time: 87.7 us -> 87.8 us (level)
  waiting for transfers between devices: 14.3 us -> 15.6 us
  starting transfers between devices: 14 us -> 13.1 us
    ppermute x4, waiting for transfers between devices: 8.8 us -> 10.5 us  [body(): lax.ppermute(gt, 'exp', [(n, (n + step) % exp_size) for n in range(exp_si...]
where the time goes in v9:
time: 87.8 us; the launch traced here: 86.4 us
  blocking collectives  36.4 us (41%)
  Pallas kernels  16.4 us (19%)
  waiting for transfers between devices  15.6 us (18%)
  starting transfers between devices  13.1 us (15%)
  between operations  5.02 us (6%)
    all_to_all x1, blocking collectives, body(): recv = lax.all_to_all(send, 'ctx', split_axis=0, concat_axis=0, tiled=True)  36.4 us
    ppermute x4, waiting for transfers between devices, body(): lax.ppermute(gt, 'exp', [(n, (n + step) % exp_size) for n in range(exp_si...  10.5 us
    ppermute x4, starting transfers between devices, body(): lax.ppermute(gt, 'exp', [(n, (n + step) % exp_size) for n in range(exp_si...  9.4 us
    pallas_call x1, Pallas kernels, body(): pl.pallas_call(attend_body, out_shape=(jax.ShapeDtypeStruct((shards, 4 *...  9.38 us
    all_to_all x1, waiting for transfers between devices, body(): lax.all_to_all(results, 'ctx', split_axis=0, concat_axis=0, tiled=True)  5.02 us
    pallas_call x1, Pallas kernels, body(): pl.pallas_call(pack_body, out_shape=jax.ShapeDtypeStruct((heads, 4 * rows...  4.01 us
    all_to_all x1, starting transfers between devices, body(): lax.all_to_all(results, 'ctx', split_axis=0, concat_axis=0, tiled=True)  3.73 us
    pallas_call x1, Pallas kernels, body(): pl.pallas_call(unpack_body, out_shape=[jax.ShapeDtypeStruct((rows, heads,...  2.96 us
  transfers between devices with their start and end apart: 5, of which 5 were waited for; matrix products, arithmetic and copies ran while one was open for 0% of the time, Pallas kernels for 0%

profile of v9, /device:TPU:192, one launch (start us, length us, event | category | flops | bytes accessed | tf_op | source)
XLA Modules:
  0.0 86.4 jit_solution(15340501393874619806)
XLA Ops:
  0.6 4.0 %shard_map.101 = bf16[16,528,128]{2,1,0:T(8,128)(2,1)} custom-call(bf16[128,16,128]{2,1,0:T(8,128)(2,1)} %bitcast.8, bf16[128,16,128]{2,1,0:T(8,128)(2,1)} %bitcast.9, bf16[128,16,128]{2,1,0:T(8,128)(2,1)} %bitcast.10, bf16[128,16,128]{2,1,0:T(8,128)(2,1)} %bitcast.11, s32[1,128]{1,0:T(1,128)} %hist_ref.1), custom_call_target="tpu_custom_call" | custom-call | tf_op jit(solution)/shard_map/pallas_call | solution.py:252
  4.7 0.0 copy-start
  4.7 36.4 %all_to_all.10.held = bf16[16,528,128]{2,1,0:T(8,128)(2,1)S(1)} all-to-all(bf16[16,528,128]{2,1,0:T(8,128)(2,1)} %shard_map.101), channel_id=1, replica_groups=mesh['ctx'=16,'exp'=16] {'ctx'}, dimensions={0} | all-to-all | bytes 4325376 | tf_op jit(solution)/shard_map/all_to_all | solution.py:266
  41.1 0.0 copy-done
  41.1 9.4 %shard_map.102 = (bf16[16,512,128]{2,1,0:T(8,128)(2,1)}, f32[1]{0:T(128)}) custom-call(f32[16]{0:T(128)S(1)} %copy-done, bf16[16,528,128]{2,1,0:T(8,128)(2,1)S(1)} %all_to_all.10.held), custom_call_target="tpu_custom_call" | custom-call | tf_op jit(solution)/shard_map/pallas_call | solution.py:267
  50.4 3.7 %all-to-all-start.1 = ((bf16[16,512,128]{2,1,0:T(8,128)(2,1)}), bf16[16,512,128]{2,1,0:T(8,128)(2,1)S(1)}, u32[]{:S(2)}, u32[]{:S(2)}) async-start(bf16[16,512,128]{2,1,0:T(8,128)(2,1)} %get-tuple-element.11), calls=%async_computation.1 | async-start | bytes 4194304 | tf_op jit(solution)/shard_map/all_to_all | solution.py:286
  54.2 0.0 collective-permute-start
  54.2 3.0 %collective-permute-done = f32[1]{0:T(128)} collective-permute-done((f32[1]{0:T(128)}, f32[1]{0:T(128)}, u32[]{:S(2)}, u32[]{:S(2)}) %collective-permute-start) | collective-permute-done | bytes 36 | tf_op jit(solution)/shard_map/ppermute | solution.py:290
  58.5 2.0 %collective-permute-start.1 = (f32[1]{0:T(128)}, f32[1]{0:T(128)}, u32[]{:S(2)}, u32[]{:S(2)}) collective-permute-start(f32[1]{0:T(128)} %add.12), channel_id=1, source_target_pairs={{0,2},{1,3},{2,4},{3,5},{4,6},{5,7},{6,8},{7,9},{8,10},{9,11},{10,... | collective-permute-start | bytes 20 | tf_op jit(solution)/shard_map/ppermute | solution.py:290
  60.5 1.6 %collective-permute-done.1 = f32[1]{0:T(128)} collective-permute-done((f32[1]{0:T(128)}, f32[1]{0:T(128)}, u32[]{:S(2)}, u32[]{:S(2)}) %collective-permute-start.1) | collective-permute-done | bytes 36 | tf_op jit(solution)/shard_map/ppermute | solution.py:290
  62.7 2.6 %collective-permute-start.2 = (f32[1]{0:T(128)}, f32[1]{0:T(128)}, u32[]{:S(2)}, u32[]{:S(2)}) collective-permute-start(f32[1]{0:T(128)} %add.13), channel_id=1, source_target_pairs={{0,4},{1,5},{2,6},{3,7},{4,8},{5,9},{6,10},{7,11},{8,12},{9,13},{1... | collective-permute-start | bytes 20 | tf_op jit(solution)/shard_map/ppermute | solution.py:290
  65.4 3.2 %collective-permute-done.2 = f32[1]{0:T(128)} collective-permute-done((f32[1]{0:T(128)}, f32[1]{0:T(128)}, u32[]{:S(2)}, u32[]{:S(2)}) %collective-permute-start.2) | collective-permute-done | bytes 36 | tf_op jit(solution)/shard_map/ppermute | solution.py:290
  69.2 4.8 %collective-permute-start.3 = (f32[1]{0:T(128)}, f32[1]{0:T(128)}, u32[]{:S(2)}, u32[]{:S(2)}) collective-permute-start(f32[1]{0:T(128)} %add.14), channel_id=1, source_target_pairs={{0,8},{1,9},{2,10},{3,11},{4,12},{5,13},{6,14},{7,15},{8,0},{9,1},... | collective-permute-start | bytes 20 | tf_op jit(solution)/shard_map/ppermute | solution.py:290
  74.0 2.7 %collective-permute-done.3 = f32[1]{0:T(128)} collective-permute-done((f32[1]{0:T(128)}, f32[1]{0:T(128)}, u32[]{:S(2)}, u32[]{:S(2)}) %collective-permute-start.3) | collective-permute-done | bytes 36 | tf_op jit(solution)/shard_map/ppermute | solution.py:290
  77.3 5.0 %all-to-all-done.1.held = bf16[16,512,128]{2,1,0:T(8,128)(2,1)S(1)} async-done(((bf16[16,512,128]{2,1,0:T(8,128)(2,1)}), bf16[16,512,128]{2,1,0:T(8,128)(2,1)S(1)}, u32[]{:S(2)}, u32[]{:S(2)}) %all-to-all-start.1) | async-done | bytes 2097184 | tf_op jit(solution)/shard_map/all_to_all | solution.py:286
  82.4 3.0 %shard_map.103 = (bf16[128,16,128]{2,1,0:T(8,128)(2,1)}, bf16[128,16,128]{2,1,0:T(8,128)(2,1)}, bf16[128,16,128]{2,1,0:T(8,128)(2,1)}, bf16[128,16,128]{2,1,0:T(8,128)(2,1)}) custom-call(bf16[16,512,128]{2,1,0:T(8,128)(2,1)S(1)} %all-to-all-done.1.held), custom_call_target="tpu_custom_call" | custom-call | tf_op jit(solution)/shard_map/pallas_call | solution.py:292
Async XLA Ops:
  4.7 36.4 %copy-start = (f32[16]{0:T(128)S(1)}, f32[16]{0:T(128)}, u32[]{:S(2)}) copy-start(f32[16]{0:T(128)} %temper_ref.1) | copy-start | bytes 196
  50.4 31.9 %all-to-all-start.1 = ((bf16[16,512,128]{2,1,0:T(8,128)(2,1)}), bf16[16,512,128]{2,1,0:T(8,128)(2,1)S(1)}, u32[]{:S(2)}, u32[]{:S(2)}) async-start(bf16[16,512,128]{2,1,0:T(8,128)(2,1)} %get-tuple-element.11), calls=%async_computation.1 | async-start | bytes 4194304 | tf_op jit(solution)/shard_map/all_to_all | solution.py:286
  54.2 3.1 %collective-permute-start = (f32[1]{0:T(128)}, f32[1]{0:T(128)}, u32[]{:S(2)}, u32[]{:S(2)}) collective-permute-start(f32[1]{0:T(128)} %get-tuple-element.16), channel_id=1, source_target_pairs={{0,1},{1,2},{2,3},{3,4},{4,5},{5,6},{6,7},{7,8},{8,9},{9,10},{10,1... | collective-permute-start | bytes 20 | tf_op jit(solution)/shard_map/ppermute | solution.py:290
  58.5 3.6 %collective-permute-start.1 = (f32[1]{0:T(128)}, f32[1]{0:T(128)}, u32[]{:S(2)}, u32[]{:S(2)}) collective-permute-start(f32[1]{0:T(128)} %add.12), channel_id=1, source_target_pairs={{0,2},{1,3},{2,4},{3,5},{4,6},{5,7},{6,8},{7,9},{8,10},{9,11},{10,... | collective-permute-start | bytes 20 | tf_op jit(solution)/shard_map/ppermute | solution.py:290
  62.7 5.8 %collective-permute-start.2 = (f32[1]{0:T(128)}, f32[1]{0:T(128)}, u32[]{:S(2)}, u32[]{:S(2)}) collective-permute-start(f32[1]{0:T(128)} %add.13), channel_id=1, source_target_pairs={{0,4},{1,5},{2,6},{3,7},{4,8},{5,9},{6,10},{7,11},{8,12},{9,13},{1... | collective-permute-start | bytes 20 | tf_op jit(solution)/shard_map/ppermute | solution.py:290
  69.2 7.5 %collective-permute-start.3 = (f32[1]{0:T(128)}, f32[1]{0:T(128)}, u32[]{:S(2)}, u32[]{:S(2)}) collective-permute-start(f32[1]{0:T(128)} %add.14), channel_id=1, source_target_pairs={{0,8},{1,9},{2,10},{3,11},{4,12},{5,13},{6,14},{7,15},{8,0},{9,1},... | collective-permute-start | bytes 20 | tf_op jit(solution)/shard_map/ppermute | solution.py:290
